TPU v7x, 128 devices: a whole 4x4x4 slice. The times are simulated.
128 devices in a mesh: dp: 4 (over y), mp: 32 (over x, z, core).
Axes of the slice: x: 4, y: 4, z: 4, core: 2. Of those that a mesh axis runs over, the one named last changes fastest.
Arguments:
- events: bfloat16 [128, 1024, 512], P(('dp', 'mp')), may hold values from -6 to 6
- lengths: int32 [128], P(('dp', 'mp')), may hold values from 1 to 1024, 81920 in all
- target_ids: int32 [128, 1024], P(('dp', 'mp')), may hold values from 0 to 524287, as said below
- neg_ids: int32 [1024], replicated, may hold values from 0 to 524287, as said below
- neg_counts: int32 [1024], replicated, may hold values from 1 to 64
- item_table: bfloat16 [524288, 512], P(('dp', 'mp')), may hold values from -2 to 2
- w_uvqk: bfloat16 [512, 2048], P('mp'), may hold values from -0.25 to 0.25
- w_out: bfloat16 [512, 512], P('mp'), may hold values from -0.25 to 0.25
Outputs:
- token_loss: float32 [128, 1024], P(('dp', 'mp'))
- table_grad: bfloat16 [524288, 512], P(('dp', 'mp'))
Inputs may be any that keep to these rules, and one draw needn't show every extreme that they name: `neg_ids`: the negatives are distinct. No device's rows hold more than 16 of them, one device's rows hold exactly 16, and the other devices' shares differ by one at most. `target_ids`: in each sequence no device's rows hold more than 16 of the targets; one device's rows, the same for every sequence, hold exactly 16 in each, and the other devices' shares in a sequence differ by one at most.
All inputs are finite; a program needn't handle non-finite values. No bound on the sum of `lengths` on one device may be relied on, other than what follows from the above.
Results may differ from a plain program's by a relative error of at most 0.0075.
Values may be sent and summed in bfloat16 or wider, within the bound.
No kernel may reach another device: no remote copies, remote signals or barrier semaphores. Data moves between devices by JAX's collectives and lax.ppermute only.
A program may use at most 128 MiB of HBM per device.

v0:
```python
import math

import jax
import jax.numpy as jnp
from jax import lax
from jax.experimental import pallas as pl
from jax.experimental.pallas import tpu as pltpu
from jax.sharding import Mesh, PartitionSpec as P

H = 4
EPSILON = 1e-05
ALL = ("y", "x", "z", "c")
CHIPS = ("y", "x", "z")
MP = ("x", "z", "c")
BF = jnp.bfloat16
F32 = jnp.float32
I32 = jnp.int32
DEVS = 128
NCHIPS = 64
CSLOTS = 24
SLOTS = NCHIPS * CSLOTS
ITEMS_DEV = 4096
B = 256
VMEM = pl.BlockSpec(memory_space=pltpu.VMEM)
SMEM = pl.BlockSpec(memory_space=pltpu.SMEM)
NT = (((1,), (1,)), ((), ()))
NEG_INF = float("-inf")
POS_INF = float("inf")
SWAP = ((0, 1), (1, 0))


def dot(a, b):
    return jnp.dot(a, b, preferred_element_type=F32)


def dot_nt(a, b):
    return lax.dot_general(a, b, NT, preferred_element_type=F32)


def iota(shape, dim):
    return lax.broadcasted_iota(I32, shape, dim)


def layer_norm(values):
    center = values - jnp.mean(values, axis=-1, keepdims=True)
    spread = jnp.mean(center * center, axis=-1, keepdims=True)
    return center * lax.rsqrt(spread + EPSILON)


def call(body, out_shape, in_specs, scratch=(), flops=0, nbytes=0):
    return pl.pallas_call(
        body,
        out_shape=out_shape,
        in_specs=in_specs,
        out_specs=jax.tree.map(lambda _: VMEM, out_shape),
        scratch_shapes=list(scratch),
        cost_estimate=pl.CostEstimate(flops=flops, bytes_accessed=nbytes, transcendentals=0),
        compiler_params=pltpu.CompilerParams(vmem_limit_bytes=56 << 20),
    )


def norm_kernel(events_ref, out_ref):
    @pl.loop(0, 4)
    def _(i):
        rows = pl.ds(pl.multiple_of(i * B, B), B)
        out_ref[rows, :] = layer_norm(events_ref[rows, :].astype(F32)).astype(BF)


def silu_of_half(h):
    return h + h * jnp.tanh(h)


def layer_kernel(
    info_ref, normed_ref, own_ref, other_ref, events_ref, follow_ref, hot_ref,
    hidden_ref, positive_ref, send_ref, w_ref, act_ref, att_ref,
):
    core, length = info_ref[0], info_ref[1]
    for b in range(16):
        block = slice(b * 16, (b + 1) * 16)
        w_ref[pl.ds(pl.multiple_of(b * 32 + core * 16, 16), 16), :] = own_ref[block, :]
        w_ref[pl.ds(pl.multiple_of(b * 32 + (1 - core) * 16, 16), 16), :] = other_ref[block, :]

    @pl.loop(0, 4)
    def _(i):
        rows = pl.ds(pl.multiple_of(i * B, B), B)
        a = normed_ref[rows, :]
        live = iota((B, 512), 0) + i * B < length
        for n in range(4):
            cols = slice(n * 512, (n + 1) * 512)
            v = silu_of_half(0.5 * dot(a, w_ref[:, cols]))
            if n == 1:
                v = jnp.where(live, v, 0.0)
            act_ref[rows, cols] = v.astype(BF)

    causal = iota((B, B), 1) <= iota((B, B), 0)
    eye = iota((B, B), 1) == iota((B, B), 0)
    scale = 0.5 / math.sqrt(128)
    for i in range(4):
        rows = slice(i * B, (i + 1) * B)
        for h in range(H):
            q = act_ref[rows, 1024 + h * 128 : 1024 + (h + 1) * 128]
            total = None
            for j in range(i + 1):
                keys = slice(j * B, (j + 1) * B)
                s = dot_nt(q, act_ref[keys, 1536 + h * 128 : 1536 + (h + 1) * 128])
                w = silu_of_half(s * scale)
                if j == i:
                    w = jnp.where(causal, w, 0.0)
                t = dot(w.astype(BF), act_ref[keys, 512 + h * 128 : 512 + (h + 1) * 128])
                total = t if total is None else total + t
            att_ref[:, h * 128 : (h + 1) * 128] = total
        gated = (layer_norm(att_ref[...]) * act_ref[rows, :512].astype(F32)).astype(BF)
        hidden = (events_ref[rows, :].astype(F32) + dot(gated, w_ref[:, 2048:])).astype(BF)
        hidden_ref[rows, :] = hidden
        pos = jnp.sum(hidden.astype(F32) * follow_ref[rows, :].astype(F32), axis=1, keepdims=True)
        positive_ref[:, rows] = jnp.sum(jnp.where(eye, pos, 0.0), axis=0, keepdims=True)

    @pl.loop(0, SLOTS // B)
    def _(m):
        rows = pl.ds(pl.multiple_of(m * B, B), B)
        send_ref[rows, :] = dot(hot_ref[rows, :], hidden_ref[...]).astype(BF)


def loss_kernel(
    info_ref, hidden_ref, own_ref, other_ref, ids_ref, logc_ref, positive_ref, targets_ref, hot_ref,
    index_ref, loss_ref, term_own_ref, term_other_ref, meta_ref, l_ref, probs_ref, coef_ref,
):
    core, length = info_ref[0], info_ref[1]
    own_cols = pl.ds(pl.multiple_of(core * B, B), B)
    other_cols = pl.ds(pl.multiple_of((1 - core) * B, B), B)
    chunks = [slice(m * B, (m + 1) * B) for m in range(SLOTS // B)]

    @pl.loop(0, 4)
    def _(t):
        at = pl.ds(pl.multiple_of(t * B, B), B)
        h_own = hidden_ref[at, own_cols]
        h_other = hidden_ref[at, other_cols]
        pos = positive_ref[:, at]
        target = targets_ref[:, at]
        top = pos
        for m in chunks:
            value = dot_nt(own_ref[m, :], h_own) + dot_nt(other_ref[m, :], h_other) - logc_ref[m, :]
            value = jnp.where(ids_ref[m, :] != target, value, NEG_INF)
            l_ref[m, :] = value
            top = jnp.maximum(top, jnp.max(value, axis=0, keepdims=True))
        total = jnp.exp(pos - top)
        for m in chunks:
            total = total + jnp.sum(jnp.exp(l_ref[m, :] - top), axis=0, keepdims=True)
        log_total = top + jnp.log(total)
        in_range = iota((1, B), 1) + t * B < length - 1
        loss_ref[:, at] = jnp.where(in_range, log_total - pos, 0.0)
        coef_ref[:, at] = jnp.where(in_range, jnp.exp(pos - log_total) - 1.0, 0.0)
        shift = jnp.where(in_range, log_total, POS_INF)
        for m in chunks:
            probs_ref[m, at] = jnp.exp(l_ref[m, :] - shift).astype(BF)

    coef = coef_ref[...]
    high = coef.astype(BF).astype(F32)
    middle = (coef - high).astype(BF).astype(F32)
    low = coef - high - middle
    pieces = jnp.concatenate(
        [high, middle, low, index_ref[...], jnp.zeros((11, 1024), F32)], axis=0
    ).astype(BF)
    for m in chunks:
        meta_ref[:, m] = dot_nt(pieces, hot_ref[m, :]).astype(BF)
        term_other_ref[m, :] = dot(probs_ref[m, :], hidden_ref[:, other_cols]).astype(BF)
        term_own_ref[m, :] = dot(probs_ref[m, :], hidden_ref[:, own_cols])


def place_kernel(index_ref, rows_ref, neg_index_ref, neg_ref, out_ref):
    tile = out_ref.shape[0]
    base = pl.program_id(0) * tile

    def onehot(index):
        return (iota((tile, index.shape[1]), 0) + base == index).astype(F32).astype(BF)

    out_ref[...] = (
        dot(onehot(index_ref[...]), rows_ref[...]) + dot(onehot(neg_index_ref[...]), neg_ref[...])
    ).astype(BF)


def chip_slots(ids):
    n = ids.shape[0]
    owner = ids // ITEMS_DEV
    hot = (iota((DEVS, n), 0) == owner[None, :]).astype(BF)
    tri = (iota((n, n), 0) < iota((n, n), 1)).astype(BF)
    rank = jnp.sum(dot(hot, tri) * hot.astype(F32), axis=0).astype(I32)
    within = jnp.where(rank < 8, (owner % 2) * 8 + rank, 8 + rank)
    return (owner // 2) * CSLOTS + within


def swap(v):
    return lax.ppermute(v, "c", SWAP)


def chips_a2a(v):
    return lax.all_to_all(v, CHIPS, split_axis=0, concat_axis=0, tiled=True)


def per_device(events, lengths, target_ids, neg_ids, neg_counts, item_table, w_uvqk, w_out):
    width = 512
    core = lax.axis_index("c")
    chip = lax.axis_index(CHIPS)
    info = jnp.stack([core, lengths[0]]).astype(I32)
    targets = target_ids[0]
    ev = events[0]

    w_mine = jnp.concatenate([w_uvqk, w_out], axis=1)
    w_own = lax.all_to_all(
        jnp.broadcast_to(w_mine[None], (16,) + w_mine.shape), ("x", "z"), split_axis=0, concat_axis=0, tiled=True
    ).reshape(256, 2560)
    w_other = swap(w_own)

    normed = call(norm_kernel, jax.ShapeDtypeStruct((1024, 512), BF), [VMEM], nbytes=2 << 20, flops=1 << 20)(ev)

    neg_slot = chip_slots(neg_ids)
    slot_ids = jnp.arange(SLOTS, dtype=I32)
    here = iota((CSLOTS, 1), 0) + chip * CSLOTS == neg_slot[None, :]
    mine = here & ((neg_ids // ITEMS_DEV) % 2 == core)[None, :]
    neg_local = jnp.sum(jnp.where(mine, (neg_ids % ITEMS_DEV)[None, :] + 1, 0), axis=1) - 1
    packed = jnp.where((neg_local >= 0)[:, None], item_table[jnp.maximum(neg_local, 0)], 0)
    packed_own = lax.dynamic_slice(packed, (0, core * B), (CSLOTS, B))
    packed_other = lax.dynamic_slice(packed, (0, (1 - core) * B), (CSLOTS, B))
    packed_own = packed_own + swap(packed_other)
    neg_own = chips_a2a(jnp.broadcast_to(packed_own[None], (NCHIPS, CSLOTS, B))).reshape(SLOTS, B)
    neg_other = swap(neg_own)
    match = slot_ids[:, None] == neg_slot[None, :]
    slot_neg_id = jnp.sum(jnp.where(match, neg_ids[None, :] + 1, 0), axis=1) - 1
    slot_count = jnp.sum(jnp.where(match, neg_counts[None, :], 0), axis=1)
    slot_logc = jnp.where(slot_count > 0, jnp.log(slot_count.astype(F32)), POS_INF)

    target_slot = chip_slots(targets)
    hot = (slot_ids[:, None] == target_slot[None, :]).astype(BF)
    chip_row = targets % (2 * ITEMS_DEV) + 1
    index = jnp.stack([chip_row // 64, chip_row % 64]).astype(F32)

    follow = jnp.concatenate([ev[1:], jnp.zeros((1, width), BF)], axis=0)
    hidden, positive, send_rows = call(
        layer_kernel,
        (
            jax.ShapeDtypeStruct((1024, width), BF),
            jax.ShapeDtypeStruct((1, 1024), F32),
            jax.ShapeDtypeStruct((SLOTS, width), BF),
        ),
        [SMEM] + [VMEM] * 6,
        scratch=[
            pltpu.VMEM((512, 2560), BF),
            pltpu.VMEM((1024, 2048), BF),
            pltpu.VMEM((B, width), F32),
        ],
        flops=9 << 30,
        nbytes=12 << 20,
    )(info, normed, w_own, w_other, ev, follow, hot)

    recv_rows = chips_a2a(send_rows.reshape(NCHIPS, CSLOTS, width))

    loss, term_own, term_other, meta = call(
        loss_kernel,
        (
            jax.ShapeDtypeStruct((1, 1024), F32),
            jax.ShapeDtypeStruct((SLOTS, B), F32),
            jax.ShapeDtypeStruct((SLOTS, B), BF),
            jax.ShapeDtypeStruct((16, SLOTS), BF),
        ),
        [SMEM] + [VMEM] * 9,
        scratch=[
            pltpu.VMEM((SLOTS, B), F32),
            pltpu.VMEM((SLOTS, 1024), BF),
            pltpu.VMEM((1, 1024), F32),
        ],
        flops=7 << 30,
        nbytes=12 << 20,
    )(
        info, hidden, neg_own, neg_other, slot_neg_id[:, None], slot_logc[:, None], positive,
        target_ids, hot, index,
    )
    term = (term_own + swap(term_other).astype(F32)).astype(BF).reshape(NCHIPS, CSLOTS, B)
    meta = meta[:8].reshape(8, NCHIPS, CSLOTS).transpose(1, 0, 2)
    meta = jnp.pad(meta, ((0, 0), (0, 0), (0, B - CSLOTS)))
    got = chips_a2a(jnp.concatenate([term, meta], axis=1))
    summed = jnp.sum(got[:, :CSLOTS].astype(F32), axis=0)
    got_meta = got[:, CSLOTS:, :CSLOTS].astype(F32)
    got_coef = got_meta[:, 0] + got_meta[:, 1] + got_meta[:, 2]
    got_row = got_meta[:, 3] * 64.0 + got_meta[:, 4]

    def split(v):
        first, second, last = v[:, :8], v[:, 8:16], v[:, 16:]
        keep = jnp.where(core == 0, first, second)
        give = jnp.where(core == 0, second, first)
        return jnp.concatenate([keep, last], axis=1), jnp.concatenate([give, last], axis=1)

    rows_keep, rows_give = split(recv_rows)
    coef_keep, coef_give = split(got_coef)
    row_keep, row_give = split(got_row)
    rows_got = swap(rows_give)
    small = jnp.concatenate([summed, coef_give.reshape(4, B), row_give.reshape(4, B)], axis=0)
    small = swap(small)
    summed_got = small[:CSLOTS]
    coef_all = jnp.concatenate([coef_keep.reshape(-1), small[CSLOTS : CSLOTS + 4].reshape(-1)])
    row_all = jnp.concatenate([row_keep.reshape(-1), small[CSLOTS + 4 :].reshape(-1)])
    row_at = row_all.astype(I32) - 1 - core * ITEMS_DEV
    rows = jnp.concatenate([rows_keep.reshape(-1, width), rows_got.reshape(-1, width)], axis=0)
    rows = (rows.astype(F32) * coef_all[:, None]).astype(BF)

    neg_sum = jnp.where(
        core == 0,
        jnp.concatenate([summed, summed_got], axis=1),
        jnp.concatenate([summed_got, summed], axis=1),
    )
    neg_high = neg_sum.astype(BF)
    neg_low = (neg_sum - neg_high.astype(F32)).astype(BF)
    rest = 128 - 2 * CSLOTS
    neg_rows = jnp.concatenate([neg_high, neg_low, jnp.zeros((rest, width), BF)], axis=0)
    neg_at = jnp.concatenate([neg_local, neg_local, jnp.full((rest,), -1, I32)])

    tile = 512
    whole = lambda shape: pl.BlockSpec(shape, lambda i: (0, 0))
    grad = pl.pallas_call(
        place_kernel,
        grid=(ITEMS_DEV // tile,),
        out_shape=jax.ShapeDtypeStruct((ITEMS_DEV, width), BF),
        in_specs=[whole((1, 2048)), whole((2048, width)), whole((1, 128)), whole((128, width))],
        out_specs=pl.BlockSpec((tile, width), lambda i: (i, 0)),
        cost_estimate=pl.CostEstimate(flops=9 << 30, bytes_accessed=8 << 20, transcendentals=0),
        compiler_params=pltpu.CompilerParams(vmem_limit_bytes=48 << 20),
    )(row_at[None], rows, neg_at[None], neg_rows)
    return loss, grad


def solution(mesh):
    fine = Mesh(mesh.devices.reshape(4, 4, 4, 2), ALL)
    in_specs = (P(ALL), P(ALL), P(ALL), P(), P(), P(ALL), P(MP), P(MP))
    return jax.shard_map(
        per_device, mesh=fine, in_specs=in_specs, out_specs=(P(ALL), P(ALL)), check_vma=False
    )
```

profile of v0, /device:TPU:1, one launch (start us, length us, event | category | flops | bytes accessed | tf_op | source)
XLA Modules:
  0.0 151.7 jit_solution(2982891093162506325)
XLA Ops:
  0.6 0.9 pad_maximum_fusion.2
  1.5 1.2 broadcast_in_dim.85
  2.7 8.6 %all-to-all-start = ((bf16[16,16,2560]{2,1,0:T(8,128)(2,1)}), bf16[16,16,2560]{2,1,0:T(8,128)(2,1)S(1)}, u32[]{:S(2)}, u32[]{:S(2)}) async-start(bf16[16,16,2560]{2,1,0:T(8,128)(2,1)} %broadcast_in_dim.85), calls=%async_computation | async-start | bytes 2621440 | tf_op jit(solution)/shard_map/all_to_all | solution.py:209
  12.1 3.3 %gather_fusion = bf16[24,512]{1,0:T(8,128)(2,1)S(1)} fusion(bf16[4096,512]{1,0:T(8,128)(2,1)} %param.13, s32[1024]{0:T(1024)S(1)} %pad_clamp_fusion), kind=kCustom, calls=%fused_computation | custom fusion | bytes 49248 | tf_op jit(solution)/shard_map/gather | solution.py:221
  15.5 1.0 collective-permute-start.1
  17.0 1.8 %select_reduce_fusion = (s32[1536]{0:T(1024)S(1)}, s32[1536]{0:T(1024)S(1)}) fusion(s32[1024]{0:T(1024)S(1)} %copy-done.4, s32[1024]{0:T(1024)S(1)} %get-tuple-element.49, s32[1024]{0:T(1024)S(1)} %get-tuple-element.44), kind=kLoop, calls=%fused_computation.1 | loop fusion | flops 7861248 | bytes 24576 | tf_op jit(solution)/shard_map/reduce_sum | solution.py:229
  19.2 10.2 %all-to-all-done = bf16[16,16,2560]{2,1,0:T(8,128)(2,1)S(1)} async-done(((bf16[16,16,2560]{2,1,0:T(8,128)(2,1)}), bf16[16,16,2560]{2,1,0:T(8,128)(2,1)S(1)}, u32[]{:S(2)}, u32[]{:S(2)}) %all-to-all-start) | async-done | bytes 1310752 | tf_op jit(solution)/shard_map/all_to_all | solution.py:209
  29.3 3.7 %collective-permute-start = (bf16[256,2560]{1,0:T(8,128)(2,1)S(1)}, bf16[256,2560]{1,0:T(8,128)(2,1)}, u32[]{:S(2)}, u32[]{:S(2)}) collective-permute-start(bf16[256,2560]{1,0:T(8,128)(2,1)S(1)} %bitcast.33), channel_id=1, source_target_pairs={{0,1},{1,0},{2,3},{3,2},{4,5},{5,4},{6,7},{7,6},{8,9},{9,8},{10,11... | collective-permute-start | bytes 3932168 | tf_op jit(solution)/shard_map/ppermute | solution.py:193
  33.7 1.2 sub.69.ids_ref
  34.9 1.2 select_n.164.logc_ref
  36.1 1.1 concatenate.63.follow_ref
  37.1 3.2 %shard_map.95.normed_ref = bf16[1024,512]{1,0:T(8,128)(2,1)} custom-call(bf16[1024,512]{1,0:T(8,128)(2,1)} %bitcast.28), custom_call_target="tpu_custom_call" | custom-call | flops 1048576 | bytes 2097152 | tf_op jit(solution)/shard_map/pallas_call | solution.py:214
  40.3 0.9 broadcast_in_dim.90
  41.3 7.0 %all-to-all-start.1 = ((bf16[64,24,256]{2,1,0:T(8,128)(2,1)}), bf16[64,24,256]{2,1,0:T(8,128)(2,1)}, u32[]{:S(2)}, u32[]{:S(2)}) async-start(bf16[64,24,256]{2,1,0:T(8,128)(2,1)} %broadcast_in_dim.90), calls=%async_computation.1 | async-start | bytes 1572864 | tf_op jit(solution)/shard_map/all_to_all | solution.py:197
  49.5 3.2 %fusion.hot_ref = bf16[1536,1024]{1,0:T(8,128)(2,1)} fusion(s32[1024]{0:T(1024)S(1)} %bitcast.39), kind=kLoop, calls=%fused_computation.5 | loop fusion | flops 3145728 | bytes 3149824 | tf_op jit(solution)/shard_map/convert_element_type | solution.py:233
  52.6 10.7 %all-to-all-done.1 = bf16[64,24,256]{2,1,0:T(8,128)(2,1)} async-done(((bf16[64,24,256]{2,1,0:T(8,128)(2,1)}), bf16[64,24,256]{2,1,0:T(8,128)(2,1)}, u32[]{:S(2)}, u32[]{:S(2)}) %all-to-all-start.1) | async-done | bytes 786464 | tf_op jit(solution)/shard_map/all_to_all | solution.py:197
  63.4 1.7 %collective-permute-start.2 = (bf16[1536,256]{1,0:T(8,128)(2,1)}, bf16[1536,256]{1,0:T(8,128)(2,1)}, u32[]{:S(2)}, u32[]{:S(2)}) collective-permute-start(bf16[1536,256]{1,0:T(8,128)(2,1)} %bitcast.7.own_ref), channel_id=1, source_target_pairs={{0,1},{1,0},{2,3},{3,2},{4,5},{5,4},{6,7},{7,6},{8,9},{9,8},{10,11... | collective-permute-start | bytes 2359304 | tf_op jit(solution)/shard_map/ppermute | solution.py:193
  65.1 17.8 %shard_map.96 = (bf16[1024,512]{1,0:T(8,128)(2,1)}, f32[1,1024]{1,0:T(1,128)}, bf16[1536,512]{1,0:T(8,128)(2,1)}) custom-call(s32[2]{0:T(128)} %pad_add_fusion.info_ref, bf16[1024,512]{1,0:T(8,128)(2,1)} %shard_map.95.normed_ref, bf16[256,2560]{1,0:T(8,128)(2,1)} %bitcast.34, bf16[256,2560]{1,0:T(8,128)(2,1)} %collective-permute-done.other_ref, ...), custom_call_target="tpu_custom_call" | custom-call | flops 9663676416 | bytes 12582912 | tf_op jit(solution)/shard_map/pallas_call | solution.py:238
  82.9 4.7 %all-to-all-start.3 = ((bf16[64,24,512]{2,1,0:T(8,128)(2,1)}), bf16[64,24,512]{2,1,0:T(8,128)(2,1)S(1)}, u32[]{:S(2)}, u32[]{:S(2)}) async-start(bf16[64,24,512]{2,1,0:T(8,128)(2,1)} %bitcast.32), calls=%async_computation.3 | async-start | bytes 3145728 | tf_op jit(solution)/shard_map/all_to_all | solution.py:197
  87.6 11.7 %shard_map.97 = (f32[1,1024]{1,0:T(1,128)}, f32[1536,256]{1,0:T(8,128)}, bf16[1536,256]{1,0:T(8,128)(2,1)}, bf16[16,1536]{1,0:T(8,128)(2,1)}) custom-call(s32[2]{0:T(128)} %pad_add_fusion.info_ref, bf16[1024,512]{1,0:T(8,128)(2,1)} %get-tuple-element.9.hidden_ref, bf16[1536,256]{1,0:T(8,128)(2,1)} %bitcast.7.own_ref, ...), custom_call_target="tpu_custom_call" | custom-call | flops 7516192768 | bytes 12582912 | tf_op jit(solution)/shard_map/pallas_call | solution.py:257
  99.3 0.7 slice.68
  100.3 1.4 collective-permute-done.3
  101.8 1.6 %add_convert_fusion = bf16[1536,256]{1,0:T(8,128)(2,1)S(1)} fusion(f32[1536,256]{1,0:T(8,128)} %get-tuple-element.12, bf16[1536,256]{1,0:T(8,128)(2,1)S(1)} %collective-permute-done.3), kind=kLoop, calls=%fused_computation.13 | loop fusion | flops 1179648 | bytes 3145728 | tf_op jit(solution)/shard_map/convert_element_type | solution.py:277
  103.4 1.1 fusion.8
  104.5 6.8 %all-to-all-done.3 = bf16[64,24,512]{2,1,0:T(8,128)(2,1)S(1)} async-done(((bf16[64,24,512]{2,1,0:T(8,128)(2,1)}), bf16[64,24,512]{2,1,0:T(8,128)(2,1)S(1)}, u32[]{:S(2)}, u32[]{:S(2)}) %all-to-all-start.3) | async-done | bytes 1572896 | tf_op jit(solution)/shard_map/all_to_all | solution.py:197
  111.3 5.3 %all-to-all-start.2 = ((bf16[64,32,256]{2,1,0:T(8,128)(2,1)}), bf16[64,32,256]{2,1,0:T(8,128)(2,1)S(1)}, u32[]{:S(2)}, u32[]{:S(2)}) async-start(bf16[64,32,256]{2,1,0:T(8,128)(2,1)} %fusion.8), calls=%async_computation.2 | async-start | bytes 2097152 | tf_op jit(solution)/shard_map/all_to_all | solution.py:197
  116.7 1.1 pad_maximum_fusion.1
  117.9 1.7 %collective-permute-start.5 = (bf16[64,16,512]{2,1,0:T(8,128)(2,1)}, bf16[64,16,512]{2,1,0:T(8,128)(2,1)}, u32[]{:S(2)}, u32[]{:S(2)}) collective-permute-start(bf16[64,16,512]{2,1,0:T(8,128)(2,1)} %get-tuple-element.26), channel_id=1, source_target_pairs={{0,1},{1,0},{2,3},{3,2},{4,5},{5,4},{6,7},{7,6},{8,9},{9,8},{10,11... | collective-permute-start | bytes 3145736 | tf_op jit(solution)/shard_map/ppermute | solution.py:193
  119.5 13.6 %all-to-all-done.2 = bf16[64,32,256]{2,1,0:T(8,128)(2,1)S(1)} async-done(((bf16[64,32,256]{2,1,0:T(8,128)(2,1)}), bf16[64,32,256]{2,1,0:T(8,128)(2,1)S(1)}, u32[]{:S(2)}, u32[]{:S(2)}) %all-to-all-start.2) | async-done | bytes 1048608 | tf_op jit(solution)/shard_map/all_to_all | solution.py:197
  133.9 3.2 %collective-permute-start.4 = (f32[32,256]{1,0:T(8,128)S(1)}, f32[32,256]{1,0:T(8,128)S(1)}, u32[]{:S(2)}, u32[]{:S(2)}) collective-permute-start(f32[32,256]{1,0:T(8,128)S(1)} %pad_maximum_fusion.6), channel_id=1, source_target_pairs={{0,1},{1,0},{2,3},{3,2},{4,5},{5,4},{6,7},{7,6},{8,9},{9,8},{10,11... | collective-permute-start | bytes 98312 | tf_op jit(solution)/shard_map/ppermute | solution.py:193
  138.2 1.7 %multiply_convert_fusion.rows_ref = bf16[2048,512]{1,0:T(8,128)(2,1)S(1)} fusion(bf16[1024,512]{1,0:T(8,128)(2,1)} %bitcast.14, bf16[1024,512]{1,0:T(8,128)(2,1)S(1)} %bitcast.30, f32[2048]{0:T(1024)S(1)} %pad_maximum_fusion.8), kind=kLoop, calls=%fused_computation.6 | loop fusion | flops 6291456 | bytes 4202496 | tf_op jit(solution)/shard_map/convert_element_type | solution.py:303
  139.9 11.8 %shard_map.98 = bf16[4096,512]{1,0:T(8,128)(2,1)} custom-call(s32[1,2048]{1,0:T(1,128)S(1)} %fusion.15.index_ref, bf16[2048,512]{1,0:T(8,128)(2,1)S(1)} %multiply_convert_fusion.rows_ref, s32[1,128]{1,0:T(1,128)S(1)} %add_bitcast_fusion.1.neg_index_ref, bf16[128,512]{1,0:T(8,128)(2,1)S(1)} %maximum_maximum_fusion.neg_ref), custom_call_target="tpu_custom_call" | custom-call | flops 9663676416 | bytes 8388608 | tf_op jit(solution)/shard_map/pallas_call | solution.py:318
  (66 shorter events, 5.1 us)
Async XLA Ops:
  0.6 10.6 %copy-start.2 = (s32[1024]{0:T(1024)S(1)}, s32[1024]{0:T(1024)}, u32[]{:S(2)}) copy-start(s32[1024]{0:T(1024)} %param.11) | copy-start | bytes 12292
  2.7 13.8 %copy-start.3 = (s32[1,1024]{1,0:T(1,128)S(1)}, s32[1,1024]{1,0:T(1,128)}, u32[]{:S(2)}) copy-start(s32[1,1024]{1,0:T(1,128)} %targets_ref.1) | copy-start | bytes 12292
  2.7 26.6 %all-to-all-start = ((bf16[16,16,2560]{2,1,0:T(8,128)(2,1)}), bf16[16,16,2560]{2,1,0:T(8,128)(2,1)S(1)}, u32[]{:S(2)}, u32[]{:S(2)}) async-start(bf16[16,16,2560]{2,1,0:T(8,128)(2,1)} %broadcast_in_dim.85), calls=%async_computation | async-start | bytes 2621440 | tf_op jit(solution)/shard_map/all_to_all | solution.py:209
  11.3 5.7 %copy-start.4 = (s32[1024]{0:T(1024)S(1)}, s32[1024]{0:T(1024)}, u32[]{:S(2)}) copy-start(s32[1024]{0:T(1024)} %param.12) | copy-start | bytes 12292
  11.3 7.6 %copy-start = (bf16[1,1024,512]{2,1,0:T(8,128)(2,1)S(1)}, bf16[1,1024,512]{2,1,0:T(8,128)(2,1)}, u32[]{:S(2)}) copy-start(bf16[1,1024,512]{2,1,0:T(8,128)(2,1)} %param.8) | copy-start | bytes 3145732
  15.5 24.8 %collective-permute-start.1 = (bf16[24,256]{1,0:T(8,128)(2,1)S(1)}, bf16[24,256]{1,0:T(8,128)(2,1)S(1)}, u32[]{:S(2)}, u32[]{:S(2)}) collective-permute-start(bf16[24,256]{1,0:T(8,128)(2,1)S(1)} %constant_dynamic-slice_fusion), channel_id=1, source_target_pairs={{0,1},{1,0},{2,3},{3,2},{4,5},{5,4},{6,7},{7,6},{8,9},{9,8},{10,11... | collective-permute-start | bytes 36872 | tf_op jit(solution)/shard_map/ppermute | solution.py:193
  29.3 11.0 %copy-start.1 = (bf16[16,16,2560]{2,1,0:T(8,128)(2,1)}, bf16[16,16,2560]{2,1,0:T(8,128)(2,1)S(1)}, u32[]{:S(2)}) copy-start(bf16[16,16,2560]{2,1,0:T(8,128)(2,1)S(1)} %all-to-all-done) | copy-start | bytes 3932164
  29.3 35.7 %collective-permute-start = (bf16[256,2560]{1,0:T(8,128)(2,1)S(1)}, bf16[256,2560]{1,0:T(8,128)(2,1)}, u32[]{:S(2)}, u32[]{:S(2)}) collective-permute-start(bf16[256,2560]{1,0:T(8,128)(2,1)S(1)} %bitcast.33), channel_id=1, source_target_pairs={{0,1},{1,0},{2,3},{3,2},{4,5},{5,4},{6,7},{7,6},{8,9},{9,8},{10,11... | collective-permute-start | bytes 3932168 | tf_op jit(solution)/shard_map/ppermute | solution.py:193
  41.3 22.1 %all-to-all-start.1 = ((bf16[64,24,256]{2,1,0:T(8,128)(2,1)}), bf16[64,24,256]{2,1,0:T(8,128)(2,1)}, u32[]{:S(2)}, u32[]{:S(2)}) async-start(bf16[64,24,256]{2,1,0:T(8,128)(2,1)} %broadcast_in_dim.90), calls=%async_computation.1 | async-start | bytes 1572864 | tf_op jit(solution)/shard_map/all_to_all | solution.py:197
  63.4 24.2 %collective-permute-start.2 = (bf16[1536,256]{1,0:T(8,128)(2,1)}, bf16[1536,256]{1,0:T(8,128)(2,1)}, u32[]{:S(2)}, u32[]{:S(2)}) collective-permute-start(bf16[1536,256]{1,0:T(8,128)(2,1)} %bitcast.7.own_ref), channel_id=1, source_target_pairs={{0,1},{1,0},{2,3},{3,2},{4,5},{5,4},{6,7},{7,6},{8,9},{9,8},{10,11... | collective-permute-start | bytes 2359304 | tf_op jit(solution)/shard_map/ppermute | solution.py:193
  82.9 28.4 %all-to-all-start.3 = ((bf16[64,24,512]{2,1,0:T(8,128)(2,1)}), bf16[64,24,512]{2,1,0:T(8,128)(2,1)S(1)}, u32[]{:S(2)}, u32[]{:S(2)}) async-start(bf16[64,24,512]{2,1,0:T(8,128)(2,1)} %bitcast.32), calls=%async_computation.3 | async-start | bytes 3145728 | tf_op jit(solution)/shard_map/all_to_all | solution.py:197
  99.3 2.5 %collective-permute-start.3 = (bf16[1536,256]{1,0:T(8,128)(2,1)}, bf16[1536,256]{1,0:T(8,128)(2,1)S(1)}, u32[]{:S(2)}, u32[]{:S(2)}) collective-permute-start(bf16[1536,256]{1,0:T(8,128)(2,1)} %get-tuple-element.13), channel_id=1, source_target_pairs={{0,1},{1,0},{2,3},{3,2},{4,5},{5,4},{6,7},{7,6},{8,9},{9,8},{10,11... | collective-permute-start | bytes 2359304 | tf_op jit(solution)/shard_map/ppermute | solution.py:193
  111.3 21.8 %all-to-all-start.2 = ((bf16[64,32,256]{2,1,0:T(8,128)(2,1)}), bf16[64,32,256]{2,1,0:T(8,128)(2,1)S(1)}, u32[]{:S(2)}, u32[]{:S(2)}) async-start(bf16[64,32,256]{2,1,0:T(8,128)(2,1)} %fusion.8), calls=%async_computation.2 | async-start | bytes 2097152 | tf_op jit(solution)/shard_map/all_to_all | solution.py:197
  117.9 20.4 %collective-permute-start.5 = (bf16[64,16,512]{2,1,0:T(8,128)(2,1)}, bf16[64,16,512]{2,1,0:T(8,128)(2,1)}, u32[]{:S(2)}, u32[]{:S(2)}) collective-permute-start(bf16[64,16,512]{2,1,0:T(8,128)(2,1)} %get-tuple-element.26), channel_id=1, source_target_pairs={{0,1},{1,0},{2,3},{3,2},{4,5},{5,4},{6,7},{7,6},{8,9},{9,8},{10,11... | collective-permute-start | bytes 3145736 | tf_op jit(solution)/shard_map/ppermute | solution.py:193
  133.9 4.1 %collective-permute-start.4 = (f32[32,256]{1,0:T(8,128)S(1)}, f32[32,256]{1,0:T(8,128)S(1)}, u32[]{:S(2)}, u32[]{:S(2)}) collective-permute-start(f32[32,256]{1,0:T(8,128)S(1)} %pad_maximum_fusion.6), channel_id=1, source_target_pairs={{0,1},{1,0},{2,3},{3,2},{4,5},{5,4},{6,7},{7,6},{8,9},{9,8},{10,11... | collective-permute-start | bytes 98312 | tf_op jit(solution)/shard_map/ppermute | solution.py:193
where the time goes:
time: 152 us
  Pallas kernels  44.5 us (29%)
  waiting for transfers between devices  43.3 us (28%)
  starting transfers between devices  36.8 us (24%)
  other arithmetic  14 us (9%)
  local copies, waits for them, and re-layouts  10.6 us (7%)
  between operations  1.63 us (1%)
    all_to_all x3, waiting for transfers between devices, chips_a2a(): return lax.all_to_all(v, CHIPS, split_axis=0, concat_axis=0, tiled=True)  31.2 us
    pallas_call x1, Pallas kernels, per_device(): call(layer_kernel, (jax.ShapeDtypeStruct((1024, width), BF), jax.ShapeDty...  17.8 us
    all_to_all x3, starting transfers between devices, chips_a2a(): return lax.all_to_all(v, CHIPS, split_axis=0, concat_axis=0, tiled=True)  16.9 us
    pallas_call x1, Pallas kernels, per_device(): pl.pallas_call(place_kernel, grid=(ITEMS_DEV // tile,), out_shape=jax.Sha...  11.8 us
    pallas_call x1, Pallas kernels, per_device(): call(loss_kernel, (jax.ShapeDtypeStruct((1, 1024), F32), jax.ShapeDtypeSt...  11.7 us
    ppermute x6, starting transfers between devices, swap(): return lax.ppermute(v, 'c', SWAP)  11.3 us
    all_to_all x1, waiting for transfers between devices, per_device(): lax.all_to_all(jnp.broadcast_to(w_mine[None], (16,) + w_mine.shape), ('x'...  10.2 us
    all_to_all x1, starting transfers between devices, per_device(): lax.all_to_all(jnp.broadcast_to(w_mine[None], (16,) + w_mine.shape), ('x'...  8.56 us
  transfers between devices with their start and end apart: 10, of which 6 were waited for; matrix products, arithmetic and copies ran while one was open for 14% of the time, Pallas kernels for 22%

commit v1 on v0

--- a/solution.py
+++ b/solution.py
@@ -71,8 +71,8 @@
 
 
 def layer_kernel(
-    info_ref, normed_ref, own_ref, other_ref, events_ref, follow_ref, hot_ref,
-    hidden_ref, positive_ref, send_ref, w_ref, act_ref, att_ref,
+    info_ref, normed_ref, own_ref, other_ref, events_ref, follow_ref,
+    hidden_ref, positive_ref, w_ref, act_ref, att_ref,
 ):
     core, length = info_ref[0], info_ref[1]
     for b in range(16):
@@ -115,6 +115,8 @@
         pos = jnp.sum(hidden.astype(F32) * follow_ref[rows, :].astype(F32), axis=1, keepdims=True)
         positive_ref[:, rows] = jnp.sum(jnp.where(eye, pos, 0.0), axis=0, keepdims=True)
 
+
+def pack_kernel(hot_ref, hidden_ref, send_ref):
     @pl.loop(0, SLOTS // B)
     def _(m):
         rows = pl.ds(pl.multiple_of(m * B, B), B)
@@ -209,8 +211,6 @@
     w_own = lax.all_to_all(
         jnp.broadcast_to(w_mine[None], (16,) + w_mine.shape), ("x", "z"), split_axis=0, concat_axis=0, tiled=True
     ).reshape(256, 2560)
-    w_other = swap(w_own)
-
     normed = call(norm_kernel, jax.ShapeDtypeStruct((1024, 512), BF), [VMEM], nbytes=2 << 20, flops=1 << 20)(ev)
 
     neg_slot = chip_slots(neg_ids)
@@ -222,8 +222,6 @@
     packed_own = lax.dynamic_slice(packed, (0, core * B), (CSLOTS, B))
     packed_other = lax.dynamic_slice(packed, (0, (1 - core) * B), (CSLOTS, B))
     packed_own = packed_own + swap(packed_other)
-    neg_own = chips_a2a(jnp.broadcast_to(packed_own[None], (NCHIPS, CSLOTS, B))).reshape(SLOTS, B)
-    neg_other = swap(neg_own)
     match = slot_ids[:, None] == neg_slot[None, :]
     slot_neg_id = jnp.sum(jnp.where(match, neg_ids[None, :] + 1, 0), axis=1) - 1
     slot_count = jnp.sum(jnp.where(match, neg_counts[None, :], 0), axis=1)
@@ -235,14 +233,19 @@
     index = jnp.stack([chip_row // 64, chip_row % 64]).astype(F32)
 
     follow = jnp.concatenate([ev[1:], jnp.zeros((1, width), BF)], axis=0)
-    hidden, positive, send_rows = call(
+    ids_col, logc_col = slot_neg_id[:, None], slot_logc[:, None]
+    w_own, normed, hot, ids_col, logc_col, follow, index, packed_own = lax.optimization_barrier(
+        (w_own, normed, hot, ids_col, logc_col, follow, index, packed_own)
+    )
+    neg_own = chips_a2a(jnp.broadcast_to(packed_own[None], (NCHIPS, CSLOTS, B))).reshape(SLOTS, B)
+    w_other = swap(w_own)
+    hidden, positive = call(
         layer_kernel,
         (
             jax.ShapeDtypeStruct((1024, width), BF),
             jax.ShapeDtypeStruct((1, 1024), F32),
-            jax.ShapeDtypeStruct((SLOTS, width), BF),
         ),
-        [SMEM] + [VMEM] * 6,
+        [SMEM] + [VMEM] * 5,
         scratch=[
             pltpu.VMEM((512, 2560), BF),
             pltpu.VMEM((1024, 2048), BF),
@@ -250,7 +253,12 @@
         ],
         flops=9 << 30,
         nbytes=12 << 20,
-    )(info, normed, w_own, w_other, ev, follow, hot)
+    )(info, normed, w_own, w_other, ev, follow)
+    neg_own, hidden = lax.optimization_barrier((neg_own, hidden))
+    neg_other = swap(neg_own)
+    send_rows = call(
+        pack_kernel, jax.ShapeDtypeStruct((SLOTS, width), BF), [VMEM] * 2, flops=2 << 30, nbytes=6 << 20
+    )(hot, hidden)
 
     recv_rows = chips_a2a(send_rows.reshape(NCHIPS, CSLOTS, width))
 
@@ -271,7 +279,7 @@
         flops=7 << 30,
         nbytes=12 << 20,
     )(
-        info, hidden, neg_own, neg_other, slot_neg_id[:, None], slot_logc[:, None], positive,
+        info, hidden, neg_own, neg_other, ids_col, logc_col, positive,
         target_ids, hot, index,
     )
     term = (term_own + swap(term_other).astype(F32)).astype(BF).reshape(NCHIPS, CSLOTS, B)

time: 152 us -> 144 us (0.947)
  waiting for transfers between devices: 43.3 us -> 30.9 us
  Pallas kernels: 44.5 us -> 46.6 us
    all_to_all x3, waiting for transfers between devices: 31.2 us -> 19.4 us  [chips_a2a(): return lax.all_to_all(v, CHIPS, split_axis=0, concat_axis=0, tiled=True)]
    pallas_call x0 -> x1, Pallas kernels: none -> 5.94 us  [per_device(): call(pack_kernel, jax.ShapeDtypeStruct((SLOTS, width), BF), [VMEM] * 2, f...]
    pallas_call x1, Pallas kernels: 17.8 us -> 13.9 us  [per_device(): call(layer_kernel, (jax.ShapeDtypeStruct((1024, width), BF), jax.ShapeDty...]
    all_to_all x3, starting transfers between devices: 16.9 us -> 19.9 us  [chips_a2a(): return lax.all_to_all(v, CHIPS, split_axis=0, concat_axis=0, tiled=True)]
    optimization_barrier x0 -> x2, local copies, waits for them, and re-layouts: none -> 2.36 us  [per_device(): lax.optimization_barrier((w_own, normed, hot, ids_col, logc_col, follow,...]
  transfers between devices with their start and end apart: 10 -> 10, of which waited for: 6 -> 6; matrix products, arithmetic and copies ran while one was open for 14% -> 13% of each run, Pallas kernels for 22% -> 24%
where the time goes in v1:
time: 144 us
  Pallas kernels  46.6 us (32%)
  starting transfers between devices  38.2 us (27%)
  waiting for transfers between devices  30.9 us (21%)
  other arithmetic  13.8 us (10%)
  local copies, waits for them, and re-layouts  11.5 us (8%)
  between operations  1.69 us (1%)
    all_to_all x3, starting transfers between devices, chips_a2a(): return lax.all_to_all(v, CHIPS, split_axis=0, concat_axis=0, tiled=True)  19.9 us
    all_to_all x3, waiting for transfers between devices, chips_a2a(): return lax.all_to_all(v, CHIPS, split_axis=0, concat_axis=0, tiled=True)  19.4 us
    pallas_call x1, Pallas kernels, per_device(): call(layer_kernel, (jax.ShapeDtypeStruct((1024, width), BF), jax.ShapeDty...  13.9 us
    pallas_call x1, Pallas kernels, per_device(): pl.pallas_call(place_kernel, grid=(ITEMS_DEV // tile,), out_shape=jax.Sha...  11.8 us
    pallas_call x1, Pallas kernels, per_device(): call(loss_kernel, (jax.ShapeDtypeStruct((1, 1024), F32), jax.ShapeDtypeSt...  11.8 us
    ppermute x6, starting transfers between devices, swap(): return lax.ppermute(v, 'c', SWAP)  10.4 us
    all_to_all x1, waiting for transfers between devices, per_device(): lax.all_to_all(jnp.broadcast_to(w_mine[None], (16,) + w_mine.shape), ('x'...  9.68 us
    all_to_all x1, starting transfers between devices, per_device(): lax.all_to_all(jnp.broadcast_to(w_mine[None], (16,) + w_mine.shape), ('x'...  7.82 us
  transfers between devices with their start and end apart: 10, of which 6 were waited for; matrix products, arithmetic and copies ran while one was open for 13% of the time, Pallas kernels for 24%

profile of v1, /device:TPU:1, one launch (start us, length us, event | category | flops | bytes accessed | tf_op | source)
XLA Modules:
  0.0 143.6 jit_solution(9634966698700766702)
XLA Ops:
  2.2 3.3 %gather_fusion = bf16[24,512]{1,0:T(8,128)(2,1)S(1)} fusion(bf16[4096,512]{1,0:T(8,128)(2,1)} %param.13, s32[1024]{0:T(1024)S(1)} %pad_clamp_fusion), kind=kCustom, calls=%fused_computation | custom fusion | bytes 49248 | tf_op jit(solution)/shard_map/gather | solution.py:221
  5.6 1.5 %collective-permute-start = (bf16[24,256]{1,0:T(8,128)(2,1)S(1)}, bf16[24,256]{1,0:T(8,128)(2,1)S(1)}, u32[]{:S(2)}, u32[]{:S(2)}) collective-permute-start(bf16[24,256]{1,0:T(8,128)(2,1)S(1)} %constant_dynamic-slice_fusion), channel_id=1, source_target_pairs={{0,1},{1,0},{2,3},{3,2},{4,5},{5,4},{6,7},{7,6},{8,9},{9,8},{10,11... | collective-permute-start | bytes 36872 | tf_op jit(solution)/shard_map/ppermute | solution.py:195
  7.1 1.2 broadcast_in_dim.85
  8.3 7.8 %all-to-all-start = ((bf16[16,16,2560]{2,1,0:T(8,128)(2,1)}), bf16[16,16,2560]{2,1,0:T(8,128)(2,1)S(1)}, u32[]{:S(2)}, u32[]{:S(2)}) async-start(bf16[16,16,2560]{2,1,0:T(8,128)(2,1)} %broadcast_in_dim.85), calls=%async_computation | async-start | bytes 2621440 | tf_op jit(solution)/shard_map/all_to_all | solution.py:211
  16.2 1.8 %select_reduce_fusion = (s32[1536]{0:T(1024)S(1)}, s32[1536]{0:T(1024)S(1)}) fusion(s32[1024]{0:T(1024)S(1)} %copy-done.7, s32[1024]{0:T(1024)S(1)} %get-tuple-element.67, s32[1024]{0:T(1024)S(1)} %get-tuple-element.61), kind=kLoop, calls=%fused_computation.1 | loop fusion | flops 7861248 | bytes 24576 | tf_op jit(solution)/shard_map/reduce_sum | solution.py:227
  18.9 3.2 %fusion.hot_ref = bf16[1536,1024]{1,0:T(8,128)(2,1)} fusion(s32[1024]{0:T(1024)S(1)} %bitcast.39), kind=kLoop, calls=%fused_computation.5 | loop fusion | flops 3145728 | bytes 3149824 | tf_op jit(solution)/shard_map/convert_element_type | solution.py:231
  22.6 1.1 concatenate.63.follow_ref
  23.7 3.2 %shard_map.95.normed_ref = bf16[1024,512]{1,0:T(8,128)(2,1)} custom-call(bf16[1024,512]{1,0:T(8,128)(2,1)} %bitcast.28), custom_call_target="tpu_custom_call" | custom-call | flops 1048576 | bytes 2097152 | tf_op jit(solution)/shard_map/pallas_call | solution.py:214
  26.9 9.7 %all-to-all-done = bf16[16,16,2560]{2,1,0:T(8,128)(2,1)S(1)} async-done(((bf16[16,16,2560]{2,1,0:T(8,128)(2,1)}), bf16[16,16,2560]{2,1,0:T(8,128)(2,1)S(1)}, u32[]{:S(2)}, u32[]{:S(2)}) %all-to-all-start) | async-done | bytes 1310752 | tf_op jit(solution)/shard_map/all_to_all | solution.py:211
  36.6 1.6 %collective-permute-start.1 = (bf16[256,2560]{1,0:T(8,128)(2,1)S(1)}, bf16[256,2560]{1,0:T(8,128)(2,1)}, u32[]{:S(2)}, u32[]{:S(2)}) collective-permute-start(bf16[256,2560]{1,0:T(8,128)(2,1)S(1)} %bitcast.33), channel_id=1, source_target_pairs={{0,1},{1,0},{2,3},{3,2},{4,5},{5,4},{6,7},{7,6},{8,9},{9,8},{10,11... | collective-permute-start | bytes 3932168 | tf_op jit(solution)/shard_map/ppermute | solution.py:195
  39.4 0.9 broadcast_in_dim.94
  40.3 7.4 %all-to-all-start.1 = ((bf16[64,24,256]{2,1,0:T(8,128)(2,1)}), bf16[64,24,256]{2,1,0:T(8,128)(2,1)}, u32[]{:S(2)}, u32[]{:S(2)}) async-start(bf16[64,24,256]{2,1,0:T(8,128)(2,1)} %broadcast_in_dim.94), calls=%async_computation.1 | async-start | bytes 1572864 | tf_op jit(solution)/shard_map/all_to_all | solution.py:199
  47.7 13.9 %shard_map.96 = (bf16[1024,512]{1,0:T(8,128)(2,1)}, f32[1,1024]{1,0:T(1,128)}) custom-call(s32[2]{0:T(128)} %pad_add_fusion.info_ref, bf16[1024,512]{1,0:T(8,128)(2,1)} %shard_map.95.normed_ref, bf16[256,2560]{1,0:T(8,128)(2,1)} %bitcast.34, bf16[256,2560]{1,0:T(8,128)(2,1)} %collective-permute-done.1.other_ref, bf16[1024,512]{1,0:T(8,128)(2,1)} %bitcast.29, ...), custom_call_target="tpu_custom_call" | custom-call | flops 9663676416 | bytes 12582912 | tf_op jit(solution)/shard_map/pallas_call | solution.py:242
  61.6 1.0 all-to-all-done.1
  62.7 1.7 %collective-permute-start.2 = (bf16[1536,256]{1,0:T(8,128)(2,1)}, bf16[1536,256]{1,0:T(8,128)(2,1)S(1)}, u32[]{:S(2)}, u32[]{:S(2)}) collective-permute-start(bf16[1536,256]{1,0:T(8,128)(2,1)} %bitcast.7.own_ref), channel_id=1, source_target_pairs={{0,1},{1,0},{2,3},{3,2},{4,5},{5,4},{6,7},{7,6},{8,9},{9,8},{10,11... | collective-permute-start | bytes 2359304 | tf_op jit(solution)/shard_map/ppermute | solution.py:195
  64.3 1.2 copy.31.ids_ref
  65.5 1.2 copy.32.logc_ref
  66.7 5.9 %shard_map.98 = bf16[1536,512]{1,0:T(8,128)(2,1)} custom-call(bf16[1536,1024]{1,0:T(8,128)(2,1)} %fusion.hot_ref, bf16[1024,512]{1,0:T(8,128)(2,1)} %get-tuple-element.23.hidden_ref), custom_call_target="tpu_custom_call" | custom-call | flops 2147483648 | bytes 6291456 | tf_op jit(solution)/shard_map/pallas_call | solution.py:259
  72.6 7.6 %all-to-all-start.3 = ((bf16[64,24,512]{2,1,0:T(8,128)(2,1)}), bf16[64,24,512]{2,1,0:T(8,128)(2,1)S(1)}, u32[]{:S(2)}, u32[]{:S(2)}) async-start(bf16[64,24,512]{2,1,0:T(8,128)(2,1)} %bitcast.32), calls=%async_computation.3 | async-start | bytes 3145728 | tf_op jit(solution)/shard_map/all_to_all | solution.py:199
  80.3 0.9 copy-done.6
  81.2 11.8 %shard_map.97 = (f32[1,1024]{1,0:T(1,128)}, f32[1536,256]{1,0:T(8,128)}, bf16[1536,256]{1,0:T(8,128)(2,1)}, bf16[16,1536]{1,0:T(8,128)(2,1)}) custom-call(s32[2]{0:T(128)} %pad_add_fusion.info_ref, bf16[1024,512]{1,0:T(8,128)(2,1)} %get-tuple-element.23.hidden_ref, bf16[1536,256]{1,0:T(8,128)(2,1)} %bitcast.7.own_ref, bf16[1536,256]{1,0:T(8,128)(2,1)} %copy-done.6, ...), custom_call_target="tpu_custom_call" | custom-call | flops 7516192768 | bytes 12582912 | tf_op jit(solution)/shard_map/pallas_call | solution.py:265
  94.2 1.2 collective-permute-done.3
  95.5 1.6 %add_convert_fusion = bf16[1536,256]{1,0:T(8,128)(2,1)S(1)} fusion(f32[1536,256]{1,0:T(8,128)} %get-tuple-element.31, bf16[1536,256]{1,0:T(8,128)(2,1)S(1)} %collective-permute-done.3), kind=kLoop, calls=%fused_computation.13 | loop fusion | flops 1179648 | bytes 3145728 | tf_op jit(solution)/shard_map/convert_element_type | solution.py:285
  97.0 1.1 fusion.8
  98.2 5.4 %all-to-all-done.3 = bf16[64,24,512]{2,1,0:T(8,128)(2,1)S(1)} async-done(((bf16[64,24,512]{2,1,0:T(8,128)(2,1)}), bf16[64,24,512]{2,1,0:T(8,128)(2,1)S(1)}, u32[]{:S(2)}, u32[]{:S(2)}) %all-to-all-start.3) | async-done | bytes 1572896 | tf_op jit(solution)/shard_map/all_to_all | solution.py:199
  103.5 4.9 %all-to-all-start.2 = ((bf16[64,32,256]{2,1,0:T(8,128)(2,1)}), bf16[64,32,256]{2,1,0:T(8,128)(2,1)S(1)}, u32[]{:S(2)}, u32[]{:S(2)}) async-start(bf16[64,32,256]{2,1,0:T(8,128)(2,1)} %fusion.8), calls=%async_computation.2 | async-start | bytes 2097152 | tf_op jit(solution)/shard_map/all_to_all | solution.py:199
  108.6 1.1 pad_maximum_fusion.1
  109.7 2.1 %collective-permute-start.5 = (bf16[64,16,512]{2,1,0:T(8,128)(2,1)}, bf16[64,16,512]{2,1,0:T(8,128)(2,1)}, u32[]{:S(2)}, u32[]{:S(2)}) collective-permute-start(bf16[64,16,512]{2,1,0:T(8,128)(2,1)} %get-tuple-element.44), channel_id=1, source_target_pairs={{0,1},{1,0},{2,3},{3,2},{4,5},{5,4},{6,7},{7,6},{8,9},{9,8},{10,11... | collective-permute-start | bytes 3145736 | tf_op jit(solution)/shard_map/ppermute | solution.py:195
  111.8 13.0 %all-to-all-done.2 = bf16[64,32,256]{2,1,0:T(8,128)(2,1)S(1)} async-done(((bf16[64,32,256]{2,1,0:T(8,128)(2,1)}), bf16[64,32,256]{2,1,0:T(8,128)(2,1)S(1)}, u32[]{:S(2)}, u32[]{:S(2)}) %all-to-all-start.2) | async-done | bytes 1048608 | tf_op jit(solution)/shard_map/all_to_all | solution.py:199
  125.7 3.4 %collective-permute-start.4 = (f32[32,256]{1,0:T(8,128)S(1)}, f32[32,256]{1,0:T(8,128)S(1)}, u32[]{:S(2)}, u32[]{:S(2)}) collective-permute-start(f32[32,256]{1,0:T(8,128)S(1)} %pad_maximum_fusion.6), channel_id=1, source_target_pairs={{0,1},{1,0},{2,3},{3,2},{4,5},{5,4},{6,7},{7,6},{8,9},{9,8},{10,11... | collective-permute-start | bytes 98312 | tf_op jit(solution)/shard_map/ppermute | solution.py:195
  130.1 1.7 %multiply_convert_fusion.rows_ref = bf16[2048,512]{1,0:T(8,128)(2,1)S(1)} fusion(bf16[1024,512]{1,0:T(8,128)(2,1)} %bitcast.14, bf16[1024,512]{1,0:T(8,128)(2,1)S(1)} %bitcast.30, f32[2048]{0:T(1024)S(1)} %pad_maximum_fusion.8), kind=kLoop, calls=%fused_computation.6 | loop fusion | flops 6291456 | bytes 4202496 | tf_op jit(solution)/shard_map/convert_element_type | solution.py:311
  131.8 11.8 %shard_map.99 = bf16[4096,512]{1,0:T(8,128)(2,1)} custom-call(s32[1,2048]{1,0:T(1,128)S(1)} %fusion.15.index_ref, bf16[2048,512]{1,0:T(8,128)(2,1)S(1)} %multiply_convert_fusion.rows_ref, s32[1,128]{1,0:T(1,128)S(1)} %add_bitcast_fusion.1.neg_index_ref, bf16[128,512]{1,0:T(8,128)(2,1)S(1)} %maximum_maximum_fusion.neg_ref), custom_call_target="tpu_custom_call" | custom-call | flops 9663676416 | bytes 8388608 | tf_op jit(solution)/shard_map/pallas_call | solution.py:326
  (75 shorter events, 6.8 us)
Async XLA Ops:
  0.6 1.2 copy-start.4
  0.6 6.5 %copy-start.2 = (bf16[16,2048]{1,0:T(8,128)(2,1)S(1)}, bf16[16,2048]{1,0:T(8,128)(2,1)}, u32[]{:S(2)}) copy-start(bf16[16,2048]{1,0:T(8,128)(2,1)} %param.14) | copy-start | bytes 196612
  0.7 6.5 %copy-start.3 = (bf16[16,512]{1,0:T(8,128)(2,1)S(1)}, bf16[16,512]{1,0:T(8,128)(2,1)}, u32[]{:S(2)}) copy-start(bf16[16,512]{1,0:T(8,128)(2,1)} %param.15) | copy-start | bytes 49156
  5.6 10.6 %copy-start.7 = (s32[1024]{0:T(1024)S(1)}, s32[1024]{0:T(1024)}, u32[]{:S(2)}) copy-start(s32[1024]{0:T(1024)} %param.12) | copy-start | bytes 12292
  5.6 12.4 %copy-start.5 = (s32[1,1024]{1,0:T(1,128)S(1)}, s32[1,1024]{1,0:T(1,128)}, u32[]{:S(2)}) copy-start(s32[1,1024]{1,0:T(1,128)} %targets_ref.1) | copy-start | bytes 12292
  5.6 21.3 %collective-permute-start = (bf16[24,256]{1,0:T(8,128)(2,1)S(1)}, bf16[24,256]{1,0:T(8,128)(2,1)S(1)}, u32[]{:S(2)}, u32[]{:S(2)}) collective-permute-start(bf16[24,256]{1,0:T(8,128)(2,1)S(1)} %constant_dynamic-slice_fusion), channel_id=1, source_target_pairs={{0,1},{1,0},{2,3},{3,2},{4,5},{5,4},{6,7},{7,6},{8,9},{9,8},{10,11... | collective-permute-start | bytes 36872 | tf_op jit(solution)/shard_map/ppermute | solution.py:195
  8.3 10.3 %copy-start = (bf16[1,1024,512]{2,1,0:T(8,128)(2,1)S(1)}, bf16[1,1024,512]{2,1,0:T(8,128)(2,1)}, u32[]{:S(2)}) copy-start(bf16[1,1024,512]{2,1,0:T(8,128)(2,1)} %param.8) | copy-start | bytes 3145732
  8.3 28.2 %all-to-all-start = ((bf16[16,16,2560]{2,1,0:T(8,128)(2,1)}), bf16[16,16,2560]{2,1,0:T(8,128)(2,1)S(1)}, u32[]{:S(2)}, u32[]{:S(2)}) async-start(bf16[16,16,2560]{2,1,0:T(8,128)(2,1)} %broadcast_in_dim.85), calls=%async_computation | async-start | bytes 2621440 | tf_op jit(solution)/shard_map/all_to_all | solution.py:211
  36.6 11.1 %copy-start.1 = (bf16[16,16,2560]{2,1,0:T(8,128)(2,1)}, bf16[16,16,2560]{2,1,0:T(8,128)(2,1)S(1)}, u32[]{:S(2)}) copy-start(bf16[16,16,2560]{2,1,0:T(8,128)(2,1)S(1)} %all-to-all-done) | copy-start | bytes 3932164
  36.6 11.1 %collective-permute-start.1 = (bf16[256,2560]{1,0:T(8,128)(2,1)S(1)}, bf16[256,2560]{1,0:T(8,128)(2,1)}, u32[]{:S(2)}, u32[]{:S(2)}) collective-permute-start(bf16[256,2560]{1,0:T(8,128)(2,1)S(1)} %bitcast.33), channel_id=1, source_target_pairs={{0,1},{1,0},{2,3},{3,2},{4,5},{5,4},{6,7},{7,6},{8,9},{9,8},{10,11... | collective-permute-start | bytes 3932168 | tf_op jit(solution)/shard_map/ppermute | solution.py:195
  40.3 22.4 %all-to-all-start.1 = ((bf16[64,24,256]{2,1,0:T(8,128)(2,1)}), bf16[64,24,256]{2,1,0:T(8,128)(2,1)}, u32[]{:S(2)}, u32[]{:S(2)}) async-start(bf16[64,24,256]{2,1,0:T(8,128)(2,1)} %broadcast_in_dim.94), calls=%async_computation.1 | async-start | bytes 1572864 | tf_op jit(solution)/shard_map/all_to_all | solution.py:199
  62.7 17.6 %collective-permute-start.2 = (bf16[1536,256]{1,0:T(8,128)(2,1)}, bf16[1536,256]{1,0:T(8,128)(2,1)S(1)}, u32[]{:S(2)}, u32[]{:S(2)}) collective-permute-start(bf16[1536,256]{1,0:T(8,128)(2,1)} %bitcast.7.own_ref), channel_id=1, source_target_pairs={{0,1},{1,0},{2,3},{3,2},{4,5},{5,4},{6,7},{7,6},{8,9},{9,8},{10,11... | collective-permute-start | bytes 2359304 | tf_op jit(solution)/shard_map/ppermute | solution.py:195
  72.6 30.9 %all-to-all-start.3 = ((bf16[64,24,512]{2,1,0:T(8,128)(2,1)}), bf16[64,24,512]{2,1,0:T(8,128)(2,1)S(1)}, u32[]{:S(2)}, u32[]{:S(2)}) async-start(bf16[64,24,512]{2,1,0:T(8,128)(2,1)} %bitcast.32), calls=%async_computation.3 | async-start | bytes 3145728 | tf_op jit(solution)/shard_map/all_to_all | solution.py:199
  80.3 0.9 copy-start.6
  93.0 2.5 %collective-permute-start.3 = (bf16[1536,256]{1,0:T(8,128)(2,1)}, bf16[1536,256]{1,0:T(8,128)(2,1)S(1)}, u32[]{:S(2)}, u32[]{:S(2)}) collective-permute-start(bf16[1536,256]{1,0:T(8,128)(2,1)} %get-tuple-element.32), channel_id=1, source_target_pairs={{0,1},{1,0},{2,3},{3,2},{4,5},{5,4},{6,7},{7,6},{8,9},{9,8},{10,11... | collective-permute-start | bytes 2359304 | tf_op jit(solution)/shard_map/ppermute | solution.py:195
  103.5 21.3 %all-to-all-start.2 = ((bf16[64,32,256]{2,1,0:T(8,128)(2,1)}), bf16[64,32,256]{2,1,0:T(8,128)(2,1)S(1)}, u32[]{:S(2)}, u32[]{:S(2)}) async-start(bf16[64,32,256]{2,1,0:T(8,128)(2,1)} %fusion.8), calls=%async_computation.2 | async-start | bytes 2097152 | tf_op jit(solution)/shard_map/all_to_all | solution.py:199
  109.7 20.3 %collective-permute-start.5 = (bf16[64,16,512]{2,1,0:T(8,128)(2,1)}, bf16[64,16,512]{2,1,0:T(8,128)(2,1)}, u32[]{:S(2)}, u32[]{:S(2)}) collective-permute-start(bf16[64,16,512]{2,1,0:T(8,128)(2,1)} %get-tuple-element.44), channel_id=1, source_target_pairs={{0,1},{1,0},{2,3},{3,2},{4,5},{5,4},{6,7},{7,6},{8,9},{9,8},{10,11... | collective-permute-start | bytes 3145736 | tf_op jit(solution)/shard_map/ppermute | solution.py:195
  125.7 4.3 %collective-permute-start.4 = (f32[32,256]{1,0:T(8,128)S(1)}, f32[32,256]{1,0:T(8,128)S(1)}, u32[]{:S(2)}, u32[]{:S(2)}) collective-permute-start(f32[32,256]{1,0:T(8,128)S(1)} %pad_maximum_fusion.6), channel_id=1, source_target_pairs={{0,1},{1,0},{2,3},{3,2},{4,5},{5,4},{6,7},{7,6},{8,9},{9,8},{10,11... | collective-permute-start | bytes 98312 | tf_op jit(solution)/shard_map/ppermute | solution.py:195

commit v2 on v1

--- a/solution.py
+++ b/solution.py
@@ -47,7 +47,7 @@
     return center * lax.rsqrt(spread + EPSILON)
 
 
-def call(body, out_shape, in_specs, scratch=(), flops=0, nbytes=0):
+def call(body, out_shape, in_specs, scratch=(), flops=0, nbytes=0, vmem=56):
     return pl.pallas_call(
         body,
         out_shape=out_shape,
@@ -55,15 +55,58 @@
         out_specs=jax.tree.map(lambda _: VMEM, out_shape),
         scratch_shapes=list(scratch),
         cost_estimate=pl.CostEstimate(flops=flops, bytes_accessed=nbytes, transcendentals=0),
-        compiler_params=pltpu.CompilerParams(vmem_limit_bytes=56 << 20),
+        compiler_params=pltpu.CompilerParams(vmem_limit_bytes=vmem << 20),
     )
 
 
-def norm_kernel(events_ref, out_ref):
+def onehot(base, count, index):
+    return (iota((count, index.shape[1]), 0) + base == index).astype(F32).astype(BF)
+
+
+def prep_kernel(
+    info_ref, events_ref, targets_ref, negs_ref, counts_ref,
+    normed_ref, ids_ref, logc_ref, slot_ref, index_ref, local_ref, tri_ref, owner_ref,
+):
+    core, chip = info_ref[0], info_ref[2]
+    targets, negs = targets_ref[...], negs_ref[...]
+    n = targets.shape[1]
+
+    for k in range(4):
+        rows = slice(k * B, (k + 1) * B)
+        tri_ref[rows, :] = (iota((B, n), 0) + k * B < iota((B, n), 1)).astype(F32).astype(BF)
+    t_owner, n_owner = targets >> 12, negs >> 12
+    owner_ref[:DEVS, :] = onehot(0, DEVS, t_owner)
+    owner_ref[DEVS:, :] = onehot(0, DEVS, n_owner)
+    before = dot(owner_ref[...], tri_ref[...]) * owner_ref[...].astype(F32)
+    t_rank = jnp.sum(before[:DEVS], axis=0, keepdims=True).astype(I32)
+    n_rank = jnp.sum(before[DEVS:], axis=0, keepdims=True).astype(I32)
+
+    def slot(owner, rank):
+        return (owner >> 1) * CSLOTS + jnp.where(rank < 8, (owner & 1) * 8 + rank, 8 + rank)
+
+    slot_ref[...] = slot(t_owner, t_rank)
+    n_slot = slot(n_owner, n_rank)
+    row = (targets & (2 * ITEMS_DEV - 1)) + 1
+    index_ref[0:1, :] = (row >> 6).astype(F32)
+    index_ref[1:2, :] = (row & 63).astype(F32)
+
+    mine = (iota((32, n), 0) + chip * CSLOTS == n_slot) & ((n_owner & 1) == core)
+    mine = mine & (iota((32, n), 0) < CSLOTS)
+    local = jnp.max(jnp.where(mine, negs & (ITEMS_DEV - 1), -1), axis=1, keepdims=True)
+    local_ref[...] = jnp.broadcast_to(local, (32, 128))
+    logs = jnp.log(counts_ref[...].astype(F32))
+    for m in range(SLOTS // B):
+        rows = slice(m * B, (m + 1) * B)
+        here = iota((B, n), 0) + m * B == n_slot
+        ids = jnp.max(jnp.where(here, negs, -1), axis=1, keepdims=True)
+        logc = jnp.min(jnp.where(here, logs, POS_INF), axis=1, keepdims=True)
+        ids_ref[rows, :] = jnp.broadcast_to(ids, (B, 128))
+        logc_ref[rows, :] = jnp.broadcast_to(logc, (B, 128))
+
     @pl.loop(0, 4)
     def _(i):
         rows = pl.ds(pl.multiple_of(i * B, B), B)
-        out_ref[rows, :] = layer_norm(events_ref[rows, :].astype(F32)).astype(BF)
+        normed_ref[rows, :] = layer_norm(events_ref[rows, :].astype(F32)).astype(BF)
 
 
 def silu_of_half(h):
@@ -116,15 +159,13 @@
         positive_ref[:, rows] = jnp.sum(jnp.where(eye, pos, 0.0), axis=0, keepdims=True)
 
 
-def pack_kernel(hot_ref, hidden_ref, send_ref):
-    @pl.loop(0, SLOTS // B)
-    def _(m):
-        rows = pl.ds(pl.multiple_of(m * B, B), B)
-        send_ref[rows, :] = dot(hot_ref[rows, :], hidden_ref[...]).astype(BF)
+def pack_kernel(slot_ref, hidden_ref, send_ref):
+    base = pl.program_id(0) * send_ref.shape[0]
+    send_ref[...] = dot(onehot(base, send_ref.shape[0], slot_ref[...]), hidden_ref[...]).astype(BF)
 
 
 def loss_kernel(
-    info_ref, hidden_ref, own_ref, other_ref, ids_ref, logc_ref, positive_ref, targets_ref, hot_ref,
+    info_ref, hidden_ref, own_ref, other_ref, ids_ref, logc_ref, positive_ref, targets_ref, slot_ref,
     index_ref, loss_ref, term_own_ref, term_other_ref, meta_ref, l_ref, probs_ref, coef_ref,
 ):
     core, length = info_ref[0], info_ref[1]
@@ -141,8 +182,10 @@
         target = targets_ref[:, at]
         top = pos
         for m in chunks:
-            value = dot_nt(own_ref[m, :], h_own) + dot_nt(other_ref[m, :], h_other) - logc_ref[m, :]
-            value = jnp.where(ids_ref[m, :] != target, value, NEG_INF)
+            logc, ids = logc_ref[m, :], ids_ref[m, :]
+            value = dot_nt(own_ref[m, :], h_own) + dot_nt(other_ref[m, :], h_other)
+            value = value - jnp.concatenate([logc, logc], axis=1)
+            value = jnp.where(jnp.concatenate([ids, ids], axis=1) != target, value, NEG_INF)
             l_ref[m, :] = value
             top = jnp.maximum(top, jnp.max(value, axis=0, keepdims=True))
         total = jnp.exp(pos - top)
@@ -164,7 +207,7 @@
         [high, middle, low, index_ref[...], jnp.zeros((11, 1024), F32)], axis=0
     ).astype(BF)
     for m in chunks:
-        meta_ref[:, m] = dot_nt(pieces, hot_ref[m, :]).astype(BF)
+        meta_ref[:, m] = dot_nt(pieces, onehot(m.start, B, slot_ref[...])).astype(BF)
         term_other_ref[m, :] = dot(probs_ref[m, :], hidden_ref[:, other_cols]).astype(BF)
         term_own_ref[m, :] = dot(probs_ref[m, :], hidden_ref[:, own_cols])
 
@@ -172,23 +215,10 @@
 def place_kernel(index_ref, rows_ref, neg_index_ref, neg_ref, out_ref):
     tile = out_ref.shape[0]
     base = pl.program_id(0) * tile
-
-    def onehot(index):
-        return (iota((tile, index.shape[1]), 0) + base == index).astype(F32).astype(BF)
-
     out_ref[...] = (
-        dot(onehot(index_ref[...]), rows_ref[...]) + dot(onehot(neg_index_ref[...]), neg_ref[...])
+        dot(onehot(base, tile, index_ref[...]), rows_ref[...])
+        + dot(onehot(base, tile, neg_index_ref[...]), neg_ref[...])
     ).astype(BF)
-
-
-def chip_slots(ids):
-    n = ids.shape[0]
-    owner = ids // ITEMS_DEV
-    hot = (iota((DEVS, n), 0) == owner[None, :]).astype(BF)
-    tri = (iota((n, n), 0) < iota((n, n), 1)).astype(BF)
-    rank = jnp.sum(dot(hot, tri) * hot.astype(F32), axis=0).astype(I32)
-    within = jnp.where(rank < 8, (owner % 2) * 8 + rank, 8 + rank)
-    return (owner // 2) * CSLOTS + within
 
 
 def swap(v):
@@ -203,41 +233,38 @@
     width = 512
     core = lax.axis_index("c")
     chip = lax.axis_index(CHIPS)
-    info = jnp.stack([core, lengths[0]]).astype(I32)
-    targets = target_ids[0]
+    info = jnp.stack([core, lengths[0], chip]).astype(I32)
     ev = events[0]
 
     w_mine = jnp.concatenate([w_uvqk, w_out], axis=1)
     w_own = lax.all_to_all(
         jnp.broadcast_to(w_mine[None], (16,) + w_mine.shape), ("x", "z"), split_axis=0, concat_axis=0, tiled=True
     ).reshape(256, 2560)
-    normed = call(norm_kernel, jax.ShapeDtypeStruct((1024, 512), BF), [VMEM], nbytes=2 << 20, flops=1 << 20)(ev)
-
-    neg_slot = chip_slots(neg_ids)
-    slot_ids = jnp.arange(SLOTS, dtype=I32)
-    here = iota((CSLOTS, 1), 0) + chip * CSLOTS == neg_slot[None, :]
-    mine = here & ((neg_ids // ITEMS_DEV) % 2 == core)[None, :]
-    neg_local = jnp.sum(jnp.where(mine, (neg_ids % ITEMS_DEV)[None, :] + 1, 0), axis=1) - 1
+    normed, ids, logc, target_slot, index, neg_local = call(
+        prep_kernel,
+        (
+            jax.ShapeDtypeStruct((1024, width), BF),
+            jax.ShapeDtypeStruct((SLOTS, 128), I32),
+            jax.ShapeDtypeStruct((SLOTS, 128), F32),
+            jax.ShapeDtypeStruct((1, 1024), I32),
+            jax.ShapeDtypeStruct((2, 1024), F32),
+            jax.ShapeDtypeStruct((32, 128), I32),
+        ),
+        [SMEM] + [VMEM] * 4,
+        scratch=[pltpu.VMEM((1024, 1024), BF), pltpu.VMEM((2 * DEVS, 1024), BF)],
+        vmem=16,
+    )(info, ev, target_ids, neg_ids[None], neg_counts[None])
+
+    neg_local = neg_local[:CSLOTS, 0]
     packed = jnp.where((neg_local >= 0)[:, None], item_table[jnp.maximum(neg_local, 0)], 0)
     packed_own = lax.dynamic_slice(packed, (0, core * B), (CSLOTS, B))
     packed_other = lax.dynamic_slice(packed, (0, (1 - core) * B), (CSLOTS, B))
     packed_own = packed_own + swap(packed_other)
-    match = slot_ids[:, None] == neg_slot[None, :]
-    slot_neg_id = jnp.sum(jnp.where(match, neg_ids[None, :] + 1, 0), axis=1) - 1
-    slot_count = jnp.sum(jnp.where(match, neg_counts[None, :], 0), axis=1)
-    slot_logc = jnp.where(slot_count > 0, jnp.log(slot_count.astype(F32)), POS_INF)
-
-    target_slot = chip_slots(targets)
-    hot = (slot_ids[:, None] == target_slot[None, :]).astype(BF)
-    chip_row = targets % (2 * ITEMS_DEV) + 1
-    index = jnp.stack([chip_row // 64, chip_row % 64]).astype(F32)
+    neg_block = jnp.broadcast_to(packed_own[None], (NCHIPS, CSLOTS, B))
 
     follow = jnp.concatenate([ev[1:], jnp.zeros((1, width), BF)], axis=0)
-    ids_col, logc_col = slot_neg_id[:, None], slot_logc[:, None]
-    w_own, normed, hot, ids_col, logc_col, follow, index, packed_own = lax.optimization_barrier(
-        (w_own, normed, hot, ids_col, logc_col, follow, index, packed_own)
-    )
-    neg_own = chips_a2a(jnp.broadcast_to(packed_own[None], (NCHIPS, CSLOTS, B))).reshape(SLOTS, B)
+    w_own, normed, follow, neg_block = lax.optimization_barrier((w_own, normed, follow, neg_block))
+    neg_own = chips_a2a(neg_block).reshape(SLOTS, B)
     w_other = swap(w_own)
     hidden, positive = call(
         layer_kernel,
@@ -253,12 +280,20 @@
         ],
         flops=9 << 30,
         nbytes=12 << 20,
+        vmem=24,
     )(info, normed, w_own, w_other, ev, follow)
-    neg_own, hidden = lax.optimization_barrier((neg_own, hidden))
+    whole = lambda shape: pl.BlockSpec(shape, lambda i: (0, 0))
+    send_rows = pl.pallas_call(
+        pack_kernel,
+        grid=(SLOTS // B,),
+        out_shape=jax.ShapeDtypeStruct((SLOTS, width), BF),
+        in_specs=[whole((1, 1024)), whole((1024, width))],
+        out_specs=pl.BlockSpec((B, width), lambda i: (i, 0)),
+        cost_estimate=pl.CostEstimate(flops=2 << 30, bytes_accessed=3 << 20, transcendentals=0),
+        compiler_params=pltpu.CompilerParams(vmem_limit_bytes=16 << 20),
+    )(target_slot, hidden)
+    neg_own, send_rows = lax.optimization_barrier((neg_own, send_rows))
     neg_other = swap(neg_own)
-    send_rows = call(
-        pack_kernel, jax.ShapeDtypeStruct((SLOTS, width), BF), [VMEM] * 2, flops=2 << 30, nbytes=6 << 20
-    )(hot, hidden)
 
     recv_rows = chips_a2a(send_rows.reshape(NCHIPS, CSLOTS, width))
 
@@ -278,9 +313,9 @@
         ],
         flops=7 << 30,
         nbytes=12 << 20,
+        vmem=28,
     )(
-        info, hidden, neg_own, neg_other, ids_col, logc_col, positive,
-        target_ids, hot, index,
+        info, hidden, neg_own, neg_other, ids, logc, positive, target_ids, target_slot, index,
     )
     term = (term_own + swap(term_other).astype(F32)).astype(BF).reshape(NCHIPS, CSLOTS, B)
     meta = meta[:8].reshape(8, NCHIPS, CSLOTS).transpose(1, 0, 2)
@@ -322,7 +357,6 @@
     neg_at = jnp.concatenate([neg_local, neg_local, jnp.full((rest,), -1, I32)])
 
     tile = 512
-    whole = lambda shape: pl.BlockSpec(shape, lambda i: (0, 0))
     grad = pl.pallas_call(
         place_kernel,
         grid=(ITEMS_DEV // tile,),
@@ -330,7 +364,7 @@
         in_specs=[whole((1, 2048)), whole((2048, width)), whole((1, 128)), whole((128, width))],
         out_specs=pl.BlockSpec((tile, width), lambda i: (i, 0)),
         cost_estimate=pl.CostEstimate(flops=9 << 30, bytes_accessed=8 << 20, transcendentals=0),
-        compiler_params=pltpu.CompilerParams(vmem_limit_bytes=48 << 20),
+        compiler_params=pltpu.CompilerParams(vmem_limit_bytes=24 << 20),
     )(row_at[None], rows, neg_at[None], neg_rows)
     return loss, grad
 

time: 144 us -> 133 us (0.924)
  other arithmetic: 13.8 us -> 6.86 us
  Pallas kernels: 46.6 us -> 40.3 us
  waiting for transfers between devices: 30.9 us -> 25.4 us
  local copies, waits for them, and re-layouts: 11.5 us -> 16.3 us
  starting transfers between devices: 38.2 us -> 42 us
    unnamed x20 -> x32, local copies, waits for them, and re-layouts: 1 us -> 7.47 us
    all_to_all x1, waiting for transfers between devices: 9.68 us -> 4.16 us  [per_device(): lax.all_to_all(jnp.broadcast_to(w_mine[None], (16,) + w_mine.shape), ('x'...]
    convert_element_type x3 -> x0, other arithmetic: 3.76 us -> none  [the longest x1 3.16 us: per_device(): hot = (slot_ids[:, None] == target_slot[None, :]).astype(BF)]
    pallas_call x1, Pallas kernels: 11.8 us -> 9 us  [per_device(): call(loss_kernel, (jax.ShapeDtypeStruct((1, 1024), F32), jax.ShapeDtypeSt...]
    all_to_all x3, starting transfers between devices: 19.9 us -> 22.3 us  [chips_a2a(): return lax.all_to_all(v, CHIPS, split_axis=0, concat_axis=0, tiled=True)]
    optimization_barrier x2 -> x0, local copies, waits for them, and re-layouts: 2.36 us -> none  [per_device(): lax.optimization_barrier((w_own, normed, hot, ids_col, logc_col, follow,...]
    pallas_call x1, Pallas kernels: 13.9 us -> 11.7 us  [per_device(): call(layer_kernel, (jax.ShapeDtypeStruct((1024, width), BF), jax.ShapeDty...]
    reduce_sum x2 -> x0, other arithmetic: 2.02 us -> none  [the longest x1 1.83 us: per_device(): slot_count = jnp.sum(jnp.where(match, neg_counts[None, :], 0), axis=1)]
  transfers between devices with their start and end apart: 10 -> 10, of which waited for: 6 -> 5; matrix products, arithmetic and copies ran while one was open for 13% -> 8% of each run, Pallas kernels for 24% -> 21%
where the time goes in v2:
time: 133 us; the launch traced here: 132 us
  starting transfers between devices  42 us (32%)
  Pallas kernels  40.3 us (30%)
  waiting for transfers between devices  25.4 us (19%)
  local copies, waits for them, and re-layouts  16.3 us (12%)
  other arithmetic  6.86 us (5%)
  between operations  1.58 us (1%)
    all_to_all x3, starting transfers between devices, chips_a2a(): return lax.all_to_all(v, CHIPS, split_axis=0, concat_axis=0, tiled=True)  22.3 us
    all_to_all x3, waiting for transfers between devices, chips_a2a(): return lax.all_to_all(v, CHIPS, split_axis=0, concat_axis=0, tiled=True)  18.9 us
    pallas_call x1, Pallas kernels, per_device(): pl.pallas_call(place_kernel, grid=(ITEMS_DEV // tile,), out_shape=jax.Sha...  11.8 us
    pallas_call x1, Pallas kernels, per_device(): call(layer_kernel, (jax.ShapeDtypeStruct((1024, width), BF), jax.ShapeDty...  11.7 us
    ppermute x6, starting transfers between devices, swap(): return lax.ppermute(v, 'c', SWAP)  11.2 us
    pallas_call x1, Pallas kernels, per_device(): call(loss_kernel, (jax.ShapeDtypeStruct((1, 1024), F32), jax.ShapeDtypeSt...  9 us
    all_to_all x1, starting transfers between devices, per_device(): lax.all_to_all(jnp.broadcast_to(w_mine[None], (16,) + w_mine.shape), ('x'...  8.43 us
    unnamed x32, local copies, waits for them, and re-layouts  7.47 us
  transfers between devices with their start and end apart: 10, of which 5 were waited for; matrix products, arithmetic and copies ran while one was open for 8% of the time, Pallas kernels for 21%

profile of v2, /device:TPU:1, one launch (start us, length us, event | category | flops | bytes accessed | tf_op | source)
XLA Modules:
  0.0 132.4 jit_solution(1719688547857871830)
XLA Ops:
  0.7 0.9 pad_maximum_fusion.2
  1.6 1.2 broadcast_in_dim.46
  2.8 8.4 %all-to-all-start = ((bf16[16,16,2560]{2,1,0:T(8,128)(2,1)}), bf16[16,16,2560]{2,1,0:T(8,128)(2,1)S(1)}, u32[]{:S(2)}, u32[]{:S(2)}) async-start(bf16[16,16,2560]{2,1,0:T(8,128)(2,1)} %broadcast_in_dim.46), calls=%async_computation | async-start | bytes 2621440 | tf_op jit(solution)/shard_map/all_to_all | solution.py:240
  12.0 3.9 %shard_map.95 = (bf16[1024,512]{1,0:T(8,128)(2,1)S(1)}, s32[1536,128]{1,0:T(8,128)S(1)}, f32[1536,128]{1,0:T(8,128)S(1)}, s32[1,1024]{1,0:T(1,128)S(1)}, f32[2,1024]{1,0:T(2,128)S(1)}, /*index=5*/s32[32,128]{1,0:T(8,128)S(1)}) custom-call(s32[3]{0:T(128)S(1)} %pad_add_fusion.info_ref, bf16[1024,512]{1,0:T(8,128)(2,1)S(1)} %bitcast.28, ...), custom_call_target="tpu_custom_call" | custom-call | tf_op jit(solution)/shard_map/pallas_call | solution.py:243
  15.9 1.0 copy-done.4
  17.8 3.5 %gather_fusion = bf16[24,512]{1,0:T(8,128)(2,1)S(1)} fusion(bf16[4096,512]{1,0:T(8,128)(2,1)} %param.13, s32[1024]{0:T(1024)S(1)} %pad_clamp_fusion), kind=kCustom, calls=%fused_computation | custom fusion | bytes 49248 | tf_op jit(solution)/shard_map/gather | solution.py:259
  21.6 1.0 collective-permute-start
  22.6 1.3 slice_bitcast_fusion
  23.8 1.3 concatenate.63.follow_ref
  25.2 4.2 %all-to-all-done = bf16[16,16,2560]{2,1,0:T(8,128)(2,1)S(1)} async-done(((bf16[16,16,2560]{2,1,0:T(8,128)(2,1)}), bf16[16,16,2560]{2,1,0:T(8,128)(2,1)S(1)}, u32[]{:S(2)}, u32[]{:S(2)}) %all-to-all-start) | async-done | bytes 1310752 | tf_op jit(solution)/shard_map/all_to_all | solution.py:240
  29.3 1.0 broadcast_in_dim.52
  30.3 3.7 %collective-permute-start.1 = (bf16[256,2560]{1,0:T(8,128)(2,1)S(1)}, bf16[256,2560]{1,0:T(8,128)(2,1)}, u32[]{:S(2)}, u32[]{:S(2)}) collective-permute-start(bf16[256,2560]{1,0:T(8,128)(2,1)S(1)} %bitcast.30), channel_id=1, source_target_pairs={{0,1},{1,0},{2,3},{3,2},{4,5},{5,4},{6,7},{7,6},{8,9},{9,8},{10,11... | collective-permute-start | bytes 3932168 | tf_op jit(solution)/shard_map/ppermute | solution.py:225
  34.0 7.1 %all-to-all-start.1 = ((bf16[64,24,256]{2,1,0:T(8,128)(2,1)}), bf16[64,24,256]{2,1,0:T(8,128)(2,1)}, u32[]{:S(2)}, u32[]{:S(2)}) async-start(bf16[64,24,256]{2,1,0:T(8,128)(2,1)} %broadcast_in_dim.52), calls=%async_computation.1 | async-start | bytes 1572864 | tf_op jit(solution)/shard_map/all_to_all | solution.py:229
  41.1 1.2 copy-done.5
  42.3 11.7 %shard_map.96 = (bf16[1024,512]{1,0:T(8,128)(2,1)S(1)}, f32[1,1024]{1,0:T(1,128)S(1)}) custom-call(s32[3]{0:T(128)S(1)} %pad_add_fusion.info_ref, bf16[1024,512]{1,0:T(8,128)(2,1)S(1)} %copy-done.5, bf16[256,2560]{1,0:T(8,128)(2,1)S(1)} %bitcast.31, bf16[256,2560]{1,0:T(8,128)(2,1)} %collective-permute-done.1.other_ref, bf16[1024,512]{1,0:T(8,128)(2,1)S(1)} %bitcast.29, ...), custom_call_target="tpu_custom_call" | custom-call | flops 9663676416 | bytes 12582912 | tf_op jit(solution)/shard_map/pallas_call | solution.py:269
  54.1 3.9 %shard_map.97 = bf16[1536,512]{1,0:T(8,128)(2,1)} custom-call(s32[1,1024]{1,0:T(1,128)S(1)} %get-tuple-element.27.slot_ref, bf16[1024,512]{1,0:T(8,128)(2,1)S(1)} %get-tuple-element.25.hidden_ref), custom_call_target="tpu_custom_call" | custom-call | flops 2147483648 | bytes 3145728 | tf_op jit(solution)/shard_map/pallas_call | solution.py:286
  58.0 1.0 copy-done.12
  59.2 10.1 %all-to-all-start.3 = ((bf16[64,24,512]{2,1,0:T(8,128)(2,1)}), bf16[64,24,512]{2,1,0:T(8,128)(2,1)}, u32[]{:S(2)}, u32[]{:S(2)}) async-start(bf16[64,24,512]{2,1,0:T(8,128)(2,1)} %bitcast.12), calls=%async_computation.3 | async-start | bytes 3145728 | tf_op jit(solution)/shard_map/all_to_all | solution.py:229
  69.3 0.9 copy-done.10
  70.2 1.1 copy-done.11
  71.4 1.2 copy-done.13
  72.6 9.0 %shard_map.98 = (f32[1,1024]{1,0:T(1,128)}, f32[1536,256]{1,0:T(8,128)S(1)}, bf16[1536,256]{1,0:T(8,128)(2,1)}, bf16[16,1536]{1,0:T(8,128)(2,1)S(1)}) custom-call(s32[3]{0:T(128)S(1)} %pad_add_fusion.info_ref, bf16[1024,512]{1,0:T(8,128)(2,1)S(1)} %copy-done.13, bf16[1536,256]{1,0:T(8,128)(2,1)} %bitcast.7.own_ref, bf16[1536,256]{1,0:T(8,128)(2,1)S(1)} %copy-done.11, ...), custom_call_target="tpu_custom_call" | custom-call | flops 7516192768 | bytes 12582912 | tf_op jit(solution)/shard_map/pallas_call | solution.py:300
  82.4 1.8 %collective-permute-done.3 = bf16[1536,256]{1,0:T(8,128)(2,1)S(1)} collective-permute-done((bf16[1536,256]{1,0:T(8,128)(2,1)}, bf16[1536,256]{1,0:T(8,128)(2,1)S(1)}, u32[]{:S(2)}, u32[]{:S(2)}) %collective-permute-start.3) | collective-permute-done | bytes 786464 | tf_op jit(solution)/shard_map/ppermute | solution.py:225
  84.3 1.1 fusion.1
  85.5 6.7 %all-to-all-done.3 = bf16[64,24,512]{2,1,0:T(8,128)(2,1)} async-done(((bf16[64,24,512]{2,1,0:T(8,128)(2,1)}), bf16[64,24,512]{2,1,0:T(8,128)(2,1)}, u32[]{:S(2)}, u32[]{:S(2)}) %all-to-all-start.3) | async-done | bytes 1572896 | tf_op jit(solution)/shard_map/all_to_all | solution.py:229
  92.2 5.1 %all-to-all-start.2 = ((bf16[64,32,256]{2,1,0:T(8,128)(2,1)}), bf16[64,32,256]{2,1,0:T(8,128)(2,1)S(1)}, u32[]{:S(2)}, u32[]{:S(2)}) async-start(bf16[64,32,256]{2,1,0:T(8,128)(2,1)} %fusion.1), calls=%async_computation.2 | async-start | bytes 2097152 | tf_op jit(solution)/shard_map/all_to_all | solution.py:229
  97.3 1.5 %broadcast_select_fusion.1 = (bf16[64,8,512]{2,1,0:T(8,128)(2,1)S(1)}, bf16[64,8,512]{2,1,0:T(8,128)(2,1)S(1)}, bf16[64,8,512]{2,1,0:T(8,128)(2,1)S(1)}) fusion(pred[]{:T(512)S(6)} %eq.2, bf16[64,24,512]{2,1,0:T(8,128)(2,1)} %all-to-all-done.3), kind=kLoop, calls=%fused_computation.11 | loop fusion | flops 524288 | bytes 3145729 | tf_op jit(solution)/shard_map/jit(_where)/select_n | solution.py:331
  99.1 2.4 %collective-permute-start.5 = (bf16[64,16,512]{2,1,0:T(8,128)(2,1)S(1)}, bf16[64,16,512]{2,1,0:T(8,128)(2,1)}, u32[]{:S(2)}, u32[]{:S(2)}) collective-permute-start(bf16[64,16,512]{2,1,0:T(8,128)(2,1)S(1)} %get-tuple-element.44), channel_id=1, source_target_pairs={{0,1},{1,0},{2,3},{3,2},{4,5},{5,4},{6,7},{7,6},{8,9},{9,8},{10,11... | collective-permute-start | bytes 3145736 | tf_op jit(solution)/shard_map/ppermute | solution.py:225
  101.4 12.2 %all-to-all-done.2 = bf16[64,32,256]{2,1,0:T(8,128)(2,1)S(1)} async-done(((bf16[64,32,256]{2,1,0:T(8,128)(2,1)}), bf16[64,32,256]{2,1,0:T(8,128)(2,1)S(1)}, u32[]{:S(2)}, u32[]{:S(2)}) %all-to-all-start.2) | async-done | bytes 1048608 | tf_op jit(solution)/shard_map/all_to_all | solution.py:229
  114.3 3.4 %collective-permute-start.4 = (f32[32,256]{1,0:T(8,128)S(1)}, f32[32,256]{1,0:T(8,128)S(1)}, u32[]{:S(2)}, u32[]{:S(2)}) collective-permute-start(f32[32,256]{1,0:T(8,128)S(1)} %pad_maximum_fusion.6), channel_id=1, source_target_pairs={{0,1},{1,0},{2,3},{3,2},{4,5},{5,4},{6,7},{7,6},{8,9},{9,8},{10,11... | collective-permute-start | bytes 98312 | tf_op jit(solution)/shard_map/ppermute | solution.py:225
  118.8 1.7 %multiply_convert_fusion.rows_ref = bf16[2048,512]{1,0:T(8,128)(2,1)S(1)} fusion(bf16[1024,512]{1,0:T(8,128)(2,1)} %bitcast.14, bf16[1024,512]{1,0:T(8,128)(2,1)S(1)} %bitcast.34, f32[2048]{0:T(1024)S(1)} %pad_maximum_fusion.8), kind=kLoop, calls=%fused_computation.1 | loop fusion | flops 6291456 | bytes 4202496 | tf_op jit(solution)/shard_map/convert_element_type | solution.py:346
  120.5 11.8 %shard_map.99 = bf16[4096,512]{1,0:T(8,128)(2,1)} custom-call(s32[1,2048]{1,0:T(1,128)S(1)} %fusion.4.index_ref, bf16[2048,512]{1,0:T(8,128)(2,1)S(1)} %multiply_convert_fusion.rows_ref, s32[1,128]{1,0:T(1,128)S(1)} %add_bitcast_fusion.1.neg_index_ref, bf16[128,512]{1,0:T(8,128)(2,1)S(1)} %maximum_maximum_fusion.neg_ref), custom_call_target="tpu_custom_call" | custom-call | flops 9663676416 | bytes 8388608 | tf_op jit(solution)/shard_map/pallas_call | solution.py:360
  (67 shorter events, 4.6 us)
Async XLA Ops:
  0.6 11.3 %copy-start = (bf16[1,1024,512]{2,1,0:T(8,128)(2,1)S(1)}, bf16[1,1024,512]{2,1,0:T(8,128)(2,1)}, u32[]{:S(2)}) copy-start(bf16[1,1024,512]{2,1,0:T(8,128)(2,1)} %param.8) | copy-start | bytes 3145732
  0.6 11.3 %copy-start.1 = (s32[1024]{0:T(1024)S(1)}, s32[1024]{0:T(1024)}, u32[]{:S(2)}) copy-start(s32[1024]{0:T(1024)} %param.11) | copy-start | bytes 12292
  0.7 11.3 %copy-start.2 = (s32[1024]{0:T(1024)S(1)}, s32[1024]{0:T(1024)}, u32[]{:S(2)}) copy-start(s32[1024]{0:T(1024)} %param.12) | copy-start | bytes 12292
  0.7 11.3 %copy-start.3 = (s32[1,1024]{1,0:T(1,128)S(1)}, s32[1,1024]{1,0:T(1,128)}, u32[]{:S(2)}) copy-start(s32[1,1024]{1,0:T(1,128)} %targets_ref.3) | copy-start | bytes 12292
  2.8 26.5 %all-to-all-start = ((bf16[16,16,2560]{2,1,0:T(8,128)(2,1)}), bf16[16,16,2560]{2,1,0:T(8,128)(2,1)S(1)}, u32[]{:S(2)}, u32[]{:S(2)}) async-start(bf16[16,16,2560]{2,1,0:T(8,128)(2,1)} %broadcast_in_dim.46), calls=%async_computation | async-start | bytes 2621440 | tf_op jit(solution)/shard_map/all_to_all | solution.py:240
  15.8 1.0 copy-start.4
  16.8 0.9 copy-start.8
  17.7 6.1 %copy-start.6 = (s32[1536,128]{1,0:T(8,128)}, s32[1536,128]{1,0:T(8,128)S(1)}, u32[]{:S(2)}) copy-start(s32[1536,128]{1,0:T(8,128)S(1)} %get-tuple-element.29.ids_ref) | copy-start | bytes 2359300
  21.6 3.6 %collective-permute-start = (bf16[24,256]{1,0:T(8,128)(2,1)S(1)}, bf16[24,256]{1,0:T(8,128)(2,1)S(1)}, u32[]{:S(2)}, u32[]{:S(2)}) collective-permute-start(bf16[24,256]{1,0:T(8,128)(2,1)S(1)} %constant_dynamic-slice_fusion), channel_id=1, source_target_pairs={{0,1},{1,0},{2,3},{3,2},{4,5},{5,4},{6,7},{7,6},{8,9},{9,8},{10,11... | collective-permute-start | bytes 36872 | tf_op jit(solution)/shard_map/ppermute | solution.py:225
  30.3 10.8 %collective-permute-start.1 = (bf16[256,2560]{1,0:T(8,128)(2,1)S(1)}, bf16[256,2560]{1,0:T(8,128)(2,1)}, u32[]{:S(2)}, u32[]{:S(2)}) collective-permute-start(bf16[256,2560]{1,0:T(8,128)(2,1)S(1)} %bitcast.30), channel_id=1, source_target_pairs={{0,1},{1,0},{2,3},{3,2},{4,5},{5,4},{6,7},{7,6},{8,9},{9,8},{10,11... | collective-permute-start | bytes 3932168 | tf_op jit(solution)/shard_map/ppermute | solution.py:225
  34.0 25.0 %all-to-all-start.1 = ((bf16[64,24,256]{2,1,0:T(8,128)(2,1)}), bf16[64,24,256]{2,1,0:T(8,128)(2,1)}, u32[]{:S(2)}, u32[]{:S(2)}) async-start(bf16[64,24,256]{2,1,0:T(8,128)(2,1)} %broadcast_in_dim.52), calls=%async_computation.1 | async-start | bytes 1572864 | tf_op jit(solution)/shard_map/all_to_all | solution.py:229
  41.1 1.2 copy-start.5
  58.0 1.0 copy-start.12
  58.9 11.3 %copy-start.7 = (s32[1536,128]{1,0:T(8,128)S(1)}, s32[1536,128]{1,0:T(8,128)}, u32[]{:S(2)}) copy-start(s32[1536,128]{1,0:T(8,128)} %copy-done.6) | copy-start | bytes 2359300
  58.9 11.3 %copy-start.9 = (f32[1536,128]{1,0:T(8,128)S(1)}, f32[1536,128]{1,0:T(8,128)}, u32[]{:S(2)}) copy-start(f32[1536,128]{1,0:T(8,128)} %copy-done.8) | copy-start | bytes 2359300
  59.0 10.3 %collective-permute-start.2 = (bf16[1536,256]{1,0:T(8,128)(2,1)}, bf16[1536,256]{1,0:T(8,128)(2,1)S(1)}, u32[]{:S(2)}, u32[]{:S(2)}) collective-permute-start(bf16[1536,256]{1,0:T(8,128)(2,1)} %bitcast.7.own_ref), channel_id=1, source_target_pairs={{0,1},{1,0},{2,3},{3,2},{4,5},{5,4},{6,7},{7,6},{8,9},{9,8},{10,11... | collective-permute-start | bytes 2359304 | tf_op jit(solution)/shard_map/ppermute | solution.py:225
  59.2 32.9 %all-to-all-start.3 = ((bf16[64,24,512]{2,1,0:T(8,128)(2,1)}), bf16[64,24,512]{2,1,0:T(8,128)(2,1)}, u32[]{:S(2)}, u32[]{:S(2)}) async-start(bf16[64,24,512]{2,1,0:T(8,128)(2,1)} %bitcast.12), calls=%async_computation.3 | async-start | bytes 3145728 | tf_op jit(solution)/shard_map/all_to_all | solution.py:229
  69.3 0.9 copy-start.10
  70.2 1.1 copy-start.11
  71.4 1.2 copy-start.13
  81.6 2.6 %collective-permute-start.3 = (bf16[1536,256]{1,0:T(8,128)(2,1)}, bf16[1536,256]{1,0:T(8,128)(2,1)S(1)}, u32[]{:S(2)}, u32[]{:S(2)}) collective-permute-start(bf16[1536,256]{1,0:T(8,128)(2,1)} %get-tuple-element.35), channel_id=1, source_target_pairs={{0,1},{1,0},{2,3},{3,2},{4,5},{5,4},{6,7},{7,6},{8,9},{9,8},{10,11... | collective-permute-start | bytes 2359304 | tf_op jit(solution)/shard_map/ppermute | solution.py:225
  92.2 21.4 %all-to-all-start.2 = ((bf16[64,32,256]{2,1,0:T(8,128)(2,1)}), bf16[64,32,256]{2,1,0:T(8,128)(2,1)S(1)}, u32[]{:S(2)}, u32[]{:S(2)}) async-start(bf16[64,32,256]{2,1,0:T(8,128)(2,1)} %fusion.1), calls=%async_computation.2 | async-start | bytes 2097152 | tf_op jit(solution)/shard_map/all_to_all | solution.py:229
  99.1 19.7 %collective-permute-start.5 = (bf16[64,16,512]{2,1,0:T(8,128)(2,1)S(1)}, bf16[64,16,512]{2,1,0:T(8,128)(2,1)}, u32[]{:S(2)}, u32[]{:S(2)}) collective-permute-start(bf16[64,16,512]{2,1,0:T(8,128)(2,1)S(1)} %get-tuple-element.44), channel_id=1, source_target_pairs={{0,1},{1,0},{2,3},{3,2},{4,5},{5,4},{6,7},{7,6},{8,9},{9,8},{10,11... | collective-permute-start | bytes 3145736 | tf_op jit(solution)/shard_map/ppermute | solution.py:225
  114.3 4.3 %collective-permute-start.4 = (f32[32,256]{1,0:T(8,128)S(1)}, f32[32,256]{1,0:T(8,128)S(1)}, u32[]{:S(2)}, u32[]{:S(2)}) collective-permute-start(f32[32,256]{1,0:T(8,128)S(1)} %pad_maximum_fusion.6), channel_id=1, source_target_pairs={{0,1},{1,0},{2,3},{3,2},{4,5},{5,4},{6,7},{7,6},{8,9},{9,8},{10,11... | collective-permute-start | bytes 98312 | tf_op jit(solution)/shard_map/ppermute | solution.py:225

commit v3 on v2

v3 whole, which is shorter than its diff:
```python
import math

import jax
import jax.numpy as jnp
from jax import lax
from jax.experimental import pallas as pl
from jax.experimental.pallas import tpu as pltpu
from jax.sharding import Mesh, PartitionSpec as P

H = 4
EPSILON = 1e-05
ALL = ("y", "x", "z", "c")
CHIPS = ("y", "x", "z")
MP = ("x", "z", "c")
BF = jnp.bfloat16
F32 = jnp.float32
I32 = jnp.int32
DEVS = 128
NCHIPS = 64
CSLOTS = 24
SLOTS = NCHIPS * CSLOTS
BLOCK = 2 * CSLOTS + 8
GROUP = 8
ITEMS_DEV = 4096
B = 256
TILE = 512
VMEM = pl.BlockSpec(memory_space=pltpu.VMEM)
SMEM = pl.BlockSpec(memory_space=pltpu.SMEM)
NT = (((1,), (1,)), ((), ()))
NEG_INF = float("-inf")
POS_INF = float("inf")
SWAP = ((0, 1), (1, 0))


def dot(a, b):
    return jnp.dot(a, b, preferred_element_type=F32)


def dot_nt(a, b):
    return lax.dot_general(a, b, NT, preferred_element_type=F32)


def iota(shape, dim):
    return lax.broadcasted_iota(I32, shape, dim)


def layer_norm(values):
    center = values - jnp.mean(values, axis=-1, keepdims=True)
    spread = jnp.mean(center * center, axis=-1, keepdims=True)
    return center * lax.rsqrt(spread + EPSILON)


def call(body, out_shape, in_specs, scratch=(), flops=0, nbytes=0, vmem=56):
    return pl.pallas_call(
        body,
        out_shape=out_shape,
        in_specs=in_specs,
        out_specs=jax.tree.map(lambda _: VMEM, out_shape),
        scratch_shapes=list(scratch),
        cost_estimate=pl.CostEstimate(flops=flops, bytes_accessed=nbytes, transcendentals=0),
        compiler_params=pltpu.CompilerParams(vmem_limit_bytes=vmem << 20),
    )


def onehot(base, count, index):
    return (iota((count, index.shape[1]), 0) + base == index).astype(F32).astype(BF)


def by_place(high, low, pieces, count, weights=(1.0, 1.0, 1.0)):
    rows = iota((count, high.shape[1]), 0) == high
    cols = onehot(0, 128, low)
    return sum(
        w * dot_nt(jnp.where(rows, p.astype(F32), 0.0).astype(BF), cols) for p, w in zip(pieces, weights)
    )


def prep_kernel(
    info_ref, events_ref, targets_ref, negs_ref, counts_ref,
    normed_ref, ids_ref, logc_ref, slot_ref, row_ref, local_ref, tri_ref, owner_ref, order_ref,
):
    core, chip = info_ref[0], info_ref[2]
    targets, negs = targets_ref[...], negs_ref[...]
    n = targets.shape[1]

    for k in range(4):
        rows = slice(k * B, (k + 1) * B)
        tri_ref[rows, :] = (iota((B, n), 0) + k * B < iota((B, n), 1)).astype(F32).astype(BF)
    t_owner, n_owner = targets >> 12, negs >> 12
    owner_ref[:DEVS, :] = onehot(0, DEVS, t_owner)
    owner_ref[DEVS:, :] = onehot(0, DEVS, n_owner)
    before = dot(owner_ref[...], tri_ref[...]) * owner_ref[...].astype(F32)
    t_rank = jnp.sum(before[:DEVS], axis=0, keepdims=True).astype(I32)
    n_rank = jnp.sum(before[DEVS:], axis=0, keepdims=True).astype(I32)

    def within(owner, rank):
        return jnp.where(rank < 8, (owner & 1) * 8 + rank, 8 + rank)

    t_within = within(t_owner, t_rank)
    slot_ref[0:1, :] = (t_owner >> 1) * CSLOTS + t_within
    slot_ref[1:2, :] = t_owner >> 1
    slot_ref[2:3, :] = t_within
    n_slot = (n_owner >> 1) * CSLOTS + within(n_owner, n_rank)
    row = (targets & (2 * ITEMS_DEV - 1)) + 1
    row_ref[0] = by_place(t_owner >> 1, t_within, [row >> 6], NCHIPS)
    row_ref[1] = by_place(t_owner >> 1, t_within, [row & 63], NCHIPS)

    mine = (iota((32, n), 0) + chip * CSLOTS == n_slot) & ((n_owner & 1) == core)
    mine = mine & (iota((32, n), 0) < CSLOTS)
    local = jnp.max(jnp.where(mine, negs & (ITEMS_DEV - 1), -1), axis=1, keepdims=True)
    local_ref[...] = jnp.broadcast_to(local, (32, 128))
    logs = jnp.log(counts_ref[...].astype(F32))
    for m in range(SLOTS // B):
        rows = slice(m * B, (m + 1) * B)
        here = iota((B, n), 0) + m * B == n_slot
        ids = jnp.max(jnp.where(here, negs, -1), axis=1, keepdims=True)
        logc = jnp.min(jnp.where(here, logs, POS_INF), axis=1, keepdims=True)
        ids_ref[rows, :] = jnp.broadcast_to(ids, (B, 128))
        logc_ref[rows, :] = jnp.broadcast_to(logc, (B, 128))

    k = iota((512, 512), 1)
    source = ((k & 255) >> 4) * 32 + jnp.where(k < 256, core, 1 - core) * 16 + (k & 15)
    order_ref[...] = (iota((512, 512), 0) == source).astype(F32).astype(BF)

    @pl.loop(0, 4)
    def _(i):
        rows = pl.ds(pl.multiple_of(i * B, B), B)
        normed = layer_norm(events_ref[rows, :].astype(F32)).astype(BF)
        normed_ref[rows, :] = dot(normed, order_ref[...]).astype(BF)


def block_of(rows, pieces):
    chips = rows.shape[0]
    pieces = [p[:, None, :] for p in pieces] + [jnp.zeros((chips, 8 - len(pieces), 128), F32)]
    return jnp.concatenate([rows[:, :, :128], rows[:, :, 128:]] + pieces, axis=1).astype(BF)


def neg_block_kernel(mine_ref, other_ref, row_ref, out_ref):
    rows = mine_ref[...].astype(F32) + other_ref[...].astype(F32)
    rows = jnp.broadcast_to(rows[None, :CSLOTS], (GROUP, CSLOTS, B))
    for g in range(NCHIPS // GROUP):
        chips = slice(g * GROUP, (g + 1) * GROUP)
        out_ref[chips] = block_of(rows, [row_ref[0, chips, :], row_ref[1, chips, :]])


def term_block_kernel(own_ref, other_ref, meta_ref, out_ref):
    for g in range(NCHIPS // GROUP):
        chips = slice(g * GROUP, (g + 1) * GROUP)
        slots = slice(g * GROUP * CSLOTS, (g + 1) * GROUP * CSLOTS)
        rows = (own_ref[slots, :] + other_ref[slots, :].astype(F32)).reshape(GROUP, CSLOTS, B)
        out_ref[chips] = block_of(rows, [meta_ref[k, chips, :] for k in range(3)])


def unpack_kernel(own_ref, other_ref, own_out_ref, other_out_ref, row_ref):
    for k, (block_ref, out_ref) in enumerate(((own_ref, own_out_ref), (other_ref, other_out_ref))):
        for g in range(NCHIPS // GROUP):
            chips = slice(g * GROUP, (g + 1) * GROUP)
            block = block_ref[chips].astype(F32)
            halves = [
                block[:, h * CSLOTS : (h + 1) * CSLOTS].reshape(GROUP * CSLOTS, 128) for h in range(2)
            ]
            slots = slice(g * GROUP * CSLOTS, (g + 1) * GROUP * CSLOTS)
            out_ref[slots, :] = jnp.concatenate(halves, axis=1).astype(BF)
            numbers = block[:, 2 * CSLOTS :]
            row_ref[k, chips, :] = (numbers[:, 0] * 64.0 + numbers[:, 1]).astype(I32)


def silu_of_half(h):
    return h + h * jnp.tanh(h)


def layer_kernel(
    info_ref, slot_ref, own_hbm, normed_hbm, other_hbm, events_hbm, follow_hbm,
    positive_ref, hidden_hbm, send_hbm,
    w_ref, own_ref, other_ref, normed_ref, events_ref, follow_ref, act_ref, att_ref, hidden_ref, send_ref, in_sem, out_sem,
):
    core, length = info_ref[0], info_ref[1]
    pairs = (
        (normed_hbm, normed_ref), (own_hbm, own_ref), (other_hbm, other_ref),
        (events_hbm, events_ref), (follow_hbm, follow_ref),
    )
    inputs = [pltpu.make_async_copy(source, to, in_sem.at[k]) for k, (source, to) in enumerate(pairs)]
    for copy in inputs:
        copy.start()
    for copy in inputs[:3]:
        copy.wait()

    @pl.loop(0, 4)
    def _(i):
        rows = pl.ds(pl.multiple_of(i * B, B), B)
        a = normed_ref[rows, :B]
        b = normed_ref[rows, B:]
        live = iota((B, 512), 0) + i * B < length
        for n in range(4):
            cols = slice(n * 512, (n + 1) * 512)
            v = silu_of_half(0.5 * (dot(a, own_ref[:, cols]) + dot(b, other_ref[:, cols])))
            if n == 1:
                v = jnp.where(live, v, 0.0)
            act_ref[rows, cols] = v.astype(BF)

    for b in range(16):
        block = slice(b * 16, (b + 1) * 16)
        w_ref[pl.ds(pl.multiple_of(b * 32 + core * 16, 16), 16), :] = own_ref[block, 2048:]
        w_ref[pl.ds(pl.multiple_of(b * 32 + (1 - core) * 16, 16), 16), :] = other_ref[block, 2048:]
    for copy in inputs[3:]:
        copy.wait()
    causal = iota((B, B), 1) <= iota((B, B), 0)
    eye = iota((B, B), 1) == iota((B, B), 0)
    scale = 0.5 / math.sqrt(128)
    for i in range(4):
        rows = slice(i * B, (i + 1) * B)
        for h in range(H):
            q = act_ref[rows, 1024 + h * 128 : 1024 + (h + 1) * 128]
            total = None
            for j in range(i + 1):
                keys = slice(j * B, (j + 1) * B)
                s = dot_nt(q, act_ref[keys, 1536 + h * 128 : 1536 + (h + 1) * 128])
                w = silu_of_half(s * scale)
                if j == i:
                    w = jnp.where(causal, w, 0.0)
                t = dot(w.astype(BF), act_ref[keys, 512 + h * 128 : 512 + (h + 1) * 128])
                total = t if total is None else total + t
            att_ref[:, h * 128 : (h + 1) * 128] = total
        gated = (layer_norm(att_ref[...]) * act_ref[rows, :512].astype(F32)).astype(BF)
        hidden = (events_ref[rows, :].astype(F32) + dot(gated, w_ref[...])).astype(BF)
        hidden_ref[rows, :] = hidden
        pos = jnp.sum(hidden.astype(F32) * follow_ref[rows, :].astype(F32), axis=1, keepdims=True)
        positive_ref[:, rows] = jnp.sum(jnp.where(eye, pos, 0.0), axis=0, keepdims=True)

    hidden_out = pltpu.make_async_copy(hidden_ref, hidden_hbm, out_sem.at[0])
    hidden_out.start()
    outs = []
    for m in range(SLOTS // B):
        rows = slice(m * B, (m + 1) * B)
        send_ref[rows, :] = dot(onehot(m * B, B, slot_ref[0:1, :]), hidden_ref[...]).astype(BF)
        outs.append(pltpu.make_async_copy(send_ref.at[rows, :], send_hbm.at[rows, :], out_sem.at[1 + m]))
        outs[-1].start()
    hidden_out.wait()
    for copy in outs:
        copy.wait()


def loss_kernel(
    info_ref, hidden_ref, own_ref, other_ref, ids_ref, logc_ref, positive_ref, targets_ref, slot_ref,
    loss_ref, term_own_ref, term_other_ref, meta_ref, l_ref, probs_ref, coef_ref,
):
    core, length = info_ref[0], info_ref[1]
    own_cols = pl.ds(pl.multiple_of(core * B, B), B)
    other_cols = pl.ds(pl.multiple_of((1 - core) * B, B), B)
    chunks = [slice(m * B, (m + 1) * B) for m in range(SLOTS // B)]

    @pl.loop(0, 4)
    def _(t):
        at = pl.ds(pl.multiple_of(t * B, B), B)
        h_own = hidden_ref[at, own_cols]
        h_other = hidden_ref[at, other_cols]
        pos = positive_ref[:, at]
        target = targets_ref[:, at]
        top = pos
        for m in chunks:
            logc, ids = logc_ref[m, :], ids_ref[m, :]
            value = dot_nt(own_ref[m, :], h_own) + dot_nt(other_ref[m, :], h_other)
            value = value - jnp.concatenate([logc, logc], axis=1)
            value = jnp.where(jnp.concatenate([ids, ids], axis=1) != target, value, NEG_INF)
            l_ref[m, :] = value
            top = jnp.maximum(top, jnp.max(value, axis=0, keepdims=True))
        total = jnp.exp(pos - top)
        for m in chunks:
            total = total + jnp.sum(jnp.exp(l_ref[m, :] - top), axis=0, keepdims=True)
        log_total = top + jnp.log(total)
        in_range = iota((1, B), 1) + t * B < length - 1
        loss_ref[:, at] = jnp.where(in_range, log_total - pos, 0.0)
        coef_ref[:, at] = jnp.where(in_range, jnp.exp(pos - log_total) - 1.0, 0.0)
        shift = jnp.where(in_range, log_total, POS_INF)
        for m in chunks:
            probs_ref[m, at] = jnp.exp(l_ref[m, :] - shift).astype(BF)

    coef = coef_ref[...]
    high = coef.astype(BF).astype(F32)
    middle = (coef - high).astype(BF).astype(F32)
    low = coef - high - middle
    for k, piece in enumerate((high, middle, low)):
        meta_ref[k] = by_place(slot_ref[1:2, :], slot_ref[2:3, :], [piece], NCHIPS)
    for m in chunks:
        term_other_ref[m, :] = dot(probs_ref[m, :], hidden_ref[:, other_cols]).astype(BF)
        term_own_ref[m, :] = dot(probs_ref[m, :], hidden_ref[:, own_cols])


def order_kernel(key_ref, key_col_ref, rows_ref, sorted_ref, at_ref, sorted_key_ref, start_ref):
    n = key_ref.shape[1]
    key = key_ref[...]
    at = jnp.zeros((1, n), F32)
    for m in range(n // B):
        col = key_col_ref[m * B : (m + 1) * B, :]
        col = jnp.concatenate([col] * (n // 128), axis=1)
        at = at + jnp.sum((col < key).astype(F32), axis=0, keepdims=True)
    at = at.astype(I32)
    at_ref[...] = at
    row = key >> 11
    for i in range(ITEMS_DEV // TILE + 1):
        start_ref[i] = jnp.sum((row < i * TILE).astype(I32))
    sorted_key_ref[...] = by_place(at >> 7, at & 127, [row >> 6, row & 63], n // 128, (64.0, 1.0)).astype(I32)
    for m in range(n // B):
        block = slice(m * B, (m + 1) * B)
        sorted_ref[block, :] = dot(onehot(m * B, B, at), rows_ref[...]).astype(BF)


def place_kernel(
    start_ref, coef_ref, at_ref, key_ref, rows_ref, neg_index_ref, neg_ref, out_ref, scaled_ref, total_ref
):
    n = coef_ref.shape[1]
    i = pl.program_id(0)
    base = i * TILE

    @pl.when(i == 0)
    def _():
        coef = coef_ref[...]
        top = coef.astype(BF).astype(F32)
        middle = (coef - top).astype(BF).astype(F32)
        at = at_ref[...]
        coef = by_place(at >> 7, at & 127, [top, middle, coef - top - middle], n // 128)
        eye = iota((128, 128), 1) == iota((128, 128), 0)
        for m in range(n // 128):
            block = slice(m * 128, (m + 1) * 128)
            col = jnp.sum(jnp.where(eye, coef[m : m + 1, :], 0.0), axis=1, keepdims=True)
            scaled_ref[block, :] = (rows_ref[block, :].astype(F32) * col).astype(BF)

    total_ref[...] = dot(onehot(base, TILE, neg_index_ref[...]), neg_ref[...])

    @pl.loop(start_ref[i] // B, (start_ref[i + 1] + B - 1) // B)
    def _(j):
        block = pl.ds(pl.multiple_of(j * B, B), B)
        key = jnp.concatenate([key_ref[pl.ds(2 * j, 1), :], key_ref[pl.ds(2 * j + 1, 1), :]], axis=1)
        total_ref[...] += dot(onehot(base, TILE, key), scaled_ref[block, :])

    out_ref[...] = total_ref[...].astype(BF)


def swap(v):
    return lax.ppermute(v, "c", SWAP)


def chips_a2a(v):
    return lax.all_to_all(v, CHIPS, split_axis=0, concat_axis=0, tiled=True)


def per_device(events, lengths, target_ids, neg_ids, neg_counts, item_table, w_uvqk, w_out):
    width = 512
    core = lax.axis_index("c")
    chip = lax.axis_index(CHIPS)
    info = jnp.stack([core, lengths[0], chip]).astype(I32)
    ev = events[0]

    w_mine = jnp.concatenate([w_uvqk, w_out], axis=1)
    w_own = lax.all_to_all(
        jnp.broadcast_to(w_mine[None], (16,) + w_mine.shape), ("x", "z"), split_axis=0, concat_axis=0, tiled=True
    ).reshape(256, 2560)

    normed, ids, logc, target_slot, send_row, neg_local = call(
        prep_kernel,
        (
            jax.ShapeDtypeStruct((1024, width), BF),
            jax.ShapeDtypeStruct((SLOTS, 128), I32),
            jax.ShapeDtypeStruct((SLOTS, 128), F32),
            jax.ShapeDtypeStruct((3, 1024), I32),
            jax.ShapeDtypeStruct((2, NCHIPS, 128), F32),
            jax.ShapeDtypeStruct((32, 128), I32),
        ),
        [SMEM] + [VMEM] * 4,
        scratch=[pltpu.VMEM((1024, 1024), BF), pltpu.VMEM((2 * DEVS, 1024), BF), pltpu.VMEM((512, 512), BF)],
        vmem=16,
    )(info, ev, target_ids, neg_ids[None], neg_counts[None])

    neg_local = neg_local[:, 0]
    packed = jnp.where((neg_local >= 0)[:, None], item_table[jnp.maximum(neg_local, 0)], 0)
    packed_own = lax.dynamic_slice(packed, (0, core * B), (32, B))
    packed_other = lax.dynamic_slice(packed, (0, (1 - core) * B), (32, B))
    neg_block = call(
        neg_block_kernel, jax.ShapeDtypeStruct((NCHIPS, BLOCK, 128), BF), [VMEM] * 3, vmem=8
    )(packed_own, swap(packed_other), send_row)

    follow = jnp.concatenate([ev[1:], jnp.zeros((1, width), BF)], axis=0)
    w_own, normed, follow, neg_block = lax.optimization_barrier((w_own, normed, follow, neg_block))
    got_neg = chips_a2a(neg_block)
    w_other = swap(w_own)
    any_space = pl.BlockSpec(memory_space=pl.ANY)
    positive, hidden, send_rows = pl.pallas_call(
        layer_kernel,
        out_shape=(
            jax.ShapeDtypeStruct((1, 1024), F32),
            jax.ShapeDtypeStruct((1024, width), BF),
            jax.ShapeDtypeStruct((SLOTS, width), BF),
        ),
        in_specs=[SMEM, VMEM] + [any_space] * 5,
        out_specs=(VMEM, any_space, any_space),
        scratch_shapes=[
            pltpu.VMEM((512, 512), BF),
            pltpu.VMEM((256, 2560), BF),
            pltpu.VMEM((256, 2560), BF),
            pltpu.VMEM((1024, width), BF),
            pltpu.VMEM((1024, width), BF),
            pltpu.VMEM((1024, width), BF),
            pltpu.VMEM((1024, 2048), BF),
            pltpu.VMEM((B, width), F32),
            pltpu.VMEM((1024, width), BF),
            pltpu.VMEM((SLOTS, width), BF),
            pltpu.SemaphoreType.DMA((5,)),
            pltpu.SemaphoreType.DMA((7,)),
        ],
        cost_estimate=pl.CostEstimate(flops=0, bytes_accessed=0, transcendentals=0),
        compiler_params=pltpu.CompilerParams(vmem_limit_bytes=56 << 20),
    )(info, target_slot, w_own, normed, w_other, ev, follow)
    got_neg, send_rows = lax.optimization_barrier((got_neg, send_rows))
    other_neg = swap(got_neg)

    neg_own, neg_other, row_table = call(
        unpack_kernel,
        (
            jax.ShapeDtypeStruct((SLOTS, B), BF),
            jax.ShapeDtypeStruct((SLOTS, B), BF),
            jax.ShapeDtypeStruct((2, NCHIPS, 128), I32),
        ),
        [VMEM] * 2,
        vmem=16,
    )(got_neg, other_neg)

    recv_rows = chips_a2a(send_rows.reshape(NCHIPS, CSLOTS, width))

    loss, term_own, term_other, meta = call(
        loss_kernel,
        (
            jax.ShapeDtypeStruct((1, 1024), F32),
            jax.ShapeDtypeStruct((SLOTS, B), F32),
            jax.ShapeDtypeStruct((SLOTS, B), BF),
            jax.ShapeDtypeStruct((3, NCHIPS, 128), F32),
        ),
        [SMEM] + [VMEM] * 8,
        scratch=[
            pltpu.VMEM((SLOTS, B), F32),
            pltpu.VMEM((SLOTS, 1024), BF),
            pltpu.VMEM((1, 1024), F32),
        ],
        flops=0,
        nbytes=0,
        vmem=28,
    )(
        info, hidden, neg_own, neg_other, ids, logc, positive, target_ids, target_slot,
    )
    block = call(
        term_block_kernel, jax.ShapeDtypeStruct((NCHIPS, BLOCK, 128), BF), [VMEM] * 3, vmem=16
    )(term_own, swap(term_other), meta)
    recv_rows, block = lax.optimization_barrier((recv_rows, block))
    got = chips_a2a(block)

    def split(v):
        first, second, last = v[:, :8], v[:, 8:16], v[:, 16:]
        keep = jnp.where(core == 0, first, second)
        give = jnp.where(core == 0, second, first)
        return jnp.concatenate([keep, last], axis=1), jnp.concatenate([give, last], axis=1)

    rows_keep, rows_give = split(recv_rows)
    rows_got = swap(rows_give)
    rows = jnp.concatenate([rows_keep.reshape(-1, width), rows_got.reshape(-1, width)], axis=0)
    first, _ = split(row_table[0, :, :CSLOTS])
    second, _ = split(row_table[1, :, :CSLOTS])
    row_at = jnp.concatenate([first.reshape(-1), second.reshape(-1)]) - 1 - core * ITEMS_DEV
    row_at = jnp.where((row_at >= 0) & (row_at < ITEMS_DEV), row_at, 2 * ITEMS_DEV - 1)
    count = row_at.shape[0]
    key = row_at * count + jnp.arange(count, dtype=I32)
    rows, at, sorted_key, starts = pl.pallas_call(
        order_kernel,
        out_shape=(
            jax.ShapeDtypeStruct((count, width), BF),
            jax.ShapeDtypeStruct((1, count), I32),
            jax.ShapeDtypeStruct((count // 128, 128), I32),
            jax.ShapeDtypeStruct((32,), I32),
        ),
        in_specs=[VMEM] * 3,
        out_specs=(VMEM, VMEM, VMEM, SMEM),
        cost_estimate=pl.CostEstimate(flops=0, bytes_accessed=0, transcendentals=0),
        compiler_params=pltpu.CompilerParams(vmem_limit_bytes=24 << 20),
    )(key[None], jnp.broadcast_to(key[:, None], (count, 128)), rows)

    got, rows, at, sorted_key, starts = lax.optimization_barrier((got, rows, at, sorted_key, starts))
    summed = jnp.sum(got[:, : 2 * CSLOTS].astype(F32), axis=0)
    summed = jnp.concatenate([summed[:CSLOTS], summed[CSLOTS:]], axis=1)
    got_coef = jnp.sum(got[:, 2 * CSLOTS : 2 * CSLOTS + 3, :CSLOTS].astype(F32), axis=1)
    coef_keep, coef_give = split(got_coef)
    small = swap(jnp.concatenate([summed, coef_give.reshape(4, B)], axis=0))
    summed_got = small[:CSLOTS]
    coef_all = jnp.concatenate([coef_keep.reshape(-1), small[CSLOTS:].reshape(-1)])

    neg_sum = jnp.where(
        core == 0,
        jnp.concatenate([summed, summed_got], axis=1),
        jnp.concatenate([summed_got, summed], axis=1),
    )
    neg_high = neg_sum.astype(BF)
    neg_low = (neg_sum - neg_high.astype(F32)).astype(BF)
    rest = 128 - 2 * CSLOTS
    neg_rows = jnp.concatenate([neg_high, neg_low, jnp.zeros((rest, width), BF)], axis=0)
    neg_at = jnp.concatenate([neg_local[:CSLOTS], neg_local[:CSLOTS], jnp.full((rest,), -1, I32)])

    whole = lambda shape: pl.BlockSpec(shape, lambda i: (0, 0))
    grad = pl.pallas_call(
        place_kernel,
        grid=(ITEMS_DEV // TILE,),
        out_shape=jax.ShapeDtypeStruct((ITEMS_DEV, width), BF),
        in_specs=[SMEM] + [whole((1, count))] * 2 + [whole((count // 128, 128)), whole((count, width)), whole((1, 128)), whole((128, width))],
        out_specs=pl.BlockSpec((TILE, width), lambda i: (i, 0)),
        scratch_shapes=[pltpu.VMEM((count, width), BF), pltpu.VMEM((TILE, width), F32)],
        cost_estimate=pl.CostEstimate(flops=0, bytes_accessed=0, transcendentals=0),
        compiler_params=pltpu.CompilerParams(vmem_limit_bytes=24 << 20),
    )(starts, coef_all[None], at, sorted_key, rows, neg_at[None], neg_rows)
    return loss, grad


def solution(mesh):
    fine = Mesh(mesh.devices.reshape(4, 4, 4, 2), ALL)
    in_specs = (P(ALL), P(ALL), P(ALL), P(), P(), P(ALL), P(MP), P(MP))
    return jax.shard_map(
        per_device, mesh=fine, in_specs=in_specs, out_specs=(P(ALL), P(ALL)), check_vma=False
    )
```

time: 133 us -> 129 us (0.970)
  Pallas kernels: 40.3 us -> 46.7 us
  waiting for transfers between devices: 25.4 us -> 20.3 us
  starting transfers between devices: 42 us -> 39 us
  local copies, waits for them, and re-layouts: 16.3 us -> 14.3 us
    pallas_call x3 -> x6, Pallas kernels: 27.4 us -> 34 us  [the longest x1 15.9 us: per_device(): pl.pallas_call(layer_kernel, out_shape=(jax.ShapeDtypeStruct((1, 1024), F...]
    all_to_all x3, waiting for transfers between devices: 18.9 us -> 16 us  [chips_a2a(): return lax.all_to_all(v, CHIPS, split_axis=0, concat_axis=0, tiled=True)]
    all_to_all x1, waiting for transfers between devices: 4.16 us -> 1.65 us  [per_device(): lax.all_to_all(jnp.broadcast_to(w_mine[None], (16,) + w_mine.shape), ('x'...]
    convert_element_type x3 -> x0, other arithmetic: 1.89 us -> none  [the longest x1 1.69 us: per_device(): rows = (rows.astype(F32) * coef_all[:, None]).astype(BF)]
    all_to_all x3, starting transfers between devices: 22.3 us -> 20.5 us  [chips_a2a(): return lax.all_to_all(v, CHIPS, split_axis=0, concat_axis=0, tiled=True)]
    pallas_call x1, Pallas kernels: 9 us -> 7.55 us  [per_device(): call(loss_kernel, (jax.ShapeDtypeStruct((1, 1024), F32), jax.ShapeDtypeSt...]
    unnamed x32 -> x40, local copies, waits for them, and re-layouts: 7.47 us -> 7.4 us
  transfers between devices with their start and end apart: 10 -> 10, of which waited for: 5 -> 6; matrix products, arithmetic and copies ran while one was open for 8% -> 6% of each run, Pallas kernels for 21% -> 29%
where the time goes in v3:
time: 129 us; the launch traced here: 128 us
  Pallas kernels  46.7 us (36%)
  starting transfers between devices  39 us (30%)
  waiting for transfers between devices  20.3 us (16%)
  local copies, waits for them, and re-layouts  14.3 us (11%)
  other arithmetic  6.31 us (5%)
  between operations  1.62 us (1%)
    all_to_all x3, starting transfers between devices, chips_a2a(): return lax.all_to_all(v, CHIPS, split_axis=0, concat_axis=0, tiled=True)  20.5 us
    all_to_all x3, waiting for transfers between devices, chips_a2a(): return lax.all_to_all(v, CHIPS, split_axis=0, concat_axis=0, tiled=True)  16 us
    pallas_call x1, Pallas kernels, per_device(): pl.pallas_call(layer_kernel, out_shape=(jax.ShapeDtypeStruct((1, 1024), F...  15.9 us
    ppermute x6, starting transfers between devices, swap(): return lax.ppermute(v, 'c', SWAP)  10.1 us
    pallas_call x1, Pallas kernels, per_device(): pl.pallas_call(place_kernel, grid=(ITEMS_DEV // TILE,), out_shape=jax.Sha...  8.86 us
    all_to_all x1, starting transfers between devices, per_device(): lax.all_to_all(jnp.broadcast_to(w_mine[None], (16,) + w_mine.shape), ('x'...  8.43 us
    pallas_call x1, Pallas kernels, per_device(): call(loss_kernel, (jax.ShapeDtypeStruct((1, 1024), F32), jax.ShapeDtypeSt...  7.55 us
    unnamed x40, local copies, waits for them, and re-layouts  7.4 us
  transfers between devices with their start and end apart: 10, of which 6 were waited for; matrix products, arithmetic and copies ran while one was open for 6% of the time, Pallas kernels for 29%

profile of v3, /device:TPU:1, one launch (start us, length us, event | category | flops | bytes accessed | tf_op | source)
XLA Modules:
  0.0 128.3 jit_solution(16812137026573724398)
XLA Ops:
  0.7 0.9 pad_maximum_fusion.3
  1.6 1.2 broadcast_in_dim.56
  2.8 8.4 %all-to-all-start = ((bf16[16,16,2560]{2,1,0:T(8,128)(2,1)}), bf16[16,16,2560]{2,1,0:T(8,128)(2,1)S(1)}, u32[]{:S(2)}, u32[]{:S(2)}) async-start(bf16[16,16,2560]{2,1,0:T(8,128)(2,1)} %broadcast_in_dim.56), calls=%async_computation | async-start | bytes 2621440 | tf_op jit(solution)/shard_map/all_to_all | solution.py:354
  12.0 5.1 %shard_map.95 = (bf16[1024,512]{1,0:T(8,128)(2,1)S(1)}, s32[1536,128]{1,0:T(8,128)S(1)}, f32[1536,128]{1,0:T(8,128)S(1)}, s32[3,1024]{1,0:T(4,128)S(1)}, f32[2,6...) custom-call(s32[3]{0:T(128)S(1)} %pad_add_fusion.2.info_ref, bf16[1024,512]{1,0:T(8,128)(2,1)S(1)} %bitcast.22, ...), custom_call_target="tpu_custom_call" | custom-call | tf_op jit(solution)/shard_map/pallas_call | solution.py:358
  17.2 1.0 copy-done.2
  18.1 0.9 copy-done.3
  19.0 1.0 copy-done.5
  20.7 3.4 %gather_fusion = bf16[32,512]{1,0:T(8,128)(2,1)S(1)} fusion(bf16[4096,512]{1,0:T(8,128)(2,1)} %param.13, s32[1024]{0:T(1024)S(1)} %pad_clamp_fusion), kind=kCustom, calls=%fused_computation | custom fusion | bytes 65664 | tf_op jit(solution)/shard_map/gather | solution.py:374
  24.3 1.0 collective-permute-start
  25.5 1.1 concatenate.75.follow_hbm
  26.6 1.0 shard_map.96
  27.7 1.6 %all-to-all-done = bf16[16,16,2560]{2,1,0:T(8,128)(2,1)S(1)} async-done(((bf16[16,16,2560]{2,1,0:T(8,128)(2,1)}), bf16[16,16,2560]{2,1,0:T(8,128)(2,1)S(1)}, u32[]{:S(2)}, u32[]{:S(2)}) %all-to-all-start) | async-done | bytes 1310752 | tf_op jit(solution)/shard_map/all_to_all | solution.py:354
  29.3 3.7 %collective-permute-start.1 = (bf16[256,2560]{1,0:T(8,128)(2,1)S(1)}, bf16[256,2560]{1,0:T(8,128)(2,1)}, u32[]{:S(2)}, u32[]{:S(2)}) collective-permute-start(bf16[256,2560]{1,0:T(8,128)(2,1)S(1)} %bitcast.26), channel_id=1, source_target_pairs={{0,1},{1,0},{2,3},{3,2},{4,5},{5,4},{6,7},{7,6},{8,9},{9,8},{10,11... | collective-permute-start | bytes 3932168 | tf_op jit(solution)/shard_map/ppermute | solution.py:339
  33.0 6.9 %all-to-all-start.1 = ((bf16[64,56,128]{2,1,0:T(8,128)(2,1)}), bf16[64,56,128]{2,1,0:T(8,128)(2,1)S(1)}, u32[]{:S(2)}, u32[]{:S(2)}) async-start(bf16[64,56,128]{2,1,0:T(8,128)(2,1)} %shard_map.96), calls=%async_computation.1 | async-start | bytes 1835008 | tf_op jit(solution)/shard_map/all_to_all | solution.py:343
  39.9 15.9 %shard_map.97 = (f32[1,1024]{1,0:T(1,128)}, bf16[1024,512]{1,0:T(8,128)(2,1)}, bf16[1536,512]{1,0:T(8,128)(2,1)}) custom-call(s32[3]{0:T(128)} %copy-done.13, s32[3,1024]{1,0:T(4,128)} %copy-done.7, bf16[256,2560]{1,0:T(8,128)(2,1)} %bitcast.27, bf16[1024,512]{1,0:T(8,128)(2,1)} %copy-done.2, bf16[256,2560]{1,0:T(8,128)(2,1)} %collective-permute-done.1.other_hbm, ...), custom_call_target="tpu_custom_call" | custom-call | tf_op jit(solution)/shard_map/pallas_call | solution.py:386
  56.3 1.7 %collective-permute-start.2 = (bf16[64,56,128]{2,1,0:T(8,128)(2,1)S(1)}, bf16[64,56,128]{2,1,0:T(8,128)(2,1)S(1)}, u32[]{:S(2)}, u32[]{:S(2)}) collective-permute-start(bf16[64,56,128]{2,1,0:T(8,128)(2,1)S(1)} %all-to-all-done.1.own_ref), channel_id=1, source_target_pairs={{0,1},{1,0},{2,3},{3,2},{4,5},{5,4},{6,7},{7,6},{8,9},{9,8},{10,11... | collective-permute-start | bytes 2752520 | tf_op jit(solution)/shard_map/ppermute | solution.py:339
  58.1 8.4 %all-to-all-start.2 = ((bf16[64,24,512]{2,1,0:T(8,128)(2,1)}), bf16[64,24,512]{2,1,0:T(8,128)(2,1)}, u32[]{:S(2)}, u32[]{:S(2)}) async-start(bf16[64,24,512]{2,1,0:T(8,128)(2,1)} %bitcast.29), calls=%async_computation.2 | async-start | bytes 3145728 | tf_op jit(solution)/shard_map/all_to_all | solution.py:343
  67.9 0.7 copy-done.8
  68.6 0.7 copy-done.12
  70.6 7.5 %shard_map.99 = (f32[1,1024]{1,0:T(1,128)}, f32[1536,256]{1,0:T(8,128)S(1)}, bf16[1536,256]{1,0:T(8,128)(2,1)S(1)}, f32[3,64,128]{2,1,0:T(8,128)S(1)}) custom-call(s32[3]{0:T(128)S(1)} %copy-done.14, bf16[1024,512]{1,0:T(8,128)(2,1)S(1)} %copy-done.1, bf16[1536,256]{1,0:T(8,128)(2,1)S(1)} %get-tuple-element.46.own_ref, ...), custom_call_target="tpu_custom_call" | custom-call | tf_op jit(solution)/shard_map/pallas_call | solution.py:428
  78.5 2.0 %collective-permute-done.3.other_ref = bf16[1536,256]{1,0:T(8,128)(2,1)S(1)} collective-permute-done((bf16[1536,256]{1,0:T(8,128)(2,1)S(1)}, bf16[1536,256]{1,0:T(8,128)(2,1)S(1)}, u32[]{:S(2)}, u32[]{:S(2)}) %collective-permute-start.3) | collective-permute-done | bytes 786464 | tf_op jit(solution)/shard_map/ppermute | solution.py:339
  80.5 1.1 shard_map.100
  81.6 8.2 %all-to-all-done.2 = bf16[64,24,512]{2,1,0:T(8,128)(2,1)} async-done(((bf16[64,24,512]{2,1,0:T(8,128)(2,1)}), bf16[64,24,512]{2,1,0:T(8,128)(2,1)}, u32[]{:S(2)}, u32[]{:S(2)}) %all-to-all-start.2) | async-done | bytes 1572896 | tf_op jit(solution)/shard_map/all_to_all | solution.py:343
  89.8 1.5 %broadcast_select_fusion.1 = (bf16[64,8,512]{2,1,0:T(8,128)(2,1)S(1)}, bf16[64,8,512]{2,1,0:T(8,128)(2,1)S(1)}, bf16[64,8,512]{2,1,0:T(8,128)(2,1)S(1)}) fusion(pred[]{:T(512)S(6)} %eq.2, bf16[64,24,512]{2,1,0:T(8,128)(2,1)} %all-to-all-done.2), kind=kLoop, calls=%fused_computation.7 | loop fusion | flops 524288 | bytes 3145729 | tf_op jit(solution)/shard_map/jit(_where)/select_n | solution.py:456
  91.3 1.3 pad_maximum_fusion.2
  92.6 1.7 %collective-permute-start.4 = (bf16[64,16,512]{2,1,0:T(8,128)(2,1)}, bf16[64,16,512]{2,1,0:T(8,128)(2,1)}, u32[]{:S(2)}, u32[]{:S(2)}) collective-permute-start(bf16[64,16,512]{2,1,0:T(8,128)(2,1)} %get-tuple-element.72), channel_id=1, source_target_pairs={{0,1},{1,0},{2,3},{3,2},{4,5},{5,4},{6,7},{7,6},{8,9},{9,8},{10,11... | collective-permute-start | bytes 3145736 | tf_op jit(solution)/shard_map/ppermute | solution.py:339
  94.3 5.1 %all-to-all-start.3 = ((bf16[64,56,128]{2,1,0:T(8,128)(2,1)}), bf16[64,56,128]{2,1,0:T(8,128)(2,1)S(1)}, u32[]{:S(2)}, u32[]{:S(2)}) async-start(bf16[64,56,128]{2,1,0:T(8,128)(2,1)} %shard_map.100), calls=%async_computation.3 | async-start | bytes 1835008 | tf_op jit(solution)/shard_map/all_to_all | solution.py:343
  100.1 1.4 %pad_maximum_fusion.rows_ref = bf16[2048,512]{1,0:T(8,128)(2,1)S(1)} fusion(bf16[1024,512]{1,0:T(8,128)(2,1)} %bitcast.11, bf16[1024,512]{1,0:T(8,128)(2,1)S(1)} %bitcast.28), kind=kLoop, calls=%fused_computation.1 | loop fusion | flops 4194304 | bytes 4194304 | tf_op jit(solution)/shard_map/concatenate | solution.py:462
  101.8 6.9 %shard_map.101 = (bf16[2048,512]{1,0:T(8,128)(2,1)S(1)}, s32[1,2048]{1,0:T(1,128)S(1)}, s32[16,128]{1,0:T(8,128)S(1)}, s32[32]{0:T(128)S(1)}) custom-call(s32[1,2048]{1,0:T(1,128)S(1)} %fusion.2.key_ref, s32[2048,128]{1,0:T(8,128)S(1)} %broadcast_in_dim.62.key_col_ref, bf16[2048,512]{1,0:T(8,128)(2,1)S(1)} %pad_maximum_fusion.rows_ref), custom_call_target="tpu_custom_call" | custom-call | tf_op jit(solution)/shard_map/pallas_call | solution.py:469
  108.8 7.3 %all-to-all-done.3 = bf16[64,56,128]{2,1,0:T(8,128)(2,1)S(1)} async-done(((bf16[64,56,128]{2,1,0:T(8,128)(2,1)}), bf16[64,56,128]{2,1,0:T(8,128)(2,1)S(1)}, u32[]{:S(2)}, u32[]{:S(2)}) %all-to-all-start.3) | async-done | bytes 917536 | tf_op jit(solution)/shard_map/all_to_all | solution.py:343
  116.6 1.8 %collective-permute-start.5 = (f32[28,256]{1,0:T(8,128)S(1)}, f32[28,256]{1,0:T(8,128)S(1)}, u32[]{:S(2)}, u32[]{:S(2)}) collective-permute-start(f32[28,256]{1,0:T(8,128)S(1)} %pad_maximum_fusion.6), channel_id=1, source_target_pairs={{0,1},{1,0},{2,3},{3,2},{4,5},{5,4},{6,7},{7,6},{8,9},{9,8},{10,11... | collective-permute-start | bytes 86024 | tf_op jit(solution)/shard_map/ppermute | solution.py:339
  119.4 8.9 %shard_map.102 = bf16[4096,512]{1,0:T(8,128)(2,1)} custom-call(s32[32]{0:T(128)S(1)} %get-tuple-element.63.start_ref, f32[1,2048]{1,0:T(1,128)S(1)} %bitcast.23, s32[1,2048]{1,0:T(1,128)S(1)} %get-tuple-element.65.at_ref, s32[16,128]{1,0:T(8,128)S(1)} %get-tuple-element.66.key_ref, bf16[2048,512]{1,0:T(8,128)(2,1)S(1)} %get-tuple-element.67.rows_ref, ...), custom_call_target="tpu_custom_call" | custom-call | tf_op jit(solution)/shard_map/pallas_call | solution.py:504
  (79 shorter events, 7.3 us)
Async XLA Ops:
  0.6 11.4 %copy-start.11 = (s32[1,1024]{1,0:T(1,128)S(1)}, s32[1,1024]{1,0:T(1,128)}, u32[]{:S(2)}) copy-start(s32[1,1024]{1,0:T(1,128)} %targets_ref.3) | copy-start | bytes 12292
  0.6 11.3 %copy-start = (bf16[1,1024,512]{2,1,0:T(8,128)(2,1)S(1)}, bf16[1,1024,512]{2,1,0:T(8,128)(2,1)}, u32[]{:S(2)}) copy-start(bf16[1,1024,512]{2,1,0:T(8,128)(2,1)} %param.8) | copy-start | bytes 3145732
  0.7 11.3 %copy-start.16 = (s32[1024]{0:T(1024)S(1)}, s32[1024]{0:T(1024)}, u32[]{:S(2)}) copy-start(s32[1024]{0:T(1024)} %param.12) | copy-start | bytes 12292
  0.7 11.3 %copy-start.15 = (s32[1024]{0:T(1024)S(1)}, s32[1024]{0:T(1024)}, u32[]{:S(2)}) copy-start(s32[1024]{0:T(1024)} %param.11) | copy-start | bytes 12292
  2.8 26.5 %all-to-all-start = ((bf16[16,16,2560]{2,1,0:T(8,128)(2,1)}), bf16[16,16,2560]{2,1,0:T(8,128)(2,1)S(1)}, u32[]{:S(2)}, u32[]{:S(2)}) async-start(bf16[16,16,2560]{2,1,0:T(8,128)(2,1)} %broadcast_in_dim.56), calls=%async_computation | async-start | bytes 2621440 | tf_op jit(solution)/shard_map/all_to_all | solution.py:354
  12.0 14.7 %copy-start.13 = (s32[3]{0:T(128)}, s32[3]{0:T(128)S(1)}, u32[]{:S(2)}) copy-start(s32[3]{0:T(128)S(1)} %pad_add_fusion.2.info_ref) | copy-start | bytes 40
  17.1 1.0 copy-start.2
  18.1 0.9 copy-start.3
  19.0 1.0 copy-start.5
  20.0 0.6 copy-start.7
  24.3 2.4 %collective-permute-start = (bf16[32,256]{1,0:T(8,128)(2,1)S(1)}, bf16[32,256]{1,0:T(8,128)(2,1)S(1)}, u32[]{:S(2)}, u32[]{:S(2)}) collective-permute-start(bf16[32,256]{1,0:T(8,128)(2,1)S(1)} %get-tuple-element.84), channel_id=1, source_target_pairs={{0,1},{1,0},{2,3},{3,2},{4,5},{5,4},{6,7},{7,6},{8,9},{9,8},{10,11... | collective-permute-start | bytes 49160 | tf_op jit(solution)/shard_map/ppermute | solution.py:339
  29.3 10.6 %copy-start.18 = (bf16[16,16,2560]{2,1,0:T(8,128)(2,1)}, bf16[16,16,2560]{2,1,0:T(8,128)(2,1)S(1)}, u32[]{:S(2)}) copy-start(bf16[16,16,2560]{2,1,0:T(8,128)(2,1)S(1)} %all-to-all-done) | copy-start | bytes 3932164
  29.3 10.6 %collective-permute-start.1 = (bf16[256,2560]{1,0:T(8,128)(2,1)S(1)}, bf16[256,2560]{1,0:T(8,128)(2,1)}, u32[]{:S(2)}, u32[]{:S(2)}) collective-permute-start(bf16[256,2560]{1,0:T(8,128)(2,1)S(1)} %bitcast.26), channel_id=1, source_target_pairs={{0,1},{1,0},{2,3},{3,2},{4,5},{5,4},{6,7},{7,6},{8,9},{9,8},{10,11... | collective-permute-start | bytes 3932168 | tf_op jit(solution)/shard_map/ppermute | solution.py:339
  33.0 23.4 %all-to-all-start.1 = ((bf16[64,56,128]{2,1,0:T(8,128)(2,1)}), bf16[64,56,128]{2,1,0:T(8,128)(2,1)S(1)}, u32[]{:S(2)}, u32[]{:S(2)}) async-start(bf16[64,56,128]{2,1,0:T(8,128)(2,1)} %shard_map.96), calls=%async_computation.1 | async-start | bytes 1835008 | tf_op jit(solution)/shard_map/all_to_all | solution.py:343
  56.3 10.2 %collective-permute-start.2 = (bf16[64,56,128]{2,1,0:T(8,128)(2,1)S(1)}, bf16[64,56,128]{2,1,0:T(8,128)(2,1)S(1)}, u32[]{:S(2)}, u32[]{:S(2)}) collective-permute-start(bf16[64,56,128]{2,1,0:T(8,128)(2,1)S(1)} %all-to-all-done.1.own_ref), channel_id=1, source_target_pairs={{0,1},{1,0},{2,3},{3,2},{4,5},{5,4},{6,7},{7,6},{8,9},{9,8},{10,11... | collective-permute-start | bytes 2752520 | tf_op jit(solution)/shard_map/ppermute | solution.py:339
  58.0 9.3 %copy-start.1 = (bf16[1024,512]{1,0:T(8,128)(2,1)S(1)}, bf16[1024,512]{1,0:T(8,128)(2,1)}, u32[]{:S(2)}) copy-start(bf16[1024,512]{1,0:T(8,128)(2,1)} %get-tuple-element.42.hidden_ref) | copy-start | bytes 3145732
  58.1 31.8 %all-to-all-start.2 = ((bf16[64,24,512]{2,1,0:T(8,128)(2,1)}), bf16[64,24,512]{2,1,0:T(8,128)(2,1)}, u32[]{:S(2)}, u32[]{:S(2)}) async-start(bf16[64,24,512]{2,1,0:T(8,128)(2,1)} %bitcast.29), calls=%async_computation.2 | async-start | bytes 3145728 | tf_op jit(solution)/shard_map/all_to_all | solution.py:343
  66.5 1.2 copy-start.4
  66.5 1.4 %copy-start.6 = (f32[1536,128]{1,0:T(8,128)S(1)}, f32[1536,128]{1,0:T(8,128)}, u32[]{:S(2)}) copy-start(f32[1536,128]{1,0:T(8,128)} %copy-done.5) | copy-start | bytes 2359300
  66.7 0.6 copy-start.9
  67.9 0.7 copy-start.8
  68.6 0.7 copy-start.12
  69.3 0.7 copy-start.14
  70.0 0.7 copy-start.17
  78.2 2.3 %collective-permute-start.3 = (bf16[1536,256]{1,0:T(8,128)(2,1)S(1)}, bf16[1536,256]{1,0:T(8,128)(2,1)S(1)}, u32[]{:S(2)}, u32[]{:S(2)}) collective-permute-start(bf16[1536,256]{1,0:T(8,128)(2,1)S(1)} %get-tuple-element.54), channel_id=1, source_target_pairs={{0,1},{1,0},{2,3},{3,2},{4,5},{5,4},{6,7},{7,6},{8,9},{9,8},{10,11... | collective-permute-start | bytes 2359304 | tf_op jit(solution)/shard_map/ppermute | solution.py:339
  91.3 3.0 %copy-start.10 = (s32[2,64,128]{2,1,0:T(8,128)S(1)}, s32[2,64,128]{2,1,0:T(8,128)}, u32[]{:S(2)}) copy-start(s32[2,64,128]{2,1,0:T(8,128)} %copy-done.9) | copy-start | bytes 196612
  92.6 7.6 %collective-permute-start.4 = (bf16[64,16,512]{2,1,0:T(8,128)(2,1)}, bf16[64,16,512]{2,1,0:T(8,128)(2,1)}, u32[]{:S(2)}, u32[]{:S(2)}) collective-permute-start(bf16[64,16,512]{2,1,0:T(8,128)(2,1)} %get-tuple-element.72), channel_id=1, source_target_pairs={{0,1},{1,0},{2,3},{3,2},{4,5},{5,4},{6,7},{7,6},{8,9},{9,8},{10,11... | collective-permute-start | bytes 3145736 | tf_op jit(solution)/shard_map/ppermute | solution.py:339
  94.3 21.7 %all-to-all-start.3 = ((bf16[64,56,128]{2,1,0:T(8,128)(2,1)}), bf16[64,56,128]{2,1,0:T(8,128)(2,1)S(1)}, u32[]{:S(2)}, u32[]{:S(2)}) async-start(bf16[64,56,128]{2,1,0:T(8,128)(2,1)} %shard_map.100), calls=%async_computation.3 | async-start | bytes 1835008 | tf_op jit(solution)/shard_map/all_to_all | solution.py:343
  116.6 2.6 %collective-permute-start.5 = (f32[28,256]{1,0:T(8,128)S(1)}, f32[28,256]{1,0:T(8,128)S(1)}, u32[]{:S(2)}, u32[]{:S(2)}) collective-permute-start(f32[28,256]{1,0:T(8,128)S(1)} %pad_maximum_fusion.6), channel_id=1, source_target_pairs={{0,1},{1,0},{2,3},{3,2},{4,5},{5,4},{6,7},{7,6},{8,9},{9,8},{10,11... | collective-permute-start | bytes 86024 | tf_op jit(solution)/shard_map/ppermute | solution.py:339

commit v4 on v3

--- a/solution.py
+++ b/solution.py
@@ -20,6 +20,7 @@
 CSLOTS = 24
 SLOTS = NCHIPS * CSLOTS
 BLOCK = 2 * CSLOTS + 8
+PLACES = 2048
 GROUP = 8
 ITEMS_DEV = 4096
 B = 256
@@ -285,54 +286,110 @@
         term_own_ref[m, :] = dot(probs_ref[m, :], hidden_ref[:, own_cols])
 
 
-def order_kernel(key_ref, key_col_ref, rows_ref, sorted_ref, at_ref, sorted_key_ref, start_ref):
-    n = key_ref.shape[1]
-    key = key_ref[...]
+def rank_kernel(info_ref, row_ref, neg_ref, at_ref, sorted_key_ref, start_ref, neg_at_ref):
+    core = info_ref[0]
+    row = row_ref[...] - 1 - core * ITEMS_DEV
+    row = jnp.where((row >= 0) & (row < ITEMS_DEV), row, 2 * ITEMS_DEV - 1)
+    n = row.shape[1]
+    key = row * 4096 + iota((1, n), 1)
+    eye = iota((128, 128), 1) == iota((128, 128), 0)
     at = jnp.zeros((1, n), F32)
-    for m in range(n // B):
-        col = key_col_ref[m * B : (m + 1) * B, :]
-        col = jnp.concatenate([col] * (n // 128), axis=1)
+    for m in range(n // 128):
+        col = jnp.sum(jnp.where(eye, key[:, m * 128 : (m + 1) * 128], 0), axis=1, keepdims=True)
         at = at + jnp.sum((col < key).astype(F32), axis=0, keepdims=True)
     at = at.astype(I32)
     at_ref[...] = at
-    row = key >> 11
     for i in range(ITEMS_DEV // TILE + 1):
         start_ref[i] = jnp.sum((row < i * TILE).astype(I32))
-    sorted_key_ref[...] = by_place(at >> 7, at & 127, [row >> 6, row & 63], n // 128, (64.0, 1.0)).astype(I32)
-    for m in range(n // B):
+    start_ref[31] = core
+    neg = neg_ref[:, :1]
+    neg = jnp.where(neg < 0, 2 * ITEMS_DEV, neg) * 64 + iota((32, 1), 0)
+    small_eye = iota((32, 32), 1) == iota((32, 32), 0)
+    neg_row = jnp.sum(jnp.where(small_eye, neg, 0), axis=0, keepdims=True)
+    neg_rank = jnp.sum((neg < neg_row).astype(I32), axis=0, keepdims=True)
+    for p in range(16):
+        found = jnp.sum(jnp.where(neg_rank == p, neg_row, 0))
+        neg_at_ref[p] = found & 63
+        neg_at_ref[16 + p] = found >> 6
+    for i in range(ITEMS_DEV // TILE + 1):
+        neg_at_ref[32 + i] = jnp.sum(((neg_row >> 6) < i * TILE).astype(I32))
+    sorted_key_ref[...] = by_place(at >> 7, at & 127, [row >> 6, row & 63], PLACES // 128, (64.0, 1.0)).astype(I32)
+
+
+def sort_kernel(at_ref, own_ref, other_ref, sorted_ref):
+    for m in range(PLACES // B):
         block = slice(m * B, (m + 1) * B)
-        sorted_ref[block, :] = dot(onehot(m * B, B, at), rows_ref[...]).astype(BF)
+        sorted_ref[block, :] = (
+            dot(onehot(m * B, B, at_ref[:, :SLOTS]), own_ref[...])
+            + dot(onehot(m * B, B, at_ref[:, SLOTS:]), other_ref[...])
+        ).astype(BF)
+
+
+def collect_kernel(got_ref, small_ref):
+    total = jnp.zeros((2 * CSLOTS, 128), F32)
+    for g in range(NCHIPS // GROUP):
+        block = got_ref[g * GROUP : (g + 1) * GROUP].astype(F32)
+        total = total + jnp.sum(block[:, : 2 * CSLOTS], axis=0)
+    small_ref[:CSLOTS, :] = jnp.concatenate([total[:CSLOTS], total[CSLOTS:]], axis=1)
+    k = iota((1, SLOTS), 1)
+    chip = ((k.astype(F32) + 0.5) * (1.0 / CSLOTS)).astype(I32)
+    spread = (iota((128, SLOTS), 0) == k - chip * CSLOTS).astype(F32).astype(BF)
+    mine = iota((NCHIPS, SLOTS), 0) == chip
+    row = jnp.zeros((1, SLOTS), F32)
+    for p in range(3):
+        piece = got_ref[:, 2 * CSLOTS + p, :]
+        row = row + jnp.sum(jnp.where(mine, dot(piece, spread), 0.0), axis=0, keepdims=True)
+    for r in range(SLOTS // B):
+        small_ref[CSLOTS + r : CSLOTS + r + 1, :] = row[:, r * B : (r + 1) * B]
+    small_ref[CSLOTS + SLOTS // B :, :] = jnp.zeros((8 - SLOTS // B, B), F32)
 
 
 def place_kernel(
-    start_ref, coef_ref, at_ref, key_ref, rows_ref, neg_index_ref, neg_ref, out_ref, scaled_ref, total_ref
+    start_ref, neg_at_ref, small_ref, small_other_ref, at_ref, key_ref, rows_ref, out_hbm,
+    scaled_ref, neg_ref, total_ref, out_ref, sems,
 ):
-    n = coef_ref.shape[1]
-    i = pl.program_id(0)
-    base = i * TILE
-
-    @pl.when(i == 0)
-    def _():
-        coef = coef_ref[...]
-        top = coef.astype(BF).astype(F32)
-        middle = (coef - top).astype(BF).astype(F32)
-        at = at_ref[...]
-        coef = by_place(at >> 7, at & 127, [top, middle, coef - top - middle], n // 128)
-        eye = iota((128, 128), 1) == iota((128, 128), 0)
-        for m in range(n // 128):
-            block = slice(m * 128, (m + 1) * 128)
-            col = jnp.sum(jnp.where(eye, coef[m : m + 1, :], 0.0), axis=1, keepdims=True)
-            scaled_ref[block, :] = (rows_ref[block, :].astype(F32) * col).astype(BF)
-
-    total_ref[...] = dot(onehot(base, TILE, neg_index_ref[...]), neg_ref[...])
-
-    @pl.loop(start_ref[i] // B, (start_ref[i + 1] + B - 1) // B)
-    def _(j):
+    coef = jnp.concatenate(
+        [ref[CSLOTS + r : CSLOTS + r + 1, :] for ref in (small_ref, small_other_ref) for r in range(SLOTS // B)],
+        axis=1,
+    )
+    top = coef.astype(BF).astype(F32)
+    middle = (coef - top).astype(BF).astype(F32)
+    at = at_ref[...]
+    coef = by_place(at >> 7, at & 127, [top, middle, coef - top - middle], PLACES // 128)
+    eye = iota((128, 128), 1) == iota((128, 128), 0)
+    for m in range(PLACES // 128):
+        block = slice(m * 128, (m + 1) * 128)
+        col = jnp.sum(jnp.where(eye, coef[m : m + 1, :], 0.0), axis=1, keepdims=True)
+        scaled_ref[block, :] = (rows_ref[block, :].astype(F32) * col).astype(BF)
+    own, other = small_ref[:CSLOTS, :], small_other_ref[:CSLOTS, :]
+    first = start_ref[31] == 0
+    neg_ref[...] = jnp.concatenate([jnp.where(first, own, other), jnp.where(first, other, own)], axis=1)
+
+    def part(base, j):
         block = pl.ds(pl.multiple_of(j * B, B), B)
         key = jnp.concatenate([key_ref[pl.ds(2 * j, 1), :], key_ref[pl.ds(2 * j + 1, 1), :]], axis=1)
-        total_ref[...] += dot(onehot(base, TILE, key), scaled_ref[block, :])
-
-    out_ref[...] = total_ref[...].astype(BF)
+        return dot(onehot(base, TILE, key), scaled_ref[block, :])
+
+    copies = []
+    for i in range(ITEMS_DEV // TILE):
+        base = i * TILE
+        tile = slice(base, base + TILE)
+        first = jnp.minimum(start_ref[i] // B, PLACES // B - 1)
+        total_ref[...] = part(base, first)
+
+        @pl.loop(first + 1, (start_ref[i + 1] + B - 1) // B)
+        def _(j):
+            total_ref[...] += part(base, j)
+
+        @pl.loop(neg_at_ref[32 + i], neg_at_ref[33 + i])
+        def _(p):
+            total_ref[pl.ds(neg_at_ref[16 + p] - base, 1), :] += neg_ref[pl.ds(neg_at_ref[p], 1), :]
+
+        out_ref[tile, :] = total_ref[...].astype(BF)
+        copies.append(pltpu.make_async_copy(out_ref.at[tile, :], out_hbm.at[tile, :], sems.at[i]))
+        copies[-1].start()
+    for copy in copies:
+        copy.wait()
 
 
 def swap(v):
@@ -355,7 +412,7 @@
         jnp.broadcast_to(w_mine[None], (16,) + w_mine.shape), ("x", "z"), split_axis=0, concat_axis=0, tiled=True
     ).reshape(256, 2560)
 
-    normed, ids, logc, target_slot, send_row, neg_local = call(
+    normed, ids, logc, target_slot, send_row, neg_table = call(
         prep_kernel,
         (
             jax.ShapeDtypeStruct((1024, width), BF),
@@ -370,7 +427,7 @@
         vmem=16,
     )(info, ev, target_ids, neg_ids[None], neg_counts[None])
 
-    neg_local = neg_local[:, 0]
+    neg_local = neg_table[:, 0]
     packed = jnp.where((neg_local >= 0)[:, None], item_table[jnp.maximum(neg_local, 0)], 0)
     packed_own = lax.dynamic_slice(packed, (0, core * B), (32, B))
     packed_other = lax.dynamic_slice(packed, (0, (1 - core) * B), (32, B))
@@ -423,7 +480,7 @@
         vmem=16,
     )(got_neg, other_neg)
 
-    recv_rows = chips_a2a(send_rows.reshape(NCHIPS, CSLOTS, width))
+    recv_rows = chips_a2a(send_rows.reshape(NCHIPS, CSLOTS, width)).reshape(SLOTS, width)
 
     loss, term_own, term_other, meta = call(
         loss_kernel,
@@ -451,66 +508,43 @@
     recv_rows, block = lax.optimization_barrier((recv_rows, block))
     got = chips_a2a(block)
 
-    def split(v):
-        first, second, last = v[:, :8], v[:, 8:16], v[:, 16:]
-        keep = jnp.where(core == 0, first, second)
-        give = jnp.where(core == 0, second, first)
-        return jnp.concatenate([keep, last], axis=1), jnp.concatenate([give, last], axis=1)
-
-    rows_keep, rows_give = split(recv_rows)
-    rows_got = swap(rows_give)
-    rows = jnp.concatenate([rows_keep.reshape(-1, width), rows_got.reshape(-1, width)], axis=0)
-    first, _ = split(row_table[0, :, :CSLOTS])
-    second, _ = split(row_table[1, :, :CSLOTS])
-    row_at = jnp.concatenate([first.reshape(-1), second.reshape(-1)]) - 1 - core * ITEMS_DEV
-    row_at = jnp.where((row_at >= 0) & (row_at < ITEMS_DEV), row_at, 2 * ITEMS_DEV - 1)
-    count = row_at.shape[0]
-    key = row_at * count + jnp.arange(count, dtype=I32)
-    rows, at, sorted_key, starts = pl.pallas_call(
-        order_kernel,
+    recv_other = swap(recv_rows)
+    at, sorted_key, starts, neg_at = pl.pallas_call(
+        rank_kernel,
         out_shape=(
-            jax.ShapeDtypeStruct((count, width), BF),
-            jax.ShapeDtypeStruct((1, count), I32),
-            jax.ShapeDtypeStruct((count // 128, 128), I32),
+            jax.ShapeDtypeStruct((1, 2 * SLOTS), I32),
+            jax.ShapeDtypeStruct((PLACES // 128, 128), I32),
             jax.ShapeDtypeStruct((32,), I32),
+            jax.ShapeDtypeStruct((48,), I32),
         ),
-        in_specs=[VMEM] * 3,
-        out_specs=(VMEM, VMEM, VMEM, SMEM),
+        in_specs=[SMEM, VMEM, VMEM],
+        out_specs=(VMEM, VMEM, SMEM, SMEM),
+        cost_estimate=pl.CostEstimate(flops=0, bytes_accessed=0, transcendentals=0),
+        compiler_params=pltpu.CompilerParams(vmem_limit_bytes=16 << 20),
+    )(info, row_table[:, :, :CSLOTS].reshape(1, 2 * SLOTS), neg_table)
+    rows = call(sort_kernel, jax.ShapeDtypeStruct((PLACES, width), BF), [VMEM] * 3, vmem=24)(
+        at, recv_rows, recv_other
+    )
+
+    got, rows = lax.optimization_barrier((got, rows))
+    small = call(collect_kernel, jax.ShapeDtypeStruct((32, B), F32), [VMEM], vmem=8)(got)
+    small_other = swap(small)
+    tiles = ITEMS_DEV // TILE
+    grad = pl.pallas_call(
+        place_kernel,
+        out_shape=jax.ShapeDtypeStruct((ITEMS_DEV, width), BF),
+        in_specs=[SMEM] * 2 + [VMEM] * 5,
+        out_specs=pl.BlockSpec(memory_space=pl.ANY),
+        scratch_shapes=[
+            pltpu.VMEM((PLACES, width), BF),
+            pltpu.VMEM((CSLOTS, width), F32),
+            pltpu.VMEM((TILE, width), F32),
+            pltpu.VMEM((ITEMS_DEV, width), BF),
+            pltpu.SemaphoreType.DMA((tiles,)),
+        ],
         cost_estimate=pl.CostEstimate(flops=0, bytes_accessed=0, transcendentals=0),
         compiler_params=pltpu.CompilerParams(vmem_limit_bytes=24 << 20),
-    )(key[None], jnp.broadcast_to(key[:, None], (count, 128)), rows)
-
-    got, rows, at, sorted_key, starts = lax.optimization_barrier((got, rows, at, sorted_key, starts))
-    summed = jnp.sum(got[:, : 2 * CSLOTS].astype(F32), axis=0)
-    summed = jnp.concatenate([summed[:CSLOTS], summed[CSLOTS:]], axis=1)
-    got_coef = jnp.sum(got[:, 2 * CSLOTS : 2 * CSLOTS + 3, :CSLOTS].astype(F32), axis=1)
-    coef_keep, coef_give = split(got_coef)
-    small = swap(jnp.concatenate([summed, coef_give.reshape(4, B)], axis=0))
-    summed_got = small[:CSLOTS]
-    coef_all = jnp.concatenate([coef_keep.reshape(-1), small[CSLOTS:].reshape(-1)])
-
-    neg_sum = jnp.where(
-        core == 0,
-        jnp.concatenate([summed, summed_got], axis=1),
-        jnp.concatenate([summed_got, summed], axis=1),
-    )
-    neg_high = neg_sum.astype(BF)
-    neg_low = (neg_sum - neg_high.astype(F32)).astype(BF)
-    rest = 128 - 2 * CSLOTS
-    neg_rows = jnp.concatenate([neg_high, neg_low, jnp.zeros((rest, width), BF)], axis=0)
-    neg_at = jnp.concatenate([neg_local[:CSLOTS], neg_local[:CSLOTS], jnp.full((rest,), -1, I32)])
-
-    whole = lambda shape: pl.BlockSpec(shape, lambda i: (0, 0))
-    grad = pl.pallas_call(
-        place_kernel,
-        grid=(ITEMS_DEV // TILE,),
-        out_shape=jax.ShapeDtypeStruct((ITEMS_DEV, width), BF),
-        in_specs=[SMEM] + [whole((1, count))] * 2 + [whole((count // 128, 128)), whole((count, width)), whole((1, 128)), whole((128, width))],
-        out_specs=pl.BlockSpec((TILE, width), lambda i: (i, 0)),
-        scratch_shapes=[pltpu.VMEM((count, width), BF), pltpu.VMEM((TILE, width), F32)],
-        cost_estimate=pl.CostEstimate(flops=0, bytes_accessed=0, transcendentals=0),
-        compiler_params=pltpu.CompilerParams(vmem_limit_bytes=24 << 20),
-    )(starts, coef_all[None], at, sorted_key, rows, neg_at[None], neg_rows)
+    )(starts, neg_at, small, small_other, at, sorted_key, rows)
     return loss, grad
 
 

time: 129 us -> 125 us (0.969)
  Pallas kernels: 46.7 us -> 52.4 us
  other arithmetic: 6.31 us -> 1.25 us
  waiting for transfers between devices: 20.3 us -> 15.6 us
    pallas_call x2 -> x4, Pallas kernels: 15.8 us -> 21.4 us  [the longest x1 8.05 us: per_device(): call(sort_kernel, jax.ShapeDtypeStruct((PLACES, width), BF), [VMEM] * 3,...]
    all_to_all x3, waiting for transfers between devices: 16 us -> 10.9 us  [chips_a2a(): return lax.all_to_all(v, CHIPS, split_axis=0, concat_axis=0, tiled=True)]
    concatenate x8 -> x0, other arithmetic: 2.95 us -> none  [the longest x4 1.49 us: split(): jnp.concatenate([keep, last], axis=1)]
    select_n x3 -> x0, other arithmetic: 1.65 us -> none  [split(): keep = jnp.where(core == 0, first, second)]
    unnamed x40 -> x36, local copies, waits for them, and re-layouts: 7.4 us -> 8.27 us
  transfers between devices with their start and end apart: 10 -> 10, of which waited for: 6 -> 5; matrix products, arithmetic and copies ran while one was open for 6% -> 4% of each run, Pallas kernels for 29% -> 36%
where the time goes in v4:
time: 125 us; the launch traced here: 124 us
  Pallas kernels  52.4 us (42%)
  starting transfers between devices  39.3 us (31%)
  waiting for transfers between devices  15.6 us (12%)
  local copies, waits for them, and re-layouts  14.3 us (11%)
  between operations  1.74 us (1%)
  other arithmetic  1.25 us (1%)
    all_to_all x3, starting transfers between devices, chips_a2a(): return lax.all_to_all(v, CHIPS, split_axis=0, concat_axis=0, tiled=True)  21.4 us
    pallas_call x1, Pallas kernels, per_device(): pl.pallas_call(layer_kernel, out_shape=(jax.ShapeDtypeStruct((1, 1024), F...  15.9 us
    all_to_all x3, waiting for transfers between devices, chips_a2a(): return lax.all_to_all(v, CHIPS, split_axis=0, concat_axis=0, tiled=True)  10.9 us
    ppermute x6, starting transfers between devices, swap(): return lax.ppermute(v, 'c', SWAP)  9.3 us
    all_to_all x1, starting transfers between devices, per_device(): lax.all_to_all(jnp.broadcast_to(w_mine[None], (16,) + w_mine.shape), ('x'...  8.62 us
    unnamed x36, local copies, waits for them, and re-layouts  8.27 us
    pallas_call x1, Pallas kernels, per_device(): call(sort_kernel, jax.ShapeDtypeStruct((PLACES, width), BF), [VMEM] * 3,...  8.05 us
    pallas_call x1, Pallas kernels, per_device(): call(loss_kernel, (jax.ShapeDtypeStruct((1, 1024), F32), jax.ShapeDtypeSt...  7.55 us
  transfers between devices with their start and end apart: 10, of which 5 were waited for; matrix products, arithmetic and copies ran while one was open for 4% of the time, Pallas kernels for 36%

profile of v4, /device:TPU:1, one launch (start us, length us, event | category | flops | bytes accessed | tf_op | source)
XLA Modules:
  0.0 124.5 jit_solution(18368513910820711721)
XLA Ops:
  0.6 0.9 pad_maximum_fusion
  1.5 1.2 broadcast_in_dim.31
  2.7 8.6 %all-to-all-start = ((bf16[16,16,2560]{2,1,0:T(8,128)(2,1)}), bf16[16,16,2560]{2,1,0:T(8,128)(2,1)}, u32[]{:S(2)}, u32[]{:S(2)}) async-start(bf16[16,16,2560]{2,1,0:T(8,128)(2,1)} %broadcast_in_dim.31), calls=%async_computation | async-start | bytes 2621440 | tf_op jit(solution)/shard_map/all_to_all | solution.py:411
  12.1 5.1 %shard_map.95 = (bf16[1024,512]{1,0:T(8,128)(2,1)S(1)}, s32[1536,128]{1,0:T(8,128)S(1)}, f32[1536,128]{1,0:T(8,128)S(1)}, s32[3,1024]{1,0:T(4,128)S(1)}, f32[2,6...) custom-call(s32[3]{0:T(128)S(1)} %pad_add_fusion.info_ref, bf16[1024,512]{1,0:T(8,128)(2,1)S(1)} %bitcast.12, ...), custom_call_target="tpu_custom_call" | custom-call | tf_op jit(solution)/shard_map/pallas_call | solution.py:415
  17.2 1.0 copy-done.4
  18.2 1.0 copy-done.5
  19.2 0.9 copy-done.7
  20.8 3.4 %gather_fusion = bf16[32,512]{1,0:T(8,128)(2,1)S(1)} fusion(bf16[4096,512]{1,0:T(8,128)(2,1)} %param.13, s32[1024]{0:T(1024)S(1)} %pad_clamp_fusion), kind=kCustom, calls=%fused_computation | custom fusion | bytes 65664 | tf_op jit(solution)/shard_map/gather | solution.py:431
  24.3 1.0 collective-permute-start
  25.6 1.1 concatenate.7.follow_hbm
  26.7 1.0 shard_map.96
  27.8 1.7 %all-to-all-done = bf16[16,16,2560]{2,1,0:T(8,128)(2,1)} async-done(((bf16[16,16,2560]{2,1,0:T(8,128)(2,1)}), bf16[16,16,2560]{2,1,0:T(8,128)(2,1)}, u32[]{:S(2)}, u32[]{:S(2)}) %all-to-all-start) | async-done | bytes 1310752 | tf_op jit(solution)/shard_map/all_to_all | solution.py:411
  29.5 3.7 %collective-permute-start.1 = (bf16[256,2560]{1,0:T(8,128)(2,1)}, bf16[256,2560]{1,0:T(8,128)(2,1)S(1)}, u32[]{:S(2)}, u32[]{:S(2)}) collective-permute-start(bf16[256,2560]{1,0:T(8,128)(2,1)} %bitcast.5.own_hbm), channel_id=1, source_target_pairs={{0,1},{1,0},{2,3},{3,2},{4,5},{5,4},{6,7},{7,6},{8,9},{9,8},{10,11... | collective-permute-start | bytes 3932168 | tf_op jit(solution)/shard_map/ppermute | solution.py:396
  33.1 6.9 %all-to-all-start.1 = ((bf16[64,56,128]{2,1,0:T(8,128)(2,1)}), bf16[64,56,128]{2,1,0:T(8,128)(2,1)S(1)}, u32[]{:S(2)}, u32[]{:S(2)}) async-start(bf16[64,56,128]{2,1,0:T(8,128)(2,1)} %shard_map.96), calls=%async_computation.1 | async-start | bytes 1835008 | tf_op jit(solution)/shard_map/all_to_all | solution.py:400
  40.1 1.1 copy-done.17
  41.1 15.9 %shard_map.97 = (f32[1,1024]{1,0:T(1,128)}, bf16[1024,512]{1,0:T(8,128)(2,1)}, bf16[1536,512]{1,0:T(8,128)(2,1)}) custom-call(s32[3]{0:T(128)} %copy-done.12, s32[3,1024]{1,0:T(4,128)} %copy-done.9, bf16[256,2560]{1,0:T(8,128)(2,1)} %bitcast.5.own_hbm, bf16[1024,512]{1,0:T(8,128)(2,1)} %copy-done.4, bf16[256,2560]{1,0:T(8,128)(2,1)} %copy-done.17, ...), custom_call_target="tpu_custom_call" | custom-call | tf_op jit(solution)/shard_map/pallas_call | solution.py:443
  57.1 1.1 collective-permute-start.2
  58.2 9.3 %all-to-all-start.2 = ((bf16[64,24,512]{2,1,0:T(8,128)(2,1)}), bf16[64,24,512]{2,1,0:T(8,128)(2,1)S(1)}, u32[]{:S(2)}, u32[]{:S(2)}) async-start(bf16[64,24,512]{2,1,0:T(8,128)(2,1)} %bitcast.18), calls=%async_computation.2 | async-start | bytes 3145728 | tf_op jit(solution)/shard_map/all_to_all | solution.py:400
  67.7 1.0 copy-done.3
  68.9 1.1 copy-done.8
  70.0 7.6 %shard_map.99 = (f32[1,1024]{1,0:T(1,128)}, f32[1536,256]{1,0:T(8,128)S(1)}, bf16[1536,256]{1,0:T(8,128)(2,1)S(1)}, f32[3,64,128]{2,1,0:T(8,128)S(1)}) custom-call(s32[3]{0:T(128)S(1)} %copy-done.13, bf16[1024,512]{1,0:T(8,128)(2,1)S(1)} %copy-done.3, bf16[1536,256]{1,0:T(8,128)(2,1)S(1)} %get-tuple-element.43.own_ref, ...), custom_call_target="tpu_custom_call" | custom-call | tf_op jit(solution)/shard_map/pallas_call | solution.py:485
  77.8 2.1 %collective-permute-done.3.other_ref = bf16[1536,256]{1,0:T(8,128)(2,1)S(1)} collective-permute-done((bf16[1536,256]{1,0:T(8,128)(2,1)S(1)}, bf16[1536,256]{1,0:T(8,128)(2,1)S(1)}, u32[]{:S(2)}, u32[]{:S(2)}) %collective-permute-start.3) | collective-permute-done | bytes 786464 | tf_op jit(solution)/shard_map/ppermute | solution.py:396
  79.9 1.2 shard_map.101
  81.1 10.0 %all-to-all-done.2 = bf16[64,24,512]{2,1,0:T(8,128)(2,1)S(1)} async-done(((bf16[64,24,512]{2,1,0:T(8,128)(2,1)}), bf16[64,24,512]{2,1,0:T(8,128)(2,1)S(1)}, u32[]{:S(2)}, u32[]{:S(2)}) %all-to-all-start.2) | async-done | bytes 1572896 | tf_op jit(solution)/shard_map/all_to_all | solution.py:400
  91.1 1.5 %collective-permute-start.4 = (bf16[1536,512]{1,0:T(8,128)(2,1)S(1)}, bf16[1536,512]{1,0:T(8,128)(2,1)}, u32[]{:S(2)}, u32[]{:S(2)}) collective-permute-start(bf16[1536,512]{1,0:T(8,128)(2,1)S(1)} %bitcast.13), channel_id=1, source_target_pairs={{0,1},{1,0},{2,3},{3,2},{4,5},{5,4},{6,7},{7,6},{8,9},{9,8},{10,11... | collective-permute-start | bytes 4718600 | tf_op jit(solution)/shard_map/ppermute | solution.py:396
  92.6 5.2 %all-to-all-start.3 = ((bf16[64,56,128]{2,1,0:T(8,128)(2,1)}), bf16[64,56,128]{2,1,0:T(8,128)(2,1)S(1)}, u32[]{:S(2)}, u32[]{:S(2)}) async-start(bf16[64,56,128]{2,1,0:T(8,128)(2,1)} %shard_map.101), calls=%async_computation.3 | async-start | bytes 1835008 | tf_op jit(solution)/shard_map/all_to_all | solution.py:400
  97.9 6.1 %shard_map.100 = (s32[1,3072]{1,0:T(1,128)S(1)}, s32[16,128]{1,0:T(8,128)S(1)}, s32[32]{0:T(128)S(1)}, s32[48]{0:T(128)S(1)}) custom-call(s32[3]{0:T(128)S(1)} %copy-done.13, s32[1,3072]{1,0:T(1,128)S(1)} %reshape.19.row_ref, s32[32,128]{1,0:T(8,128)S(1)} %get-tuple-element.34.neg_ref), custom_call_target="tpu_custom_call" | custom-call | tf_op jit(solution)/shard_map/pallas_call | solution.py:512
  104.0 1.4 %copy-done.2 = bf16[64,24,512]{2,1,0:T(8,128)(2,1)S(1)} copy-done((bf16[64,24,512]{2,1,0:T(8,128)(2,1)S(1)}, bf16[64,24,512]{2,1,0:T(8,128)(2,1)}, u32[]{:S(2)}) %copy-start.2) | copy-done | bytes 1572888
  105.4 8.1 %shard_map.102.rows_ref = bf16[2048,512]{1,0:T(8,128)(2,1)S(1)} custom-call(s32[1,3072]{1,0:T(1,128)S(1)} %get-tuple-element.57.at_ref, bf16[1536,512]{1,0:T(8,128)(2,1)S(1)} %bitcast.14, bf16[1536,512]{1,0:T(8,128)(2,1)} %collective-permute-done.4.other_ref), custom_call_target="tpu_custom_call" | custom-call | tf_op jit(solution)/shard_map/pallas_call | solution.py:525
  113.5 0.9 all-to-all-done.3.got_ref
  114.9 1.8 %collective-permute-start.5 = (f32[32,256]{1,0:T(8,128)S(1)}, f32[32,256]{1,0:T(8,128)S(1)}, u32[]{:S(2)}, u32[]{:S(2)}) collective-permute-start(f32[32,256]{1,0:T(8,128)S(1)} %shard_map.103.small_ref), channel_id=1, source_target_pairs={{0,1},{1,0},{2,3},{3,2},{4,5},{5,4},{6,7},{7,6},{8,9},{9,8},{10,11... | collective-permute-start | bytes 98312 | tf_op jit(solution)/shard_map/ppermute | solution.py:396
  117.6 6.7 %shard_map.104 = bf16[4096,512]{1,0:T(8,128)(2,1)} custom-call(s32[32]{0:T(128)S(1)} %get-tuple-element.50.start_ref, s32[48]{0:T(128)S(1)} %get-tuple-element.51.neg_at_ref, f32[32,256]{1,0:T(8,128)S(1)} %shard_map.103.small_ref, f32[32,256]{1,0:T(8,128)S(1)} %collective-permute-done.5.small_other_ref, s32[1,3072]{1,0:T(1,128)S(1)} %get-tuple-element.57.at_ref, ...), custom_call_target="tpu_custom_call" | custom-call | tf_op jit(solution)/shard_map/pallas_call | solution.py:533
  (46 shorter events, 3.4 us)
Async XLA Ops:
  2.7 9.4 %copy-start = (bf16[1,1024,512]{2,1,0:T(8,128)(2,1)S(1)}, bf16[1,1024,512]{2,1,0:T(8,128)(2,1)}, u32[]{:S(2)}) copy-start(bf16[1,1024,512]{2,1,0:T(8,128)(2,1)} %param.8) | copy-start | bytes 3145732
  2.7 9.4 %copy-start.11 = (s32[1,1024]{1,0:T(1,128)S(1)}, s32[1,1024]{1,0:T(1,128)}, u32[]{:S(2)}) copy-start(s32[1,1024]{1,0:T(1,128)} %targets_ref.3) | copy-start | bytes 12292
  2.7 9.4 %copy-start.14 = (s32[1024]{0:T(1024)S(1)}, s32[1024]{0:T(1024)}, u32[]{:S(2)}) copy-start(s32[1024]{0:T(1024)} %param.11) | copy-start | bytes 12292
  2.7 9.4 %copy-start.15 = (s32[1024]{0:T(1024)S(1)}, s32[1024]{0:T(1024)}, u32[]{:S(2)}) copy-start(s32[1024]{0:T(1024)} %param.12) | copy-start | bytes 12292
  2.7 26.8 %all-to-all-start = ((bf16[16,16,2560]{2,1,0:T(8,128)(2,1)}), bf16[16,16,2560]{2,1,0:T(8,128)(2,1)}, u32[]{:S(2)}, u32[]{:S(2)}) async-start(bf16[16,16,2560]{2,1,0:T(8,128)(2,1)} %broadcast_in_dim.31), calls=%async_computation | async-start | bytes 2621440 | tf_op jit(solution)/shard_map/all_to_all | solution.py:411
  12.0 13.6 %copy-start.12 = (s32[3]{0:T(128)}, s32[3]{0:T(128)S(1)}, u32[]{:S(2)}) copy-start(s32[3]{0:T(128)S(1)} %pad_add_fusion.info_ref) | copy-start | bytes 40
  17.2 1.0 copy-start.4
  18.2 1.0 copy-start.5
  19.2 0.9 copy-start.7
  20.0 0.6 copy-start.9
  24.3 2.4 %collective-permute-start = (bf16[32,256]{1,0:T(8,128)(2,1)S(1)}, bf16[32,256]{1,0:T(8,128)(2,1)S(1)}, u32[]{:S(2)}, u32[]{:S(2)}) collective-permute-start(bf16[32,256]{1,0:T(8,128)(2,1)S(1)} %get-tuple-element.62), channel_id=1, source_target_pairs={{0,1},{1,0},{2,3},{3,2},{4,5},{5,4},{6,7},{7,6},{8,9},{9,8},{10,11... | collective-permute-start | bytes 49160 | tf_op jit(solution)/shard_map/ppermute | solution.py:396
  29.5 10.6 %collective-permute-start.1 = (bf16[256,2560]{1,0:T(8,128)(2,1)}, bf16[256,2560]{1,0:T(8,128)(2,1)S(1)}, u32[]{:S(2)}, u32[]{:S(2)}) collective-permute-start(bf16[256,2560]{1,0:T(8,128)(2,1)} %bitcast.5.own_hbm), channel_id=1, source_target_pairs={{0,1},{1,0},{2,3},{3,2},{4,5},{5,4},{6,7},{7,6},{8,9},{9,8},{10,11... | collective-permute-start | bytes 3932168 | tf_op jit(solution)/shard_map/ppermute | solution.py:396
  33.1 23.9 %all-to-all-start.1 = ((bf16[64,56,128]{2,1,0:T(8,128)(2,1)}), bf16[64,56,128]{2,1,0:T(8,128)(2,1)S(1)}, u32[]{:S(2)}, u32[]{:S(2)}) async-start(bf16[64,56,128]{2,1,0:T(8,128)(2,1)} %shard_map.96), calls=%async_computation.1 | async-start | bytes 1835008 | tf_op jit(solution)/shard_map/all_to_all | solution.py:400
  40.1 1.1 copy-start.17
  57.1 10.4 %collective-permute-start.2 = (bf16[64,56,128]{2,1,0:T(8,128)(2,1)S(1)}, bf16[64,56,128]{2,1,0:T(8,128)(2,1)S(1)}, u32[]{:S(2)}, u32[]{:S(2)}) collective-permute-start(bf16[64,56,128]{2,1,0:T(8,128)(2,1)S(1)} %all-to-all-done.1.own_ref), channel_id=1, source_target_pairs={{0,1},{1,0},{2,3},{3,2},{4,5},{5,4},{6,7},{7,6},{8,9},{9,8},{10,11... | collective-permute-start | bytes 2752520 | tf_op jit(solution)/shard_map/ppermute | solution.py:396
  58.2 9.5 %copy-start.10 = (s32[3,1024]{1,0:T(4,128)S(1)}, s32[3,1024]{1,0:T(4,128)}, u32[]{:S(2)}) copy-start(s32[3,1024]{1,0:T(4,128)} %copy-done.9) | copy-start | bytes 36868
  58.2 32.9 %all-to-all-start.2 = ((bf16[64,24,512]{2,1,0:T(8,128)(2,1)}), bf16[64,24,512]{2,1,0:T(8,128)(2,1)S(1)}, u32[]{:S(2)}, u32[]{:S(2)}) async-start(bf16[64,24,512]{2,1,0:T(8,128)(2,1)} %bitcast.18), calls=%async_computation.2 | async-start | bytes 3145728 | tf_op jit(solution)/shard_map/all_to_all | solution.py:400
  67.4 1.2 copy-start.3
  67.5 1.4 %copy-start.6 = (s32[1536,128]{1,0:T(8,128)S(1)}, s32[1536,128]{1,0:T(8,128)}, u32[]{:S(2)}) copy-start(s32[1536,128]{1,0:T(8,128)} %copy-done.5) | copy-start | bytes 2359300
  67.5 1.4 %copy-start.13 = (s32[3]{0:T(128)S(1)}, s32[3]{0:T(128)}, u32[]{:S(2)}) copy-start(s32[3]{0:T(128)} %copy-done.12) | copy-start | bytes 40
  67.5 1.4 %copy-start.16 = (f32[1,1024]{1,0:T(1,128)S(1)}, f32[1,1024]{1,0:T(1,128)}, u32[]{:S(2)}) copy-start(f32[1,1024]{1,0:T(1,128)} %get-tuple-element.47.positive_ref) | copy-start | bytes 12292
  68.9 1.1 copy-start.8
  77.6 2.3 %collective-permute-start.3 = (bf16[1536,256]{1,0:T(8,128)(2,1)S(1)}, bf16[1536,256]{1,0:T(8,128)(2,1)S(1)}, u32[]{:S(2)}, u32[]{:S(2)}) collective-permute-start(bf16[1536,256]{1,0:T(8,128)(2,1)S(1)} %get-tuple-element.54), channel_id=1, source_target_pairs={{0,1},{1,0},{2,3},{3,2},{4,5},{5,4},{6,7},{7,6},{8,9},{9,8},{10,11... | collective-permute-start | bytes 2359304 | tf_op jit(solution)/shard_map/ppermute | solution.py:396
  91.1 13.0 %copy-start.1 = (bf16[64,24,512]{2,1,0:T(8,128)(2,1)}, bf16[64,24,512]{2,1,0:T(8,128)(2,1)S(1)}, u32[]{:S(2)}) copy-start(bf16[64,24,512]{2,1,0:T(8,128)(2,1)S(1)} %all-to-all-done.2) | copy-start | bytes 4718596
  91.1 12.9 %collective-permute-start.4 = (bf16[1536,512]{1,0:T(8,128)(2,1)S(1)}, bf16[1536,512]{1,0:T(8,128)(2,1)}, u32[]{:S(2)}, u32[]{:S(2)}) collective-permute-start(bf16[1536,512]{1,0:T(8,128)(2,1)S(1)} %bitcast.13), channel_id=1, source_target_pairs={{0,1},{1,0},{2,3},{3,2},{4,5},{5,4},{6,7},{7,6},{8,9},{9,8},{10,11... | collective-permute-start | bytes 4718600 | tf_op jit(solution)/shard_map/ppermute | solution.py:396
  92.6 21.8 %all-to-all-start.3 = ((bf16[64,56,128]{2,1,0:T(8,128)(2,1)}), bf16[64,56,128]{2,1,0:T(8,128)(2,1)S(1)}, u32[]{:S(2)}, u32[]{:S(2)}) async-start(bf16[64,56,128]{2,1,0:T(8,128)(2,1)} %shard_map.101), calls=%async_computation.3 | async-start | bytes 1835008 | tf_op jit(solution)/shard_map/all_to_all | solution.py:400
  104.0 1.4 %copy-start.2 = (bf16[64,24,512]{2,1,0:T(8,128)(2,1)S(1)}, bf16[64,24,512]{2,1,0:T(8,128)(2,1)}, u32[]{:S(2)}) copy-start(bf16[64,24,512]{2,1,0:T(8,128)(2,1)} %copy-done.1) | copy-start | bytes 4718596
  114.9 2.6 %collective-permute-start.5 = (f32[32,256]{1,0:T(8,128)S(1)}, f32[32,256]{1,0:T(8,128)S(1)}, u32[]{:S(2)}, u32[]{:S(2)}) collective-permute-start(f32[32,256]{1,0:T(8,128)S(1)} %shard_map.103.small_ref), channel_id=1, source_target_pairs={{0,1},{1,0},{2,3},{3,2},{4,5},{5,4},{6,7},{7,6},{8,9},{9,8},{10,11... | collective-permute-start | bytes 98312 | tf_op jit(solution)/shard_map/ppermute | solution.py:396

commit v5 on v4

--- a/solution.py
+++ b/solution.py
@@ -172,71 +172,84 @@
 def layer_kernel(
     info_ref, slot_ref, own_hbm, normed_hbm, other_hbm, events_hbm, follow_hbm,
     positive_ref, hidden_hbm, send_hbm,
-    w_ref, own_ref, other_ref, normed_ref, events_ref, follow_ref, act_ref, att_ref, hidden_ref, send_ref, in_sem, out_sem,
+    w_ref, all_ref, normed_ref, events_ref, follow_ref, act_ref, att_ref, hidden_ref, send_ref, in_sem, out_sem,
 ):
     core, length = info_ref[0], info_ref[1]
-    pairs = (
-        (normed_hbm, normed_ref), (own_hbm, own_ref), (other_hbm, other_ref),
-        (events_hbm, events_ref), (follow_hbm, follow_ref),
-    )
-    inputs = [pltpu.make_async_copy(source, to, in_sem.at[k]) for k, (source, to) in enumerate(pairs)]
-    for copy in inputs:
+    blocks = [slice(i * B, (i + 1) * B) for i in range(4)]
+
+    def fetch(k, source, to):
+        return [pltpu.make_async_copy(source.at[r, :], to.at[r, :], in_sem.at[k, i]) for i, r in enumerate(blocks)]
+
+    w_in = [
+        pltpu.make_async_copy(source, all_ref.at[pl.ds(k * B, B), :], in_sem.at[3, k])
+        for k, source in enumerate((own_hbm, other_hbm))
+    ]
+    normed_in = fetch(0, normed_hbm, normed_ref)
+    events_in = fetch(1, events_hbm, events_ref)
+    follow_in = fetch(2, follow_hbm, follow_ref)
+    for copy in normed_in[:1] + w_in + normed_in[1:] + [c for p in zip(events_in, follow_in) for c in p]:
         copy.start()
-    for copy in inputs[:3]:
+    for copy in w_in:
         copy.wait()
 
     @pl.loop(0, 4)
     def _(i):
         rows = pl.ds(pl.multiple_of(i * B, B), B)
-        a = normed_ref[rows, :B]
-        b = normed_ref[rows, B:]
+        pltpu.make_async_copy(normed_hbm.at[rows, :], normed_ref.at[rows, :], in_sem.at[0, i]).wait()
+        a = normed_ref[rows, :]
         live = iota((B, 512), 0) + i * B < length
         for n in range(4):
             cols = slice(n * 512, (n + 1) * 512)
-            v = silu_of_half(0.5 * (dot(a, own_ref[:, cols]) + dot(b, other_ref[:, cols])))
+            v = silu_of_half(0.5 * dot(a, all_ref[:, cols]))
             if n == 1:
                 v = jnp.where(live, v, 0.0)
             act_ref[rows, cols] = v.astype(BF)
 
     for b in range(16):
-        block = slice(b * 16, (b + 1) * 16)
-        w_ref[pl.ds(pl.multiple_of(b * 32 + core * 16, 16), 16), :] = own_ref[block, 2048:]
-        w_ref[pl.ds(pl.multiple_of(b * 32 + (1 - core) * 16, 16), 16), :] = other_ref[block, 2048:]
-    for copy in inputs[3:]:
-        copy.wait()
+        own, other = slice(b * 16, (b + 1) * 16), slice(B + b * 16, B + (b + 1) * 16)
+        w_ref[pl.ds(pl.multiple_of(b * 32 + core * 16, 16), 16), :] = all_ref[own, 2048:]
+        w_ref[pl.ds(pl.multiple_of(b * 32 + (1 - core) * 16, 16), 16), :] = all_ref[other, 2048:]
+
     causal = iota((B, B), 1) <= iota((B, B), 0)
     eye = iota((B, B), 1) == iota((B, B), 0)
     scale = 0.5 / math.sqrt(128)
-    for i in range(4):
-        rows = slice(i * B, (i + 1) * B)
-        for h in range(H):
+    hidden_out = []
+    for i, rows in enumerate(blocks):
+
+        def scores(h, j):
             q = act_ref[rows, 1024 + h * 128 : 1024 + (h + 1) * 128]
-            total = None
-            for j in range(i + 1):
-                keys = slice(j * B, (j + 1) * B)
-                s = dot_nt(q, act_ref[keys, 1536 + h * 128 : 1536 + (h + 1) * 128])
-                w = silu_of_half(s * scale)
-                if j == i:
-                    w = jnp.where(causal, w, 0.0)
-                t = dot(w.astype(BF), act_ref[keys, 512 + h * 128 : 512 + (h + 1) * 128])
-                total = t if total is None else total + t
-            att_ref[:, h * 128 : (h + 1) * 128] = total
+            return dot_nt(q, act_ref[blocks[j], 1536 + h * 128 : 1536 + (h + 1) * 128])
+
+        work = [(h, j) for h in range(H) for j in range(i + 1)]
+        ahead = [scores(*work[0]), scores(*work[1])]
+        for n, (h, j) in enumerate(work):
+            s = ahead.pop(0)
+            if n + 2 < len(work):
+                ahead.append(scores(*work[n + 2]))
+            w = silu_of_half(s * scale)
+            if j == i:
+                w = jnp.where(causal, w, 0.0)
+            t = dot(w.astype(BF), act_ref[blocks[j], 512 + h * 128 : 512 + (h + 1) * 128])
+            total = t if j == 0 else total + t
+            if j == i:
+                att_ref[:, h * 128 : (h + 1) * 128] = total
         gated = (layer_norm(att_ref[...]) * act_ref[rows, :512].astype(F32)).astype(BF)
+        events_in[i].wait()
+        follow_in[i].wait()
         hidden = (events_ref[rows, :].astype(F32) + dot(gated, w_ref[...])).astype(BF)
         hidden_ref[rows, :] = hidden
+        hidden_out.append(pltpu.make_async_copy(hidden_ref.at[rows, :], hidden_hbm.at[rows, :], out_sem.at[6 + i]))
+        hidden_out[-1].start()
         pos = jnp.sum(hidden.astype(F32) * follow_ref[rows, :].astype(F32), axis=1, keepdims=True)
         positive_ref[:, rows] = jnp.sum(jnp.where(eye, pos, 0.0), axis=0, keepdims=True)
 
-    hidden_out = pltpu.make_async_copy(hidden_ref, hidden_hbm, out_sem.at[0])
-    hidden_out.start()
     outs = []
     for m in range(SLOTS // B):
         rows = slice(m * B, (m + 1) * B)
         send_ref[rows, :] = dot(onehot(m * B, B, slot_ref[0:1, :]), hidden_ref[...]).astype(BF)
-        outs.append(pltpu.make_async_copy(send_ref.at[rows, :], send_hbm.at[rows, :], out_sem.at[1 + m]))
+        outs.append(pltpu.make_async_copy(send_ref.at[rows, :], send_hbm.at[rows, :], out_sem.at[m]))
         outs[-1].start()
-    hidden_out.wait()
-    for copy in outs:
+    for copy in hidden_out + outs:
         copy.wait()
 
 
@@ -451,8 +464,7 @@
         out_specs=(VMEM, any_space, any_space),
         scratch_shapes=[
             pltpu.VMEM((512, 512), BF),
-            pltpu.VMEM((256, 2560), BF),
-            pltpu.VMEM((256, 2560), BF),
+            pltpu.VMEM((512, 2560), BF),
             pltpu.VMEM((1024, width), BF),
             pltpu.VMEM((1024, width), BF),
             pltpu.VMEM((1024, width), BF),
@@ -460,11 +472,11 @@
             pltpu.VMEM((B, width), F32),
             pltpu.VMEM((1024, width), BF),
             pltpu.VMEM((SLOTS, width), BF),
-            pltpu.SemaphoreType.DMA((5,)),
-            pltpu.SemaphoreType.DMA((7,)),
+            pltpu.SemaphoreType.DMA((4, 4)),
+            pltpu.SemaphoreType.DMA((10,)),
         ],
         cost_estimate=pl.CostEstimate(flops=0, bytes_accessed=0, transcendentals=0),
-        compiler_params=pltpu.CompilerParams(vmem_limit_bytes=56 << 20),
+        compiler_params=pltpu.CompilerParams(vmem_limit_bytes=52 << 20),
     )(info, target_slot, w_own, normed, w_other, ev, follow)
     got_neg, send_rows = lax.optimization_barrier((got_neg, send_rows))
     other_neg = swap(got_neg)

time: 125 us -> 123 us (0.984)
  local copies, waits for them, and re-layouts: 14.3 us -> 11.4 us
  waiting for transfers between devices: 15.6 us -> 18 us
  starting transfers between devices: 39.3 us -> 37.9 us
    unnamed x36 -> x42, local copies, waits for them, and re-layouts: 8.27 us -> 5.42 us
    all_to_all x3, starting transfers between devices: 21.4 us -> 18.9 us  [chips_a2a(): return lax.all_to_all(v, CHIPS, split_axis=0, concat_axis=0, tiled=True)]
    all_to_all x3, waiting for transfers between devices: 10.9 us -> 12.7 us  [chips_a2a(): return lax.all_to_all(v, CHIPS, split_axis=0, concat_axis=0, tiled=True)]
    pallas_call x1, Pallas kernels: 15.9 us -> 14.2 us  [per_device(): pl.pallas_call(layer_kernel, out_shape=(jax.ShapeDtypeStruct((1, 1024), F...]
    pallas_call x1, Pallas kernels: 0.17 us -> 1.45 us  [per_device(): call(unpack_kernel, (jax.ShapeDtypeStruct((SLOTS, B), BF), jax.ShapeDtype...]
  transfers between devices with their start and end apart: 10 -> 10, of which waited for: 5 -> 6; matrix products, arithmetic and copies ran while one was open for 4% -> 4% of each run, Pallas kernels for 36% -> 37%
where the time goes in v5:
time: 123 us; the launch traced here: 122 us
  Pallas kernels  51.7 us (42%)
  starting transfers between devices  37.9 us (31%)
  waiting for transfers between devices  18 us (15%)
  local copies, waits for them, and re-layouts  11.4 us (9%)
  between operations  1.79 us (1%)
  other arithmetic  1.25 us (1%)
    all_to_all x3, starting transfers between devices, chips_a2a(): return lax.all_to_all(v, CHIPS, split_axis=0, concat_axis=0, tiled=True)  18.9 us
    pallas_call x1, Pallas kernels, per_device(): pl.pallas_call(layer_kernel, out_shape=(jax.ShapeDtypeStruct((1, 1024), F...  14.2 us
    all_to_all x3, waiting for transfers between devices, chips_a2a(): return lax.all_to_all(v, CHIPS, split_axis=0, concat_axis=0, tiled=True)  12.7 us
    ppermute x6, starting transfers between devices, swap(): return lax.ppermute(v, 'c', SWAP)  10.4 us
    all_to_all x1, starting transfers between devices, per_device(): lax.all_to_all(jnp.broadcast_to(w_mine[None], (16,) + w_mine.shape), ('x'...  8.62 us
    pallas_call x1, Pallas kernels, per_device(): call(sort_kernel, jax.ShapeDtypeStruct((PLACES, width), BF), [VMEM] * 3,...  8.05 us
    pallas_call x1, Pallas kernels, per_device(): call(loss_kernel, (jax.ShapeDtypeStruct((1, 1024), F32), jax.ShapeDtypeSt...  7.56 us
    pallas_call x1, Pallas kernels, per_device(): pl.pallas_call(place_kernel, out_shape=jax.ShapeDtypeStruct((ITEMS_DEV, w...  6.44 us
  transfers between devices with their start and end apart: 10, of which 6 were waited for; matrix products, arithmetic and copies ran while one was open for 4% of the time, Pallas kernels for 37%

profile of v5, /device:TPU:1, one launch (start us, length us, event | category | flops | bytes accessed | tf_op | source)
XLA Modules:
  0.0 122.0 jit_solution(1495048653915200028)
XLA Ops:
  0.6 0.9 pad_maximum_fusion
  1.5 1.2 broadcast_in_dim.31
  2.7 8.6 %all-to-all-start = ((bf16[16,16,2560]{2,1,0:T(8,128)(2,1)}), bf16[16,16,2560]{2,1,0:T(8,128)(2,1)}, u32[]{:S(2)}, u32[]{:S(2)}) async-start(bf16[16,16,2560]{2,1,0:T(8,128)(2,1)} %broadcast_in_dim.31), calls=%async_computation | async-start | bytes 2621440 | tf_op jit(solution)/shard_map/all_to_all | solution.py:424
  12.1 5.1 %shard_map.95 = (bf16[1024,512]{1,0:T(8,128)(2,1)S(1)}, s32[1536,128]{1,0:T(8,128)S(1)}, f32[1536,128]{1,0:T(8,128)S(1)}, s32[3,1024]{1,0:T(4,128)S(1)}, f32[2,6...) custom-call(s32[3]{0:T(128)S(1)} %pad_add_fusion.info_ref, bf16[1024,512]{1,0:T(8,128)(2,1)S(1)} %bitcast.12, ...), custom_call_target="tpu_custom_call" | custom-call | tf_op jit(solution)/shard_map/pallas_call | solution.py:428
  17.2 1.0 copy-done.3
  18.2 0.9 copy-done.4
  19.1 0.9 copy-done.6
  20.1 3.4 %gather_fusion = bf16[32,512]{1,0:T(8,128)(2,1)S(1)} fusion(bf16[4096,512]{1,0:T(8,128)(2,1)} %param.13, s32[1024]{0:T(1024)S(1)} %pad_clamp_fusion), kind=kCustom, calls=%fused_computation | custom fusion | bytes 65664 | tf_op jit(solution)/shard_map/gather | solution.py:444
  23.7 1.0 collective-permute-start
  25.0 1.0 concatenate.7.follow_hbm
  26.0 1.1 shard_map.96
  27.1 2.4 %all-to-all-done = bf16[16,16,2560]{2,1,0:T(8,128)(2,1)} async-done(((bf16[16,16,2560]{2,1,0:T(8,128)(2,1)}), bf16[16,16,2560]{2,1,0:T(8,128)(2,1)}, u32[]{:S(2)}, u32[]{:S(2)}) %all-to-all-start) | async-done | bytes 1310752 | tf_op jit(solution)/shard_map/all_to_all | solution.py:424
  29.5 3.7 %collective-permute-start.1 = (bf16[256,2560]{1,0:T(8,128)(2,1)}, bf16[256,2560]{1,0:T(8,128)(2,1)}, u32[]{:S(2)}, u32[]{:S(2)}) collective-permute-start(bf16[256,2560]{1,0:T(8,128)(2,1)} %bitcast.5.own_hbm), channel_id=1, source_target_pairs={{0,1},{1,0},{2,3},{3,2},{4,5},{5,4},{6,7},{7,6},{8,9},{9,8},{10,11... | collective-permute-start | bytes 3932168 | tf_op jit(solution)/shard_map/ppermute | solution.py:409
  33.1 6.9 %all-to-all-start.1 = ((bf16[64,56,128]{2,1,0:T(8,128)(2,1)}), bf16[64,56,128]{2,1,0:T(8,128)(2,1)S(1)}, u32[]{:S(2)}, u32[]{:S(2)}) async-start(bf16[64,56,128]{2,1,0:T(8,128)(2,1)} %shard_map.96), calls=%async_computation.1 | async-start | bytes 1835008 | tf_op jit(solution)/shard_map/all_to_all | solution.py:413
  40.1 14.2 %shard_map.97 = (f32[1,1024]{1,0:T(1,128)S(1)}, bf16[1024,512]{1,0:T(8,128)(2,1)S(1)}, bf16[1536,512]{1,0:T(8,128)(2,1)}) custom-call(s32[3]{0:T(128)S(1)} %pad_add_fusion.info_ref, s32[3,1024]{1,0:T(4,128)S(1)} %get-tuple-element.32.slot_ref, bf16[256,2560]{1,0:T(8,128)(2,1)} %bitcast.5.own_hbm, bf16[1024,512]{1,0:T(8,128)(2,1)} %copy-done.3, ...), custom_call_target="tpu_custom_call" | custom-call | tf_op jit(solution)/shard_map/pallas_call | solution.py:456
  54.9 1.6 %all-to-all-done.1.own_ref = bf16[64,56,128]{2,1,0:T(8,128)(2,1)S(1)} async-done(((bf16[64,56,128]{2,1,0:T(8,128)(2,1)}), bf16[64,56,128]{2,1,0:T(8,128)(2,1)S(1)}, u32[]{:S(2)}, u32[]{:S(2)}) %all-to-all-start.1) | async-done | bytes 917536 | tf_op jit(solution)/shard_map/all_to_all | solution.py:413
  56.5 1.7 %collective-permute-start.2 = (bf16[64,56,128]{2,1,0:T(8,128)(2,1)S(1)}, bf16[64,56,128]{2,1,0:T(8,128)(2,1)}, u32[]{:S(2)}, u32[]{:S(2)}) collective-permute-start(bf16[64,56,128]{2,1,0:T(8,128)(2,1)S(1)} %all-to-all-done.1.own_ref), channel_id=1, source_target_pairs={{0,1},{1,0},{2,3},{3,2},{4,5},{5,4},{6,7},{7,6},{8,9},{9,8},{10,11... | collective-permute-start | bytes 2752520 | tf_op jit(solution)/shard_map/ppermute | solution.py:409
  58.2 6.9 %all-to-all-start.2 = ((bf16[64,24,512]{2,1,0:T(8,128)(2,1)}), bf16[64,24,512]{2,1,0:T(8,128)(2,1)S(1)}, u32[]{:S(2)}, u32[]{:S(2)}) async-start(bf16[64,24,512]{2,1,0:T(8,128)(2,1)} %bitcast.18), calls=%async_computation.2 | async-start | bytes 3145728 | tf_op jit(solution)/shard_map/all_to_all | solution.py:413
  65.1 1.5 %shard_map.98 = (bf16[1536,256]{1,0:T(8,128)(2,1)S(1)}, bf16[1536,256]{1,0:T(8,128)(2,1)S(1)}, s32[2,64,128]{2,1,0:T(8,128)S(1)}) custom-call(bf16[64,56,128]{2,1,0:T(8,128)(2,1)S(1)} %all-to-all-done.1.own_ref, bf16[64,56,128]{2,1,0:T(8,128)(2,1)} %collective-permute-done.2.other_ref), custom_call_target="tpu_custom_call" | custom-call | tf_op jit(solution)/shard_map/pallas_call | solution.py:484
  67.2 7.6 %shard_map.99 = (f32[1,1024]{1,0:T(1,128)}, f32[1536,256]{1,0:T(8,128)S(1)}, bf16[1536,256]{1,0:T(8,128)(2,1)S(1)}, f32[3,64,128]{2,1,0:T(8,128)S(1)}) custom-call(s32[3]{0:T(128)S(1)} %copy-done.15, bf16[1024,512]{1,0:T(8,128)(2,1)S(1)} %get-tuple-element.39.hidden_ref, bf16[1536,256]{1,0:T(8,128)(2,1)S(1)} %get-tuple-element.43.own_ref, ...), custom_call_target="tpu_custom_call" | custom-call | tf_op jit(solution)/shard_map/pallas_call | solution.py:497
  75.1 2.0 %collective-permute-done.3.other_ref = bf16[1536,256]{1,0:T(8,128)(2,1)S(1)} collective-permute-done((bf16[1536,256]{1,0:T(8,128)(2,1)S(1)}, bf16[1536,256]{1,0:T(8,128)(2,1)S(1)}, u32[]{:S(2)}, u32[]{:S(2)}) %collective-permute-start.3) | collective-permute-done | bytes 786464 | tf_op jit(solution)/shard_map/ppermute | solution.py:409
  77.1 1.2 shard_map.101
  78.3 10.3 %all-to-all-done.2 = bf16[64,24,512]{2,1,0:T(8,128)(2,1)S(1)} async-done(((bf16[64,24,512]{2,1,0:T(8,128)(2,1)}), bf16[64,24,512]{2,1,0:T(8,128)(2,1)S(1)}, u32[]{:S(2)}, u32[]{:S(2)}) %all-to-all-start.2) | async-done | bytes 1572896 | tf_op jit(solution)/shard_map/all_to_all | solution.py:413
  88.5 1.6 %collective-permute-start.4 = (bf16[1536,512]{1,0:T(8,128)(2,1)S(1)}, bf16[1536,512]{1,0:T(8,128)(2,1)}, u32[]{:S(2)}, u32[]{:S(2)}) collective-permute-start(bf16[1536,512]{1,0:T(8,128)(2,1)S(1)} %bitcast.13), channel_id=1, source_target_pairs={{0,1},{1,0},{2,3},{3,2},{4,5},{5,4},{6,7},{7,6},{8,9},{9,8},{10,11... | collective-permute-start | bytes 4718600 | tf_op jit(solution)/shard_map/ppermute | solution.py:409
  90.2 5.1 %all-to-all-start.3 = ((bf16[64,56,128]{2,1,0:T(8,128)(2,1)}), bf16[64,56,128]{2,1,0:T(8,128)(2,1)S(1)}, u32[]{:S(2)}, u32[]{:S(2)}) async-start(bf16[64,56,128]{2,1,0:T(8,128)(2,1)} %shard_map.101), calls=%async_computation.3 | async-start | bytes 1835008 | tf_op jit(solution)/shard_map/all_to_all | solution.py:413
  95.4 6.1 %shard_map.100 = (s32[1,3072]{1,0:T(1,128)S(1)}, s32[16,128]{1,0:T(8,128)S(1)}, s32[32]{0:T(128)S(1)}, s32[48]{0:T(128)S(1)}) custom-call(s32[3]{0:T(128)S(1)} %copy-done.16, s32[1,3072]{1,0:T(1,128)S(1)} %reshape.19.row_ref, s32[32,128]{1,0:T(8,128)S(1)} %get-tuple-element.34.neg_ref), custom_call_target="tpu_custom_call" | custom-call | tf_op jit(solution)/shard_map/pallas_call | solution.py:524
  101.6 1.4 %copy-done.2 = bf16[64,24,512]{2,1,0:T(8,128)(2,1)S(1)} copy-done((bf16[64,24,512]{2,1,0:T(8,128)(2,1)S(1)}, bf16[64,24,512]{2,1,0:T(8,128)(2,1)}, u32[]{:S(2)}) %copy-start.2) | copy-done | bytes 1572888
  103.0 8.1 %shard_map.102.rows_ref = bf16[2048,512]{1,0:T(8,128)(2,1)S(1)} custom-call(s32[1,3072]{1,0:T(1,128)S(1)} %get-tuple-element.57.at_ref, bf16[1536,512]{1,0:T(8,128)(2,1)S(1)} %bitcast.14, bf16[1536,512]{1,0:T(8,128)(2,1)} %collective-permute-done.4.other_ref), custom_call_target="tpu_custom_call" | custom-call | tf_op jit(solution)/shard_map/pallas_call | solution.py:537
  111.0 0.9 all-to-all-done.3.got_ref
  112.4 2.0 %collective-permute-start.5 = (f32[32,256]{1,0:T(8,128)S(1)}, f32[32,256]{1,0:T(8,128)S(1)}, u32[]{:S(2)}, u32[]{:S(2)}) collective-permute-start(f32[32,256]{1,0:T(8,128)S(1)} %shard_map.103.small_ref), channel_id=1, source_target_pairs={{0,1},{1,0},{2,3},{3,2},{4,5},{5,4},{6,7},{7,6},{8,9},{9,8},{10,11... | collective-permute-start | bytes 98312 | tf_op jit(solution)/shard_map/ppermute | solution.py:409
  114.5 0.9 collective-permute-done.5.small_other_ref
  115.3 6.4 %shard_map.104 = bf16[4096,512]{1,0:T(8,128)(2,1)} custom-call(s32[32]{0:T(128)S(1)} %get-tuple-element.50.start_ref, s32[48]{0:T(128)S(1)} %get-tuple-element.51.neg_at_ref, f32[32,256]{1,0:T(8,128)S(1)} %shard_map.103.small_ref, f32[32,256]{1,0:T(8,128)S(1)} %collective-permute-done.5.small_other_ref, s32[1,3072]{1,0:T(1,128)S(1)} %get-tuple-element.57.at_ref, ...), custom_call_target="tpu_custom_call" | custom-call | tf_op jit(solution)/shard_map/pallas_call | solution.py:545
  (52 shorter events, 2.8 us)
Async XLA Ops:
  2.7 9.4 %copy-start = (bf16[1,1024,512]{2,1,0:T(8,128)(2,1)S(1)}, bf16[1,1024,512]{2,1,0:T(8,128)(2,1)}, u32[]{:S(2)}) copy-start(bf16[1,1024,512]{2,1,0:T(8,128)(2,1)} %param.8) | copy-start | bytes 3145732
  2.7 9.4 %copy-start.12 = (s32[1,1024]{1,0:T(1,128)S(1)}, s32[1,1024]{1,0:T(1,128)}, u32[]{:S(2)}) copy-start(s32[1,1024]{1,0:T(1,128)} %targets_ref.3) | copy-start | bytes 12292
  2.7 9.4 %copy-start.17 = (s32[1024]{0:T(1024)S(1)}, s32[1024]{0:T(1024)}, u32[]{:S(2)}) copy-start(s32[1024]{0:T(1024)} %param.11) | copy-start | bytes 12292
  2.7 9.4 %copy-start.18 = (s32[1024]{0:T(1024)S(1)}, s32[1024]{0:T(1024)}, u32[]{:S(2)}) copy-start(s32[1024]{0:T(1024)} %param.12) | copy-start | bytes 12292
  2.7 26.8 %all-to-all-start = ((bf16[16,16,2560]{2,1,0:T(8,128)(2,1)}), bf16[16,16,2560]{2,1,0:T(8,128)(2,1)}, u32[]{:S(2)}, u32[]{:S(2)}) async-start(bf16[16,16,2560]{2,1,0:T(8,128)(2,1)} %broadcast_in_dim.31), calls=%async_computation | async-start | bytes 2621440 | tf_op jit(solution)/shard_map/all_to_all | solution.py:424
  12.0 28.0 %copy-start.14 = (s32[3]{0:T(128)}, s32[3]{0:T(128)S(1)}, u32[]{:S(2)}) copy-start(s32[3]{0:T(128)S(1)} %pad_add_fusion.info_ref) | copy-start | bytes 40
  17.2 1.0 copy-start.3
  18.2 0.9 copy-start.4
  19.1 0.9 copy-start.6
  20.0 20.1 %copy-start.8 = (s32[3,1024]{1,0:T(4,128)}, s32[3,1024]{1,0:T(4,128)S(1)}, u32[]{:S(2)}) copy-start(s32[3,1024]{1,0:T(4,128)S(1)} %get-tuple-element.32.slot_ref) | copy-start | bytes 36868
  23.7 2.3 %collective-permute-start = (bf16[32,256]{1,0:T(8,128)(2,1)S(1)}, bf16[32,256]{1,0:T(8,128)(2,1)S(1)}, u32[]{:S(2)}, u32[]{:S(2)}) collective-permute-start(bf16[32,256]{1,0:T(8,128)(2,1)S(1)} %get-tuple-element.62), channel_id=1, source_target_pairs={{0,1},{1,0},{2,3},{3,2},{4,5},{5,4},{6,7},{7,6},{8,9},{9,8},{10,11... | collective-permute-start | bytes 49160 | tf_op jit(solution)/shard_map/ppermute | solution.py:409
  29.5 10.6 %collective-permute-start.1 = (bf16[256,2560]{1,0:T(8,128)(2,1)}, bf16[256,2560]{1,0:T(8,128)(2,1)}, u32[]{:S(2)}, u32[]{:S(2)}) collective-permute-start(bf16[256,2560]{1,0:T(8,128)(2,1)} %bitcast.5.own_hbm), channel_id=1, source_target_pairs={{0,1},{1,0},{2,3},{3,2},{4,5},{5,4},{6,7},{7,6},{8,9},{9,8},{10,11... | collective-permute-start | bytes 3932168 | tf_op jit(solution)/shard_map/ppermute | solution.py:409
  33.1 23.4 %all-to-all-start.1 = ((bf16[64,56,128]{2,1,0:T(8,128)(2,1)}), bf16[64,56,128]{2,1,0:T(8,128)(2,1)S(1)}, u32[]{:S(2)}, u32[]{:S(2)}) async-start(bf16[64,56,128]{2,1,0:T(8,128)(2,1)} %shard_map.96), calls=%async_computation.1 | async-start | bytes 1835008 | tf_op jit(solution)/shard_map/all_to_all | solution.py:413
  54.3 0.6 copy-start.19
  56.5 8.6 %collective-permute-start.2 = (bf16[64,56,128]{2,1,0:T(8,128)(2,1)S(1)}, bf16[64,56,128]{2,1,0:T(8,128)(2,1)}, u32[]{:S(2)}, u32[]{:S(2)}) collective-permute-start(bf16[64,56,128]{2,1,0:T(8,128)(2,1)S(1)} %all-to-all-done.1.own_ref), channel_id=1, source_target_pairs={{0,1},{1,0},{2,3},{3,2},{4,5},{5,4},{6,7},{7,6},{8,9},{9,8},{10,11... | collective-permute-start | bytes 2752520 | tf_op jit(solution)/shard_map/ppermute | solution.py:409
  58.2 30.4 %all-to-all-start.2 = ((bf16[64,24,512]{2,1,0:T(8,128)(2,1)}), bf16[64,24,512]{2,1,0:T(8,128)(2,1)S(1)}, u32[]{:S(2)}, u32[]{:S(2)}) async-start(bf16[64,24,512]{2,1,0:T(8,128)(2,1)} %bitcast.18), calls=%async_computation.2 | async-start | bytes 3145728 | tf_op jit(solution)/shard_map/all_to_all | solution.py:413
  65.1 2.1 %copy-start.5 = (s32[1536,128]{1,0:T(8,128)S(1)}, s32[1536,128]{1,0:T(8,128)}, u32[]{:S(2)}) copy-start(s32[1536,128]{1,0:T(8,128)} %copy-done.4) | copy-start | bytes 2359300
  65.1 2.1 %copy-start.7 = (f32[1536,128]{1,0:T(8,128)S(1)}, f32[1536,128]{1,0:T(8,128)}, u32[]{:S(2)}) copy-start(f32[1536,128]{1,0:T(8,128)} %copy-done.6) | copy-start | bytes 2359300
  65.1 2.1 %copy-start.9 = (s32[3,1024]{1,0:T(4,128)S(1)}, s32[3,1024]{1,0:T(4,128)}, u32[]{:S(2)}) copy-start(s32[3,1024]{1,0:T(4,128)} %copy-done.8) | copy-start | bytes 36868
  65.1 2.1 %copy-start.13 = (s32[1,1024]{1,0:T(1,128)S(1)}, s32[1,1024]{1,0:T(1,128)}, u32[]{:S(2)}) copy-start(s32[1,1024]{1,0:T(1,128)} %targets_ref.3) | copy-start | bytes 12292
  65.1 2.1 %copy-start.15 = (s32[3]{0:T(128)S(1)}, s32[3]{0:T(128)}, u32[]{:S(2)}) copy-start(s32[3]{0:T(128)} %copy-done.14) | copy-start | bytes 40
  65.1 2.1 %copy-start.20 = (f32[1,1024]{1,0:T(1,128)S(1)}, f32[1,1024]{1,0:T(1,128)}, u32[]{:S(2)}) copy-start(f32[1,1024]{1,0:T(1,128)} %copy-done.19) | copy-start | bytes 12292
  66.6 0.6 copy-start.10
  74.8 2.3 %collective-permute-start.3 = (bf16[1536,256]{1,0:T(8,128)(2,1)S(1)}, bf16[1536,256]{1,0:T(8,128)(2,1)S(1)}, u32[]{:S(2)}, u32[]{:S(2)}) collective-permute-start(bf16[1536,256]{1,0:T(8,128)(2,1)S(1)} %get-tuple-element.54), channel_id=1, source_target_pairs={{0,1},{1,0},{2,3},{3,2},{4,5},{5,4},{6,7},{7,6},{8,9},{9,8},{10,11... | collective-permute-start | bytes 2359304 | tf_op jit(solution)/shard_map/ppermute | solution.py:409
  78.2 17.0 %copy-start.11 = (s32[2,64,128]{2,1,0:T(8,128)S(1)}, s32[2,64,128]{2,1,0:T(8,128)}, u32[]{:S(2)}) copy-start(s32[2,64,128]{2,1,0:T(8,128)} %copy-done.10) | copy-start | bytes 196612
  78.3 17.1 %copy-start.16 = (s32[3]{0:T(128)S(1)}, s32[3]{0:T(128)}, u32[]{:S(2)}) copy-start(s32[3]{0:T(128)} %copy-done.14) | copy-start | bytes 40
  88.5 13.0 %copy-start.1 = (bf16[64,24,512]{2,1,0:T(8,128)(2,1)}, bf16[64,24,512]{2,1,0:T(8,128)(2,1)S(1)}, u32[]{:S(2)}) copy-start(bf16[64,24,512]{2,1,0:T(8,128)(2,1)S(1)} %all-to-all-done.2) | copy-start | bytes 4718596
  88.5 13.0 %collective-permute-start.4 = (bf16[1536,512]{1,0:T(8,128)(2,1)S(1)}, bf16[1536,512]{1,0:T(8,128)(2,1)}, u32[]{:S(2)}, u32[]{:S(2)}) collective-permute-start(bf16[1536,512]{1,0:T(8,128)(2,1)S(1)} %bitcast.13), channel_id=1, source_target_pairs={{0,1},{1,0},{2,3},{3,2},{4,5},{5,4},{6,7},{7,6},{8,9},{9,8},{10,11... | collective-permute-start | bytes 4718600 | tf_op jit(solution)/shard_map/ppermute | solution.py:409
  90.2 21.7 %all-to-all-start.3 = ((bf16[64,56,128]{2,1,0:T(8,128)(2,1)}), bf16[64,56,128]{2,1,0:T(8,128)(2,1)S(1)}, u32[]{:S(2)}, u32[]{:S(2)}) async-start(bf16[64,56,128]{2,1,0:T(8,128)(2,1)} %shard_map.101), calls=%async_computation.3 | async-start | bytes 1835008 | tf_op jit(solution)/shard_map/all_to_all | solution.py:413
  101.6 1.4 %copy-start.2 = (bf16[64,24,512]{2,1,0:T(8,128)(2,1)S(1)}, bf16[64,24,512]{2,1,0:T(8,128)(2,1)}, u32[]{:S(2)}) copy-start(bf16[64,24,512]{2,1,0:T(8,128)(2,1)} %copy-done.1) | copy-start | bytes 4718596
  112.4 2.9 %collective-permute-start.5 = (f32[32,256]{1,0:T(8,128)S(1)}, f32[32,256]{1,0:T(8,128)S(1)}, u32[]{:S(2)}, u32[]{:S(2)}) collective-permute-start(f32[32,256]{1,0:T(8,128)S(1)} %shard_map.103.small_ref), channel_id=1, source_target_pairs={{0,1},{1,0},{2,3},{3,2},{4,5},{5,4},{6,7},{7,6},{8,9},{9,8},{10,11... | collective-permute-start | bytes 98312 | tf_op jit(solution)/shard_map/ppermute | solution.py:409

commit v6 on v5

--- a/solution.py
+++ b/solution.py
@@ -67,12 +67,11 @@
     return (iota((count, index.shape[1]), 0) + base == index).astype(F32).astype(BF)
 
 
-def by_place(high, low, pieces, count, weights=(1.0, 1.0, 1.0)):
+def by_place(high, low, pieces, count):
     rows = iota((count, high.shape[1]), 0) == high
-    cols = onehot(0, 128, low)
-    return sum(
-        w * dot_nt(jnp.where(rows, p.astype(F32), 0.0).astype(BF), cols) for p, w in zip(pieces, weights)
-    )
+    stacked = jnp.concatenate([jnp.where(rows, p.astype(F32), 0.0) for p in pieces], axis=0).astype(BF)
+    got = dot_nt(stacked, onehot(0, 128, low))
+    return [got[k * count : (k + 1) * count] for k in range(len(pieces))]
 
 
 def prep_kernel(
@@ -102,8 +101,7 @@
     slot_ref[2:3, :] = t_within
     n_slot = (n_owner >> 1) * CSLOTS + within(n_owner, n_rank)
     row = (targets & (2 * ITEMS_DEV - 1)) + 1
-    row_ref[0] = by_place(t_owner >> 1, t_within, [row >> 6], NCHIPS)
-    row_ref[1] = by_place(t_owner >> 1, t_within, [row & 63], NCHIPS)
+    row_ref[0], row_ref[1] = by_place(t_owner >> 1, t_within, [row >> 6, row & 63], NCHIPS)
 
     mine = (iota((32, n), 0) + chip * CSLOTS == n_slot) & ((n_owner & 1) == core)
     mine = mine & (iota((32, n), 0) < CSLOTS)
@@ -292,8 +290,9 @@
     high = coef.astype(BF).astype(F32)
     middle = (coef - high).astype(BF).astype(F32)
     low = coef - high - middle
-    for k, piece in enumerate((high, middle, low)):
-        meta_ref[k] = by_place(slot_ref[1:2, :], slot_ref[2:3, :], [piece], NCHIPS)
+    pieces = by_place(slot_ref[1:2, :], slot_ref[2:3, :], [high, middle, low], NCHIPS)
+    for k, piece in enumerate(pieces):
+        meta_ref[k] = piece
     for m in chunks:
         term_other_ref[m, :] = dot(probs_ref[m, :], hidden_ref[:, other_cols]).astype(BF)
         term_own_ref[m, :] = dot(probs_ref[m, :], hidden_ref[:, own_cols])
@@ -326,7 +325,8 @@
         neg_at_ref[16 + p] = found >> 6
     for i in range(ITEMS_DEV // TILE + 1):
         neg_at_ref[32 + i] = jnp.sum(((neg_row >> 6) < i * TILE).astype(I32))
-    sorted_key_ref[...] = by_place(at >> 7, at & 127, [row >> 6, row & 63], PLACES // 128, (64.0, 1.0)).astype(I32)
+    key_high, key_low = by_place(at >> 7, at & 127, [row >> 6, row & 63], PLACES // 128)
+    sorted_key_ref[...] = (key_high * 64.0 + key_low).astype(I32)
 
 
 def sort_kernel(at_ref, own_ref, other_ref, sorted_ref):
@@ -368,12 +368,12 @@
     top = coef.astype(BF).astype(F32)
     middle = (coef - top).astype(BF).astype(F32)
     at = at_ref[...]
-    coef = by_place(at >> 7, at & 127, [top, middle, coef - top - middle], PLACES // 128)
-    eye = iota((128, 128), 1) == iota((128, 128), 0)
+    top, middle, low = by_place(at >> 7, at & 127, [top, middle, coef - top - middle], PLACES // 128)
+    coef = top + middle + low
+    cols = jnp.transpose(jnp.concatenate([coef, jnp.zeros((128 - coef.shape[0], 128), F32)], axis=0))
     for m in range(PLACES // 128):
         block = slice(m * 128, (m + 1) * 128)
-        col = jnp.sum(jnp.where(eye, coef[m : m + 1, :], 0.0), axis=1, keepdims=True)
-        scaled_ref[block, :] = (rows_ref[block, :].astype(F32) * col).astype(BF)
+        scaled_ref[block, :] = (rows_ref[block, :].astype(F32) * cols[:, m : m + 1]).astype(BF)
     own, other = small_ref[:CSLOTS, :], small_other_ref[:CSLOTS, :]
     first = start_ref[31] == 0
     neg_ref[...] = jnp.concatenate([jnp.where(first, own, other), jnp.where(first, other, own)], axis=1)
@@ -527,7 +527,7 @@
             jax.ShapeDtypeStruct((1, 2 * SLOTS), I32),
             jax.ShapeDtypeStruct((PLACES // 128, 128), I32),
             jax.ShapeDtypeStruct((32,), I32),
-            jax.ShapeDtypeStruct((48,), I32),
+            jax.ShapeDtypeStruct((64,), I32),
         ),
         in_specs=[SMEM, VMEM, VMEM],
         out_specs=(VMEM, VMEM, SMEM, SMEM),

time: 123 us -> 122 us (level)
  no operation moved by 1% of the time
where the time goes in v6:
time: 122 us
  Pallas kernels  51.3 us (42%)
  starting transfers between devices  37.9 us (31%)
  waiting for transfers between devices  18.1 us (15%)
  local copies, waits for them, and re-layouts  11.4 us (9%)
  between operations  1.79 us (1%)
  other arithmetic  1.25 us (1%)
    all_to_all x3, starting transfers between devices, chips_a2a(): return lax.all_to_all(v, CHIPS, split_axis=0, concat_axis=0, tiled=True)  18.9 us
    pallas_call x1, Pallas kernels, per_device(): pl.pallas_call(layer_kernel, out_shape=(jax.ShapeDtypeStruct((1, 1024), F...  14.2 us
    all_to_all x3, waiting for transfers between devices, chips_a2a(): return lax.all_to_all(v, CHIPS, split_axis=0, concat_axis=0, tiled=True)  12.9 us
    ppermute x6, starting transfers between devices, swap(): return lax.ppermute(v, 'c', SWAP)  10.4 us
    all_to_all x1, starting transfers between devices, per_device(): lax.all_to_all(jnp.broadcast_to(w_mine[None], (16,) + w_mine.shape), ('x'...  8.62 us
    pallas_call x1, Pallas kernels, per_device(): call(sort_kernel, jax.ShapeDtypeStruct((PLACES, width), BF), [VMEM] * 3,...  8.05 us
    pallas_call x1, Pallas kernels, per_device(): call(loss_kernel, (jax.ShapeDtypeStruct((1, 1024), F32), jax.ShapeDtypeSt...  7.39 us
    pallas_call x1, Pallas kernels, per_device(): pl.pallas_call(rank_kernel, out_shape=(jax.ShapeDtypeStruct((1, 2 * SLOTS...  6.14 us
  transfers between devices with their start and end apart: 10, of which 6 were waited for; matrix products, arithmetic and copies ran while one was open for 4% of the time, Pallas kernels for 37%

profile of v6, /device:TPU:1, one launch (start us, length us, event | category | flops | bytes accessed | tf_op | source)
XLA Modules:
  0.0 121.6 jit_solution(16445834289868653979)
XLA Ops:
  0.6 0.9 pad_maximum_fusion
  1.5 1.2 broadcast_in_dim.31
  2.7 8.6 %all-to-all-start = ((bf16[16,16,2560]{2,1,0:T(8,128)(2,1)}), bf16[16,16,2560]{2,1,0:T(8,128)(2,1)}, u32[]{:S(2)}, u32[]{:S(2)}) async-start(bf16[16,16,2560]{2,1,0:T(8,128)(2,1)} %broadcast_in_dim.31), calls=%async_computation | async-start | bytes 2621440 | tf_op jit(solution)/shard_map/all_to_all | solution.py:424
  12.1 5.2 %shard_map.95 = (bf16[1024,512]{1,0:T(8,128)(2,1)S(1)}, s32[1536,128]{1,0:T(8,128)S(1)}, f32[1536,128]{1,0:T(8,128)S(1)}, s32[3,1024]{1,0:T(4,128)S(1)}, f32[2,6...) custom-call(s32[3]{0:T(128)S(1)} %pad_add_fusion.info_ref, bf16[1024,512]{1,0:T(8,128)(2,1)S(1)} %bitcast.12, ...), custom_call_target="tpu_custom_call" | custom-call | tf_op jit(solution)/shard_map/pallas_call | solution.py:428
  17.3 1.0 copy-done.3
  18.2 0.9 copy-done.4
  19.1 0.9 copy-done.6
  20.1 3.4 %gather_fusion = bf16[32,512]{1,0:T(8,128)(2,1)S(1)} fusion(bf16[4096,512]{1,0:T(8,128)(2,1)} %param.13, s32[1024]{0:T(1024)S(1)} %pad_clamp_fusion), kind=kCustom, calls=%fused_computation | custom fusion | bytes 65664 | tf_op jit(solution)/shard_map/gather | solution.py:444
  23.7 1.0 collective-permute-start
  25.0 1.0 concatenate.7.follow_hbm
  26.0 1.1 shard_map.96
  27.1 2.3 %all-to-all-done = bf16[16,16,2560]{2,1,0:T(8,128)(2,1)} async-done(((bf16[16,16,2560]{2,1,0:T(8,128)(2,1)}), bf16[16,16,2560]{2,1,0:T(8,128)(2,1)}, u32[]{:S(2)}, u32[]{:S(2)}) %all-to-all-start) | async-done | bytes 1310752 | tf_op jit(solution)/shard_map/all_to_all | solution.py:424
  29.5 3.7 %collective-permute-start.1 = (bf16[256,2560]{1,0:T(8,128)(2,1)}, bf16[256,2560]{1,0:T(8,128)(2,1)}, u32[]{:S(2)}, u32[]{:S(2)}) collective-permute-start(bf16[256,2560]{1,0:T(8,128)(2,1)} %bitcast.5.own_hbm), channel_id=1, source_target_pairs={{0,1},{1,0},{2,3},{3,2},{4,5},{5,4},{6,7},{7,6},{8,9},{9,8},{10,11... | collective-permute-start | bytes 3932168 | tf_op jit(solution)/shard_map/ppermute | solution.py:409
  33.1 6.9 %all-to-all-start.1 = ((bf16[64,56,128]{2,1,0:T(8,128)(2,1)}), bf16[64,56,128]{2,1,0:T(8,128)(2,1)S(1)}, u32[]{:S(2)}, u32[]{:S(2)}) async-start(bf16[64,56,128]{2,1,0:T(8,128)(2,1)} %shard_map.96), calls=%async_computation.1 | async-start | bytes 1835008 | tf_op jit(solution)/shard_map/all_to_all | solution.py:413
  40.1 14.2 %shard_map.97 = (f32[1,1024]{1,0:T(1,128)S(1)}, bf16[1024,512]{1,0:T(8,128)(2,1)S(1)}, bf16[1536,512]{1,0:T(8,128)(2,1)}) custom-call(s32[3]{0:T(128)S(1)} %pad_add_fusion.info_ref, s32[3,1024]{1,0:T(4,128)S(1)} %get-tuple-element.32.slot_ref, bf16[256,2560]{1,0:T(8,128)(2,1)} %bitcast.5.own_hbm, bf16[1024,512]{1,0:T(8,128)(2,1)} %copy-done.3, ...), custom_call_target="tpu_custom_call" | custom-call | tf_op jit(solution)/shard_map/pallas_call | solution.py:456
  54.9 1.6 %all-to-all-done.1.own_ref = bf16[64,56,128]{2,1,0:T(8,128)(2,1)S(1)} async-done(((bf16[64,56,128]{2,1,0:T(8,128)(2,1)}), bf16[64,56,128]{2,1,0:T(8,128)(2,1)S(1)}, u32[]{:S(2)}, u32[]{:S(2)}) %all-to-all-start.1) | async-done | bytes 917536 | tf_op jit(solution)/shard_map/all_to_all | solution.py:413
  56.5 1.7 %collective-permute-start.2 = (bf16[64,56,128]{2,1,0:T(8,128)(2,1)S(1)}, bf16[64,56,128]{2,1,0:T(8,128)(2,1)}, u32[]{:S(2)}, u32[]{:S(2)}) collective-permute-start(bf16[64,56,128]{2,1,0:T(8,128)(2,1)S(1)} %all-to-all-done.1.own_ref), channel_id=1, source_target_pairs={{0,1},{1,0},{2,3},{3,2},{4,5},{5,4},{6,7},{7,6},{8,9},{9,8},{10,11... | collective-permute-start | bytes 2752520 | tf_op jit(solution)/shard_map/ppermute | solution.py:409
  58.2 6.9 %all-to-all-start.2 = ((bf16[64,24,512]{2,1,0:T(8,128)(2,1)}), bf16[64,24,512]{2,1,0:T(8,128)(2,1)S(1)}, u32[]{:S(2)}, u32[]{:S(2)}) async-start(bf16[64,24,512]{2,1,0:T(8,128)(2,1)} %bitcast.18), calls=%async_computation.2 | async-start | bytes 3145728 | tf_op jit(solution)/shard_map/all_to_all | solution.py:413
  65.1 1.5 %shard_map.98 = (bf16[1536,256]{1,0:T(8,128)(2,1)S(1)}, bf16[1536,256]{1,0:T(8,128)(2,1)S(1)}, s32[2,64,128]{2,1,0:T(8,128)S(1)}) custom-call(bf16[64,56,128]{2,1,0:T(8,128)(2,1)S(1)} %all-to-all-done.1.own_ref, bf16[64,56,128]{2,1,0:T(8,128)(2,1)} %collective-permute-done.2.other_ref), custom_call_target="tpu_custom_call" | custom-call | tf_op jit(solution)/shard_map/pallas_call | solution.py:484
  67.2 7.4 %shard_map.99 = (f32[1,1024]{1,0:T(1,128)}, f32[1536,256]{1,0:T(8,128)S(1)}, bf16[1536,256]{1,0:T(8,128)(2,1)S(1)}, f32[3,64,128]{2,1,0:T(8,128)S(1)}) custom-call(s32[3]{0:T(128)S(1)} %copy-done.15, bf16[1024,512]{1,0:T(8,128)(2,1)S(1)} %get-tuple-element.39.hidden_ref, bf16[1536,256]{1,0:T(8,128)(2,1)S(1)} %get-tuple-element.43.own_ref, ...), custom_call_target="tpu_custom_call" | custom-call | tf_op jit(solution)/shard_map/pallas_call | solution.py:497
  74.9 2.0 %collective-permute-done.3.other_ref = bf16[1536,256]{1,0:T(8,128)(2,1)S(1)} collective-permute-done((bf16[1536,256]{1,0:T(8,128)(2,1)S(1)}, bf16[1536,256]{1,0:T(8,128)(2,1)S(1)}, u32[]{:S(2)}, u32[]{:S(2)}) %collective-permute-start.3) | collective-permute-done | bytes 786464 | tf_op jit(solution)/shard_map/ppermute | solution.py:409
  76.9 1.2 shard_map.101
  78.1 10.4 %all-to-all-done.2 = bf16[64,24,512]{2,1,0:T(8,128)(2,1)S(1)} async-done(((bf16[64,24,512]{2,1,0:T(8,128)(2,1)}), bf16[64,24,512]{2,1,0:T(8,128)(2,1)S(1)}, u32[]{:S(2)}, u32[]{:S(2)}) %all-to-all-start.2) | async-done | bytes 1572896 | tf_op jit(solution)/shard_map/all_to_all | solution.py:413
  88.5 1.6 %collective-permute-start.4 = (bf16[1536,512]{1,0:T(8,128)(2,1)S(1)}, bf16[1536,512]{1,0:T(8,128)(2,1)}, u32[]{:S(2)}, u32[]{:S(2)}) collective-permute-start(bf16[1536,512]{1,0:T(8,128)(2,1)S(1)} %bitcast.13), channel_id=1, source_target_pairs={{0,1},{1,0},{2,3},{3,2},{4,5},{5,4},{6,7},{7,6},{8,9},{9,8},{10,11... | collective-permute-start | bytes 4718600 | tf_op jit(solution)/shard_map/ppermute | solution.py:409
  90.2 5.1 %all-to-all-start.3 = ((bf16[64,56,128]{2,1,0:T(8,128)(2,1)}), bf16[64,56,128]{2,1,0:T(8,128)(2,1)S(1)}, u32[]{:S(2)}, u32[]{:S(2)}) async-start(bf16[64,56,128]{2,1,0:T(8,128)(2,1)} %shard_map.101), calls=%async_computation.3 | async-start | bytes 1835008 | tf_op jit(solution)/shard_map/all_to_all | solution.py:413
  95.4 6.1 %shard_map.100 = (s32[1,3072]{1,0:T(1,128)S(1)}, s32[16,128]{1,0:T(8,128)S(1)}, s32[32]{0:T(128)S(1)}, s32[64]{0:T(128)S(1)}) custom-call(s32[3]{0:T(128)S(1)} %copy-done.16, s32[1,3072]{1,0:T(1,128)S(1)} %reshape.19.row_ref, s32[32,128]{1,0:T(8,128)S(1)} %get-tuple-element.34.neg_ref), custom_call_target="tpu_custom_call" | custom-call | tf_op jit(solution)/shard_map/pallas_call | solution.py:524
  101.6 1.4 %copy-done.2 = bf16[64,24,512]{2,1,0:T(8,128)(2,1)S(1)} copy-done((bf16[64,24,512]{2,1,0:T(8,128)(2,1)S(1)}, bf16[64,24,512]{2,1,0:T(8,128)(2,1)}, u32[]{:S(2)}) %copy-start.2) | copy-done | bytes 1572888
  103.0 8.1 %shard_map.102.rows_ref = bf16[2048,512]{1,0:T(8,128)(2,1)S(1)} custom-call(s32[1,3072]{1,0:T(1,128)S(1)} %get-tuple-element.57.at_ref, bf16[1536,512]{1,0:T(8,128)(2,1)S(1)} %bitcast.14, bf16[1536,512]{1,0:T(8,128)(2,1)} %collective-permute-done.4.other_ref), custom_call_target="tpu_custom_call" | custom-call | tf_op jit(solution)/shard_map/pallas_call | solution.py:537
  111.0 0.8 all-to-all-done.3.got_ref
  112.4 2.0 %collective-permute-start.5 = (f32[32,256]{1,0:T(8,128)S(1)}, f32[32,256]{1,0:T(8,128)S(1)}, u32[]{:S(2)}, u32[]{:S(2)}) collective-permute-start(f32[32,256]{1,0:T(8,128)S(1)} %shard_map.103.small_ref), channel_id=1, source_target_pairs={{0,1},{1,0},{2,3},{3,2},{4,5},{5,4},{6,7},{7,6},{8,9},{9,8},{10,11... | collective-permute-start | bytes 98312 | tf_op jit(solution)/shard_map/ppermute | solution.py:409
  114.5 0.9 collective-permute-done.5.small_other_ref
  115.3 6.1 %shard_map.104 = bf16[4096,512]{1,0:T(8,128)(2,1)} custom-call(s32[32]{0:T(128)S(1)} %get-tuple-element.50.start_ref, s32[64]{0:T(128)S(1)} %get-tuple-element.51.neg_at_ref, f32[32,256]{1,0:T(8,128)S(1)} %shard_map.103.small_ref, f32[32,256]{1,0:T(8,128)S(1)} %collective-permute-done.5.small_other_ref, s32[1,3072]{1,0:T(1,128)S(1)} %get-tuple-element.57.at_ref, ...), custom_call_target="tpu_custom_call" | custom-call | tf_op jit(solution)/shard_map/pallas_call | solution.py:545
  (52 shorter events, 2.8 us)
Async XLA Ops:
  2.7 9.4 %copy-start = (bf16[1,1024,512]{2,1,0:T(8,128)(2,1)S(1)}, bf16[1,1024,512]{2,1,0:T(8,128)(2,1)}, u32[]{:S(2)}) copy-start(bf16[1,1024,512]{2,1,0:T(8,128)(2,1)} %param.8) | copy-start | bytes 3145732
  2.7 9.4 %copy-start.12 = (s32[1,1024]{1,0:T(1,128)S(1)}, s32[1,1024]{1,0:T(1,128)}, u32[]{:S(2)}) copy-start(s32[1,1024]{1,0:T(1,128)} %targets_ref.3) | copy-start | bytes 12292
  2.7 9.4 %copy-start.17 = (s32[1024]{0:T(1024)S(1)}, s32[1024]{0:T(1024)}, u32[]{:S(2)}) copy-start(s32[1024]{0:T(1024)} %param.11) | copy-start | bytes 12292
  2.7 9.4 %copy-start.18 = (s32[1024]{0:T(1024)S(1)}, s32[1024]{0:T(1024)}, u32[]{:S(2)}) copy-start(s32[1024]{0:T(1024)} %param.12) | copy-start | bytes 12292
  2.7 26.8 %all-to-all-start = ((bf16[16,16,2560]{2,1,0:T(8,128)(2,1)}), bf16[16,16,2560]{2,1,0:T(8,128)(2,1)}, u32[]{:S(2)}, u32[]{:S(2)}) async-start(bf16[16,16,2560]{2,1,0:T(8,128)(2,1)} %broadcast_in_dim.31), calls=%async_computation | async-start | bytes 2621440 | tf_op jit(solution)/shard_map/all_to_all | solution.py:424
  12.0 28.0 %copy-start.14 = (s32[3]{0:T(128)}, s32[3]{0:T(128)S(1)}, u32[]{:S(2)}) copy-start(s32[3]{0:T(128)S(1)} %pad_add_fusion.info_ref) | copy-start | bytes 40
  17.2 1.0 copy-start.3
  18.2 0.9 copy-start.4
  19.1 0.9 copy-start.6
  20.0 20.1 %copy-start.8 = (s32[3,1024]{1,0:T(4,128)}, s32[3,1024]{1,0:T(4,128)S(1)}, u32[]{:S(2)}) copy-start(s32[3,1024]{1,0:T(4,128)S(1)} %get-tuple-element.32.slot_ref) | copy-start | bytes 36868
  23.7 2.3 %collective-permute-start = (bf16[32,256]{1,0:T(8,128)(2,1)S(1)}, bf16[32,256]{1,0:T(8,128)(2,1)S(1)}, u32[]{:S(2)}, u32[]{:S(2)}) collective-permute-start(bf16[32,256]{1,0:T(8,128)(2,1)S(1)} %get-tuple-element.62), channel_id=1, source_target_pairs={{0,1},{1,0},{2,3},{3,2},{4,5},{5,4},{6,7},{7,6},{8,9},{9,8},{10,11... | collective-permute-start | bytes 49160 | tf_op jit(solution)/shard_map/ppermute | solution.py:409
  29.5 10.6 %collective-permute-start.1 = (bf16[256,2560]{1,0:T(8,128)(2,1)}, bf16[256,2560]{1,0:T(8,128)(2,1)}, u32[]{:S(2)}, u32[]{:S(2)}) collective-permute-start(bf16[256,2560]{1,0:T(8,128)(2,1)} %bitcast.5.own_hbm), channel_id=1, source_target_pairs={{0,1},{1,0},{2,3},{3,2},{4,5},{5,4},{6,7},{7,6},{8,9},{9,8},{10,11... | collective-permute-start | bytes 3932168 | tf_op jit(solution)/shard_map/ppermute | solution.py:409
  33.1 23.4 %all-to-all-start.1 = ((bf16[64,56,128]{2,1,0:T(8,128)(2,1)}), bf16[64,56,128]{2,1,0:T(8,128)(2,1)S(1)}, u32[]{:S(2)}, u32[]{:S(2)}) async-start(bf16[64,56,128]{2,1,0:T(8,128)(2,1)} %shard_map.96), calls=%async_computation.1 | async-start | bytes 1835008 | tf_op jit(solution)/shard_map/all_to_all | solution.py:413
  54.3 0.6 copy-start.19
  56.5 8.6 %collective-permute-start.2 = (bf16[64,56,128]{2,1,0:T(8,128)(2,1)S(1)}, bf16[64,56,128]{2,1,0:T(8,128)(2,1)}, u32[]{:S(2)}, u32[]{:S(2)}) collective-permute-start(bf16[64,56,128]{2,1,0:T(8,128)(2,1)S(1)} %all-to-all-done.1.own_ref), channel_id=1, source_target_pairs={{0,1},{1,0},{2,3},{3,2},{4,5},{5,4},{6,7},{7,6},{8,9},{9,8},{10,11... | collective-permute-start | bytes 2752520 | tf_op jit(solution)/shard_map/ppermute | solution.py:409
  58.2 30.4 %all-to-all-start.2 = ((bf16[64,24,512]{2,1,0:T(8,128)(2,1)}), bf16[64,24,512]{2,1,0:T(8,128)(2,1)S(1)}, u32[]{:S(2)}, u32[]{:S(2)}) async-start(bf16[64,24,512]{2,1,0:T(8,128)(2,1)} %bitcast.18), calls=%async_computation.2 | async-start | bytes 3145728 | tf_op jit(solution)/shard_map/all_to_all | solution.py:413
  65.1 2.1 %copy-start.5 = (s32[1536,128]{1,0:T(8,128)S(1)}, s32[1536,128]{1,0:T(8,128)}, u32[]{:S(2)}) copy-start(s32[1536,128]{1,0:T(8,128)} %copy-done.4) | copy-start | bytes 2359300
  65.1 2.1 %copy-start.7 = (f32[1536,128]{1,0:T(8,128)S(1)}, f32[1536,128]{1,0:T(8,128)}, u32[]{:S(2)}) copy-start(f32[1536,128]{1,0:T(8,128)} %copy-done.6) | copy-start | bytes 2359300
  65.1 2.1 %copy-start.9 = (s32[3,1024]{1,0:T(4,128)S(1)}, s32[3,1024]{1,0:T(4,128)}, u32[]{:S(2)}) copy-start(s32[3,1024]{1,0:T(4,128)} %copy-done.8) | copy-start | bytes 36868
  65.1 2.1 %copy-start.13 = (s32[1,1024]{1,0:T(1,128)S(1)}, s32[1,1024]{1,0:T(1,128)}, u32[]{:S(2)}) copy-start(s32[1,1024]{1,0:T(1,128)} %targets_ref.3) | copy-start | bytes 12292
  65.1 2.1 %copy-start.15 = (s32[3]{0:T(128)S(1)}, s32[3]{0:T(128)}, u32[]{:S(2)}) copy-start(s32[3]{0:T(128)} %copy-done.14) | copy-start | bytes 40
  65.1 2.1 %copy-start.20 = (f32[1,1024]{1,0:T(1,128)S(1)}, f32[1,1024]{1,0:T(1,128)}, u32[]{:S(2)}) copy-start(f32[1,1024]{1,0:T(1,128)} %copy-done.19) | copy-start | bytes 12292
  66.6 0.6 copy-start.10
  74.6 2.3 %collective-permute-start.3 = (bf16[1536,256]{1,0:T(8,128)(2,1)S(1)}, bf16[1536,256]{1,0:T(8,128)(2,1)S(1)}, u32[]{:S(2)}, u32[]{:S(2)}) collective-permute-start(bf16[1536,256]{1,0:T(8,128)(2,1)S(1)} %get-tuple-element.54), channel_id=1, source_target_pairs={{0,1},{1,0},{2,3},{3,2},{4,5},{5,4},{6,7},{7,6},{8,9},{9,8},{10,11... | collective-permute-start | bytes 2359304 | tf_op jit(solution)/shard_map/ppermute | solution.py:409
  78.1 17.2 %copy-start.11 = (s32[2,64,128]{2,1,0:T(8,128)S(1)}, s32[2,64,128]{2,1,0:T(8,128)}, u32[]{:S(2)}) copy-start(s32[2,64,128]{2,1,0:T(8,128)} %copy-done.10) | copy-start | bytes 196612
  78.1 17.3 %copy-start.16 = (s32[3]{0:T(128)S(1)}, s32[3]{0:T(128)}, u32[]{:S(2)}) copy-start(s32[3]{0:T(128)} %copy-done.14) | copy-start | bytes 40
  88.5 13.0 %copy-start.1 = (bf16[64,24,512]{2,1,0:T(8,128)(2,1)}, bf16[64,24,512]{2,1,0:T(8,128)(2,1)S(1)}, u32[]{:S(2)}) copy-start(bf16[64,24,512]{2,1,0:T(8,128)(2,1)S(1)} %all-to-all-done.2) | copy-start | bytes 4718596
  88.5 13.0 %collective-permute-start.4 = (bf16[1536,512]{1,0:T(8,128)(2,1)S(1)}, bf16[1536,512]{1,0:T(8,128)(2,1)}, u32[]{:S(2)}, u32[]{:S(2)}) collective-permute-start(bf16[1536,512]{1,0:T(8,128)(2,1)S(1)} %bitcast.13), channel_id=1, source_target_pairs={{0,1},{1,0},{2,3},{3,2},{4,5},{5,4},{6,7},{7,6},{8,9},{9,8},{10,11... | collective-permute-start | bytes 4718600 | tf_op jit(solution)/shard_map/ppermute | solution.py:409
  90.2 21.7 %all-to-all-start.3 = ((bf16[64,56,128]{2,1,0:T(8,128)(2,1)}), bf16[64,56,128]{2,1,0:T(8,128)(2,1)S(1)}, u32[]{:S(2)}, u32[]{:S(2)}) async-start(bf16[64,56,128]{2,1,0:T(8,128)(2,1)} %shard_map.101), calls=%async_computation.3 | async-start | bytes 1835008 | tf_op jit(solution)/shard_map/all_to_all | solution.py:413
  101.6 1.4 %copy-start.2 = (bf16[64,24,512]{2,1,0:T(8,128)(2,1)S(1)}, bf16[64,24,512]{2,1,0:T(8,128)(2,1)}, u32[]{:S(2)}) copy-start(bf16[64,24,512]{2,1,0:T(8,128)(2,1)} %copy-done.1) | copy-start | bytes 4718596
  112.4 2.9 %collective-permute-start.5 = (f32[32,256]{1,0:T(8,128)S(1)}, f32[32,256]{1,0:T(8,128)S(1)}, u32[]{:S(2)}, u32[]{:S(2)}) collective-permute-start(f32[32,256]{1,0:T(8,128)S(1)} %shard_map.103.small_ref), channel_id=1, source_target_pairs={{0,1},{1,0},{2,3},{3,2},{4,5},{5,4},{6,7},{7,6},{8,9},{9,8},{10,11... | collective-permute-start | bytes 98312 | tf_op jit(solution)/shard_map/ppermute | solution.py:409

commit v7 on v6

--- a/solution.py
+++ b/solution.py
@@ -340,9 +340,12 @@
 
 def collect_kernel(got_ref, small_ref):
     total = jnp.zeros((2 * CSLOTS, 128), F32)
+    parts = [[], [], []]
     for g in range(NCHIPS // GROUP):
         block = got_ref[g * GROUP : (g + 1) * GROUP].astype(F32)
         total = total + jnp.sum(block[:, : 2 * CSLOTS], axis=0)
+        for p in range(3):
+            parts[p].append(block[:, 2 * CSLOTS + p])
     small_ref[:CSLOTS, :] = jnp.concatenate([total[:CSLOTS], total[CSLOTS:]], axis=1)
     k = iota((1, SLOTS), 1)
     chip = ((k.astype(F32) + 0.5) * (1.0 / CSLOTS)).astype(I32)
@@ -350,7 +353,7 @@
     mine = iota((NCHIPS, SLOTS), 0) == chip
     row = jnp.zeros((1, SLOTS), F32)
     for p in range(3):
-        piece = got_ref[:, 2 * CSLOTS + p, :]
+        piece = jnp.concatenate(parts[p], axis=0).astype(BF)
         row = row + jnp.sum(jnp.where(mine, dot(piece, spread), 0.0), axis=0, keepdims=True)
     for r in range(SLOTS // B):
         small_ref[CSLOTS + r : CSLOTS + r + 1, :] = row[:, r * B : (r + 1) * B]

time: 122 us -> 122 us (level)
  no operation moved by 1% of the time
where the time goes in v7:
time: 122 us
  Pallas kernels  51.2 us (42%)
  starting transfers between devices  37.9 us (31%)
  waiting for transfers between devices  18.1 us (15%)
  local copies, waits for them, and re-layouts  11.4 us (9%)
  between operations  1.79 us (1%)
  other arithmetic  1.25 us (1%)
    all_to_all x3, starting transfers between devices, chips_a2a(): return lax.all_to_all(v, CHIPS, split_axis=0, concat_axis=0, tiled=True)  18.9 us
    pallas_call x1, Pallas kernels, per_device(): pl.pallas_call(layer_kernel, out_shape=(jax.ShapeDtypeStruct((1, 1024), F...  14.2 us
    all_to_all x3, waiting for transfers between devices, chips_a2a(): return lax.all_to_all(v, CHIPS, split_axis=0, concat_axis=0, tiled=True)  12.9 us
    ppermute x6, starting transfers between devices, swap(): return lax.ppermute(v, 'c', SWAP)  10.4 us
    all_to_all x1, starting transfers between devices, per_device(): lax.all_to_all(jnp.broadcast_to(w_mine[None], (16,) + w_mine.shape), ('x'...  8.62 us
    pallas_call x1, Pallas kernels, per_device(): call(sort_kernel, jax.ShapeDtypeStruct((PLACES, width), BF), [VMEM] * 3,...  8.05 us
    pallas_call x1, Pallas kernels, per_device(): call(loss_kernel, (jax.ShapeDtypeStruct((1, 1024), F32), jax.ShapeDtypeSt...  7.39 us
    pallas_call x1, Pallas kernels, per_device(): pl.pallas_call(rank_kernel, out_shape=(jax.ShapeDtypeStruct((1, 2 * SLOTS...  6.14 us
  transfers between devices with their start and end apart: 10, of which 6 were waited for; matrix products, arithmetic and copies ran while one was open for 4% of the time, Pallas kernels for 37%

profile of v7, /device:TPU:1, one launch (start us, length us, event | category | flops | bytes accessed | tf_op | source)
XLA Modules:
  0.0 121.6 jit_solution(9898316270231598424)
XLA Ops:
  0.6 0.9 pad_maximum_fusion
  1.5 1.2 broadcast_in_dim.31
  2.7 8.6 %all-to-all-start = ((bf16[16,16,2560]{2,1,0:T(8,128)(2,1)}), bf16[16,16,2560]{2,1,0:T(8,128)(2,1)}, u32[]{:S(2)}, u32[]{:S(2)}) async-start(bf16[16,16,2560]{2,1,0:T(8,128)(2,1)} %broadcast_in_dim.31), calls=%async_computation | async-start | bytes 2621440 | tf_op jit(solution)/shard_map/all_to_all | solution.py:427
  12.1 5.2 %shard_map.95 = (bf16[1024,512]{1,0:T(8,128)(2,1)S(1)}, s32[1536,128]{1,0:T(8,128)S(1)}, f32[1536,128]{1,0:T(8,128)S(1)}, s32[3,1024]{1,0:T(4,128)S(1)}, f32[2,6...) custom-call(s32[3]{0:T(128)S(1)} %pad_add_fusion.info_ref, bf16[1024,512]{1,0:T(8,128)(2,1)S(1)} %bitcast.12, ...), custom_call_target="tpu_custom_call" | custom-call | tf_op jit(solution)/shard_map/pallas_call | solution.py:431
  17.3 1.0 copy-done.3
  18.2 0.9 copy-done.4
  19.1 0.9 copy-done.6
  20.1 3.4 %gather_fusion = bf16[32,512]{1,0:T(8,128)(2,1)S(1)} fusion(bf16[4096,512]{1,0:T(8,128)(2,1)} %param.13, s32[1024]{0:T(1024)S(1)} %pad_clamp_fusion), kind=kCustom, calls=%fused_computation | custom fusion | bytes 65664 | tf_op jit(solution)/shard_map/gather | solution.py:447
  23.7 1.0 collective-permute-start
  25.0 1.0 concatenate.7.follow_hbm
  26.0 1.1 shard_map.96
  27.1 2.3 %all-to-all-done = bf16[16,16,2560]{2,1,0:T(8,128)(2,1)} async-done(((bf16[16,16,2560]{2,1,0:T(8,128)(2,1)}), bf16[16,16,2560]{2,1,0:T(8,128)(2,1)}, u32[]{:S(2)}, u32[]{:S(2)}) %all-to-all-start) | async-done | bytes 1310752 | tf_op jit(solution)/shard_map/all_to_all | solution.py:427
  29.5 3.7 %collective-permute-start.1 = (bf16[256,2560]{1,0:T(8,128)(2,1)}, bf16[256,2560]{1,0:T(8,128)(2,1)}, u32[]{:S(2)}, u32[]{:S(2)}) collective-permute-start(bf16[256,2560]{1,0:T(8,128)(2,1)} %bitcast.5.own_hbm), channel_id=1, source_target_pairs={{0,1},{1,0},{2,3},{3,2},{4,5},{5,4},{6,7},{7,6},{8,9},{9,8},{10,11... | collective-permute-start | bytes 3932168 | tf_op jit(solution)/shard_map/ppermute | solution.py:412
  33.1 6.9 %all-to-all-start.1 = ((bf16[64,56,128]{2,1,0:T(8,128)(2,1)}), bf16[64,56,128]{2,1,0:T(8,128)(2,1)S(1)}, u32[]{:S(2)}, u32[]{:S(2)}) async-start(bf16[64,56,128]{2,1,0:T(8,128)(2,1)} %shard_map.96), calls=%async_computation.1 | async-start | bytes 1835008 | tf_op jit(solution)/shard_map/all_to_all | solution.py:416
  40.1 14.2 %shard_map.97 = (f32[1,1024]{1,0:T(1,128)S(1)}, bf16[1024,512]{1,0:T(8,128)(2,1)S(1)}, bf16[1536,512]{1,0:T(8,128)(2,1)}) custom-call(s32[3]{0:T(128)S(1)} %pad_add_fusion.info_ref, s32[3,1024]{1,0:T(4,128)S(1)} %get-tuple-element.32.slot_ref, bf16[256,2560]{1,0:T(8,128)(2,1)} %bitcast.5.own_hbm, bf16[1024,512]{1,0:T(8,128)(2,1)} %copy-done.3, ...), custom_call_target="tpu_custom_call" | custom-call | tf_op jit(solution)/shard_map/pallas_call | solution.py:459
  54.9 1.6 %all-to-all-done.1.own_ref = bf16[64,56,128]{2,1,0:T(8,128)(2,1)S(1)} async-done(((bf16[64,56,128]{2,1,0:T(8,128)(2,1)}), bf16[64,56,128]{2,1,0:T(8,128)(2,1)S(1)}, u32[]{:S(2)}, u32[]{:S(2)}) %all-to-all-start.1) | async-done | bytes 917536 | tf_op jit(solution)/shard_map/all_to_all | solution.py:416
  56.5 1.7 %collective-permute-start.2 = (bf16[64,56,128]{2,1,0:T(8,128)(2,1)S(1)}, bf16[64,56,128]{2,1,0:T(8,128)(2,1)}, u32[]{:S(2)}, u32[]{:S(2)}) collective-permute-start(bf16[64,56,128]{2,1,0:T(8,128)(2,1)S(1)} %all-to-all-done.1.own_ref), channel_id=1, source_target_pairs={{0,1},{1,0},{2,3},{3,2},{4,5},{5,4},{6,7},{7,6},{8,9},{9,8},{10,11... | collective-permute-start | bytes 2752520 | tf_op jit(solution)/shard_map/ppermute | solution.py:412
  58.2 6.9 %all-to-all-start.2 = ((bf16[64,24,512]{2,1,0:T(8,128)(2,1)}), bf16[64,24,512]{2,1,0:T(8,128)(2,1)S(1)}, u32[]{:S(2)}, u32[]{:S(2)}) async-start(bf16[64,24,512]{2,1,0:T(8,128)(2,1)} %bitcast.18), calls=%async_computation.2 | async-start | bytes 3145728 | tf_op jit(solution)/shard_map/all_to_all | solution.py:416
  65.1 1.5 %shard_map.98 = (bf16[1536,256]{1,0:T(8,128)(2,1)S(1)}, bf16[1536,256]{1,0:T(8,128)(2,1)S(1)}, s32[2,64,128]{2,1,0:T(8,128)S(1)}) custom-call(bf16[64,56,128]{2,1,0:T(8,128)(2,1)S(1)} %all-to-all-done.1.own_ref, bf16[64,56,128]{2,1,0:T(8,128)(2,1)} %collective-permute-done.2.other_ref), custom_call_target="tpu_custom_call" | custom-call | tf_op jit(solution)/shard_map/pallas_call | solution.py:487
  67.2 7.4 %shard_map.99 = (f32[1,1024]{1,0:T(1,128)}, f32[1536,256]{1,0:T(8,128)S(1)}, bf16[1536,256]{1,0:T(8,128)(2,1)S(1)}, f32[3,64,128]{2,1,0:T(8,128)S(1)}) custom-call(s32[3]{0:T(128)S(1)} %copy-done.15, bf16[1024,512]{1,0:T(8,128)(2,1)S(1)} %get-tuple-element.39.hidden_ref, bf16[1536,256]{1,0:T(8,128)(2,1)S(1)} %get-tuple-element.43.own_ref, ...), custom_call_target="tpu_custom_call" | custom-call | tf_op jit(solution)/shard_map/pallas_call | solution.py:500
  74.9 2.0 %collective-permute-done.3.other_ref = bf16[1536,256]{1,0:T(8,128)(2,1)S(1)} collective-permute-done((bf16[1536,256]{1,0:T(8,128)(2,1)S(1)}, bf16[1536,256]{1,0:T(8,128)(2,1)S(1)}, u32[]{:S(2)}, u32[]{:S(2)}) %collective-permute-start.3) | collective-permute-done | bytes 786464 | tf_op jit(solution)/shard_map/ppermute | solution.py:412
  76.9 1.2 shard_map.101
  78.1 10.4 %all-to-all-done.2 = bf16[64,24,512]{2,1,0:T(8,128)(2,1)S(1)} async-done(((bf16[64,24,512]{2,1,0:T(8,128)(2,1)}), bf16[64,24,512]{2,1,0:T(8,128)(2,1)S(1)}, u32[]{:S(2)}, u32[]{:S(2)}) %all-to-all-start.2) | async-done | bytes 1572896 | tf_op jit(solution)/shard_map/all_to_all | solution.py:416
  88.5 1.6 %collective-permute-start.4 = (bf16[1536,512]{1,0:T(8,128)(2,1)S(1)}, bf16[1536,512]{1,0:T(8,128)(2,1)}, u32[]{:S(2)}, u32[]{:S(2)}) collective-permute-start(bf16[1536,512]{1,0:T(8,128)(2,1)S(1)} %bitcast.13), channel_id=1, source_target_pairs={{0,1},{1,0},{2,3},{3,2},{4,5},{5,4},{6,7},{7,6},{8,9},{9,8},{10,11... | collective-permute-start | bytes 4718600 | tf_op jit(solution)/shard_map/ppermute | solution.py:412
  90.2 5.1 %all-to-all-start.3 = ((bf16[64,56,128]{2,1,0:T(8,128)(2,1)}), bf16[64,56,128]{2,1,0:T(8,128)(2,1)S(1)}, u32[]{:S(2)}, u32[]{:S(2)}) async-start(bf16[64,56,128]{2,1,0:T(8,128)(2,1)} %shard_map.101), calls=%async_computation.3 | async-start | bytes 1835008 | tf_op jit(solution)/shard_map/all_to_all | solution.py:416
  95.4 6.1 %shard_map.100 = (s32[1,3072]{1,0:T(1,128)S(1)}, s32[16,128]{1,0:T(8,128)S(1)}, s32[32]{0:T(128)S(1)}, s32[64]{0:T(128)S(1)}) custom-call(s32[3]{0:T(128)S(1)} %copy-done.16, s32[1,3072]{1,0:T(1,128)S(1)} %reshape.19.row_ref, s32[32,128]{1,0:T(8,128)S(1)} %get-tuple-element.34.neg_ref), custom_call_target="tpu_custom_call" | custom-call | tf_op jit(solution)/shard_map/pallas_call | solution.py:527
  101.6 1.4 %copy-done.2 = bf16[64,24,512]{2,1,0:T(8,128)(2,1)S(1)} copy-done((bf16[64,24,512]{2,1,0:T(8,128)(2,1)S(1)}, bf16[64,24,512]{2,1,0:T(8,128)(2,1)}, u32[]{:S(2)}) %copy-start.2) | copy-done | bytes 1572888
  103.0 8.1 %shard_map.102.rows_ref = bf16[2048,512]{1,0:T(8,128)(2,1)S(1)} custom-call(s32[1,3072]{1,0:T(1,128)S(1)} %get-tuple-element.57.at_ref, bf16[1536,512]{1,0:T(8,128)(2,1)S(1)} %bitcast.14, bf16[1536,512]{1,0:T(8,128)(2,1)} %collective-permute-done.4.other_ref), custom_call_target="tpu_custom_call" | custom-call | tf_op jit(solution)/shard_map/pallas_call | solution.py:540
  111.0 0.8 all-to-all-done.3.got_ref
  112.4 2.0 %collective-permute-start.5 = (f32[32,256]{1,0:T(8,128)S(1)}, f32[32,256]{1,0:T(8,128)S(1)}, u32[]{:S(2)}, u32[]{:S(2)}) collective-permute-start(f32[32,256]{1,0:T(8,128)S(1)} %shard_map.103.small_ref), channel_id=1, source_target_pairs={{0,1},{1,0},{2,3},{3,2},{4,5},{5,4},{6,7},{7,6},{8,9},{9,8},{10,11... | collective-permute-start | bytes 98312 | tf_op jit(solution)/shard_map/ppermute | solution.py:412
  114.4 0.9 collective-permute-done.5.small_other_ref
  115.3 6.1 %shard_map.104 = bf16[4096,512]{1,0:T(8,128)(2,1)} custom-call(s32[32]{0:T(128)S(1)} %get-tuple-element.50.start_ref, s32[64]{0:T(128)S(1)} %get-tuple-element.51.neg_at_ref, f32[32,256]{1,0:T(8,128)S(1)} %shard_map.103.small_ref, f32[32,256]{1,0:T(8,128)S(1)} %collective-permute-done.5.small_other_ref, s32[1,3072]{1,0:T(1,128)S(1)} %get-tuple-element.57.at_ref, ...), custom_call_target="tpu_custom_call" | custom-call | tf_op jit(solution)/shard_map/pallas_call | solution.py:548
  (52 shorter events, 2.8 us)
Async XLA Ops:
  2.7 9.4 %copy-start = (bf16[1,1024,512]{2,1,0:T(8,128)(2,1)S(1)}, bf16[1,1024,512]{2,1,0:T(8,128)(2,1)}, u32[]{:S(2)}) copy-start(bf16[1,1024,512]{2,1,0:T(8,128)(2,1)} %param.8) | copy-start | bytes 3145732
  2.7 9.4 %copy-start.12 = (s32[1,1024]{1,0:T(1,128)S(1)}, s32[1,1024]{1,0:T(1,128)}, u32[]{:S(2)}) copy-start(s32[1,1024]{1,0:T(1,128)} %targets_ref.3) | copy-start | bytes 12292
  2.7 9.4 %copy-start.17 = (s32[1024]{0:T(1024)S(1)}, s32[1024]{0:T(1024)}, u32[]{:S(2)}) copy-start(s32[1024]{0:T(1024)} %param.11) | copy-start | bytes 12292
  2.7 9.4 %copy-start.18 = (s32[1024]{0:T(1024)S(1)}, s32[1024]{0:T(1024)}, u32[]{:S(2)}) copy-start(s32[1024]{0:T(1024)} %param.12) | copy-start | bytes 12292
  2.7 26.8 %all-to-all-start = ((bf16[16,16,2560]{2,1,0:T(8,128)(2,1)}), bf16[16,16,2560]{2,1,0:T(8,128)(2,1)}, u32[]{:S(2)}, u32[]{:S(2)}) async-start(bf16[16,16,2560]{2,1,0:T(8,128)(2,1)} %broadcast_in_dim.31), calls=%async_computation | async-start | bytes 2621440 | tf_op jit(solution)/shard_map/all_to_all | solution.py:427
  12.0 28.0 %copy-start.14 = (s32[3]{0:T(128)}, s32[3]{0:T(128)S(1)}, u32[]{:S(2)}) copy-start(s32[3]{0:T(128)S(1)} %pad_add_fusion.info_ref) | copy-start | bytes 40
  17.2 1.0 copy-start.3
  18.2 0.9 copy-start.4
  19.1 0.9 copy-start.6
  20.0 20.1 %copy-start.8 = (s32[3,1024]{1,0:T(4,128)}, s32[3,1024]{1,0:T(4,128)S(1)}, u32[]{:S(2)}) copy-start(s32[3,1024]{1,0:T(4,128)S(1)} %get-tuple-element.32.slot_ref) | copy-start | bytes 36868
  23.7 2.3 %collective-permute-start = (bf16[32,256]{1,0:T(8,128)(2,1)S(1)}, bf16[32,256]{1,0:T(8,128)(2,1)S(1)}, u32[]{:S(2)}, u32[]{:S(2)}) collective-permute-start(bf16[32,256]{1,0:T(8,128)(2,1)S(1)} %get-tuple-element.62), channel_id=1, source_target_pairs={{0,1},{1,0},{2,3},{3,2},{4,5},{5,4},{6,7},{7,6},{8,9},{9,8},{10,11... | collective-permute-start | bytes 49160 | tf_op jit(solution)/shard_map/ppermute | solution.py:412
  29.5 10.6 %collective-permute-start.1 = (bf16[256,2560]{1,0:T(8,128)(2,1)}, bf16[256,2560]{1,0:T(8,128)(2,1)}, u32[]{:S(2)}, u32[]{:S(2)}) collective-permute-start(bf16[256,2560]{1,0:T(8,128)(2,1)} %bitcast.5.own_hbm), channel_id=1, source_target_pairs={{0,1},{1,0},{2,3},{3,2},{4,5},{5,4},{6,7},{7,6},{8,9},{9,8},{10,11... | collective-permute-start | bytes 3932168 | tf_op jit(solution)/shard_map/ppermute | solution.py:412
  33.1 23.4 %all-to-all-start.1 = ((bf16[64,56,128]{2,1,0:T(8,128)(2,1)}), bf16[64,56,128]{2,1,0:T(8,128)(2,1)S(1)}, u32[]{:S(2)}, u32[]{:S(2)}) async-start(bf16[64,56,128]{2,1,0:T(8,128)(2,1)} %shard_map.96), calls=%async_computation.1 | async-start | bytes 1835008 | tf_op jit(solution)/shard_map/all_to_all | solution.py:416
  54.3 0.6 copy-start.19
  56.5 8.6 %collective-permute-start.2 = (bf16[64,56,128]{2,1,0:T(8,128)(2,1)S(1)}, bf16[64,56,128]{2,1,0:T(8,128)(2,1)}, u32[]{:S(2)}, u32[]{:S(2)}) collective-permute-start(bf16[64,56,128]{2,1,0:T(8,128)(2,1)S(1)} %all-to-all-done.1.own_ref), channel_id=1, source_target_pairs={{0,1},{1,0},{2,3},{3,2},{4,5},{5,4},{6,7},{7,6},{8,9},{9,8},{10,11... | collective-permute-start | bytes 2752520 | tf_op jit(solution)/shard_map/ppermute | solution.py:412
  58.2 30.4 %all-to-all-start.2 = ((bf16[64,24,512]{2,1,0:T(8,128)(2,1)}), bf16[64,24,512]{2,1,0:T(8,128)(2,1)S(1)}, u32[]{:S(2)}, u32[]{:S(2)}) async-start(bf16[64,24,512]{2,1,0:T(8,128)(2,1)} %bitcast.18), calls=%async_computation.2 | async-start | bytes 3145728 | tf_op jit(solution)/shard_map/all_to_all | solution.py:416
  65.1 2.1 %copy-start.5 = (s32[1536,128]{1,0:T(8,128)S(1)}, s32[1536,128]{1,0:T(8,128)}, u32[]{:S(2)}) copy-start(s32[1536,128]{1,0:T(8,128)} %copy-done.4) | copy-start | bytes 2359300
  65.1 2.1 %copy-start.7 = (f32[1536,128]{1,0:T(8,128)S(1)}, f32[1536,128]{1,0:T(8,128)}, u32[]{:S(2)}) copy-start(f32[1536,128]{1,0:T(8,128)} %copy-done.6) | copy-start | bytes 2359300
  65.1 2.1 %copy-start.9 = (s32[3,1024]{1,0:T(4,128)S(1)}, s32[3,1024]{1,0:T(4,128)}, u32[]{:S(2)}) copy-start(s32[3,1024]{1,0:T(4,128)} %copy-done.8) | copy-start | bytes 36868
  65.1 2.1 %copy-start.13 = (s32[1,1024]{1,0:T(1,128)S(1)}, s32[1,1024]{1,0:T(1,128)}, u32[]{:S(2)}) copy-start(s32[1,1024]{1,0:T(1,128)} %targets_ref.3) | copy-start | bytes 12292
  65.1 2.1 %copy-start.15 = (s32[3]{0:T(128)S(1)}, s32[3]{0:T(128)}, u32[]{:S(2)}) copy-start(s32[3]{0:T(128)} %copy-done.14) | copy-start | bytes 40
  65.1 2.1 %copy-start.20 = (f32[1,1024]{1,0:T(1,128)S(1)}, f32[1,1024]{1,0:T(1,128)}, u32[]{:S(2)}) copy-start(f32[1,1024]{1,0:T(1,128)} %copy-done.19) | copy-start | bytes 12292
  66.6 0.6 copy-start.10
  74.6 2.3 %collective-permute-start.3 = (bf16[1536,256]{1,0:T(8,128)(2,1)S(1)}, bf16[1536,256]{1,0:T(8,128)(2,1)S(1)}, u32[]{:S(2)}, u32[]{:S(2)}) collective-permute-start(bf16[1536,256]{1,0:T(8,128)(2,1)S(1)} %get-tuple-element.54), channel_id=1, source_target_pairs={{0,1},{1,0},{2,3},{3,2},{4,5},{5,4},{6,7},{7,6},{8,9},{9,8},{10,11... | collective-permute-start | bytes 2359304 | tf_op jit(solution)/shard_map/ppermute | solution.py:412
  78.1 17.2 %copy-start.11 = (s32[2,64,128]{2,1,0:T(8,128)S(1)}, s32[2,64,128]{2,1,0:T(8,128)}, u32[]{:S(2)}) copy-start(s32[2,64,128]{2,1,0:T(8,128)} %copy-done.10) | copy-start | bytes 196612
  78.1 17.3 %copy-start.16 = (s32[3]{0:T(128)S(1)}, s32[3]{0:T(128)}, u32[]{:S(2)}) copy-start(s32[3]{0:T(128)} %copy-done.14) | copy-start | bytes 40
  88.5 13.0 %copy-start.1 = (bf16[64,24,512]{2,1,0:T(8,128)(2,1)}, bf16[64,24,512]{2,1,0:T(8,128)(2,1)S(1)}, u32[]{:S(2)}) copy-start(bf16[64,24,512]{2,1,0:T(8,128)(2,1)S(1)} %all-to-all-done.2) | copy-start | bytes 4718596
  88.5 13.0 %collective-permute-start.4 = (bf16[1536,512]{1,0:T(8,128)(2,1)S(1)}, bf16[1536,512]{1,0:T(8,128)(2,1)}, u32[]{:S(2)}, u32[]{:S(2)}) collective-permute-start(bf16[1536,512]{1,0:T(8,128)(2,1)S(1)} %bitcast.13), channel_id=1, source_target_pairs={{0,1},{1,0},{2,3},{3,2},{4,5},{5,4},{6,7},{7,6},{8,9},{9,8},{10,11... | collective-permute-start | bytes 4718600 | tf_op jit(solution)/shard_map/ppermute | solution.py:412
  90.2 21.7 %all-to-all-start.3 = ((bf16[64,56,128]{2,1,0:T(8,128)(2,1)}), bf16[64,56,128]{2,1,0:T(8,128)(2,1)S(1)}, u32[]{:S(2)}, u32[]{:S(2)}) async-start(bf16[64,56,128]{2,1,0:T(8,128)(2,1)} %shard_map.101), calls=%async_computation.3 | async-start | bytes 1835008 | tf_op jit(solution)/shard_map/all_to_all | solution.py:416
  101.6 1.4 %copy-start.2 = (bf16[64,24,512]{2,1,0:T(8,128)(2,1)S(1)}, bf16[64,24,512]{2,1,0:T(8,128)(2,1)}, u32[]{:S(2)}) copy-start(bf16[64,24,512]{2,1,0:T(8,128)(2,1)} %copy-done.1) | copy-start | bytes 4718596
  112.4 2.9 %collective-permute-start.5 = (f32[32,256]{1,0:T(8,128)S(1)}, f32[32,256]{1,0:T(8,128)S(1)}, u32[]{:S(2)}, u32[]{:S(2)}) collective-permute-start(f32[32,256]{1,0:T(8,128)S(1)} %shard_map.103.small_ref), channel_id=1, source_target_pairs={{0,1},{1,0},{2,3},{3,2},{4,5},{5,4},{6,7},{7,6},{8,9},{9,8},{10,11... | collective-permute-start | bytes 98312 | tf_op jit(solution)/shard_map/ppermute | solution.py:412

commit v8 on v7

--- a/solution.py
+++ b/solution.py
@@ -479,7 +479,7 @@
             pltpu.SemaphoreType.DMA((10,)),
         ],
         cost_estimate=pl.CostEstimate(flops=0, bytes_accessed=0, transcendentals=0),
-        compiler_params=pltpu.CompilerParams(vmem_limit_bytes=52 << 20),
+        compiler_params=pltpu.CompilerParams(vmem_limit_bytes=48 << 20),
     )(info, target_slot, w_own, normed, w_other, ev, follow)
     got_neg, send_rows = lax.optimization_barrier((got_neg, send_rows))
     other_neg = swap(got_neg)
@@ -520,10 +520,7 @@
     block = call(
         term_block_kernel, jax.ShapeDtypeStruct((NCHIPS, BLOCK, 128), BF), [VMEM] * 3, vmem=16
     )(term_own, swap(term_other), meta)
-    recv_rows, block = lax.optimization_barrier((recv_rows, block))
-    got = chips_a2a(block)
-
-    recv_other = swap(recv_rows)
+
     at, sorted_key, starts, neg_at = pl.pallas_call(
         rank_kernel,
         out_shape=(
@@ -537,6 +534,9 @@
         cost_estimate=pl.CostEstimate(flops=0, bytes_accessed=0, transcendentals=0),
         compiler_params=pltpu.CompilerParams(vmem_limit_bytes=16 << 20),
     )(info, row_table[:, :, :CSLOTS].reshape(1, 2 * SLOTS), neg_table)
+    recv_rows, block, at = lax.optimization_barrier((recv_rows, block, at))
+    got = chips_a2a(block)
+    recv_other = swap(recv_rows)
     rows = call(sort_kernel, jax.ShapeDtypeStruct((PLACES, width), BF), [VMEM] * 3, vmem=24)(
         at, recv_rows, recv_other
     )

time: 122 us -> 124 us (1.016)
  waiting for transfers between devices: 18.1 us -> 15.4 us
  local copies, waits for them, and re-layouts: 11.4 us -> 13.6 us
  starting transfers between devices: 37.9 us -> 39.3 us
    unnamed x42 -> x30, local copies, waits for them, and re-layouts: 5.42 us -> 8.68 us
    all_to_all x3, waiting for transfers between devices: 12.9 us -> 11.3 us  [chips_a2a(): return lax.all_to_all(v, CHIPS, split_axis=0, concat_axis=0, tiled=True)]
    all_to_all x3, starting transfers between devices: 18.9 us -> 20.4 us  [chips_a2a(): return lax.all_to_all(v, CHIPS, split_axis=0, concat_axis=0, tiled=True)]
    ppermute x6, waiting for transfers between devices: 2.88 us -> 1.38 us  [swap(): return lax.ppermute(v, 'c', SWAP)]
  transfers between devices with their start and end apart: 10 -> 10, of which waited for: 6 -> 6; matrix products, arithmetic and copies ran while one was open for 4% -> 3% of each run, Pallas kernels for 37% -> 37%
where the time goes in v8:
time: 124 us; the launch traced here: 123 us
  Pallas kernels  51.5 us (42%)
  starting transfers between devices  39.3 us (32%)
  waiting for transfers between devices  15.4 us (12%)
  local copies, waits for them, and re-layouts  13.6 us (11%)
  between operations  1.73 us (1%)
  other arithmetic  1.25 us (1%)
    all_to_all x3, starting transfers between devices, chips_a2a(): return lax.all_to_all(v, CHIPS, split_axis=0, concat_axis=0, tiled=True)  20.4 us
    pallas_call x1, Pallas kernels, per_device(): pl.pallas_call(layer_kernel, out_shape=(jax.ShapeDtypeStruct((1, 1024), F...  13.8 us
    all_to_all x3, waiting for transfers between devices, chips_a2a(): return lax.all_to_all(v, CHIPS, split_axis=0, concat_axis=0, tiled=True)  11.3 us
    ppermute x6, starting transfers between devices, swap(): return lax.ppermute(v, 'c', SWAP)  10.4 us
    unnamed x30, local copies, waits for them, and re-layouts  8.68 us
    all_to_all x1, starting transfers between devices, per_device(): lax.all_to_all(jnp.broadcast_to(w_mine[None], (16,) + w_mine.shape), ('x'...  8.57 us
    pallas_call x1, Pallas kernels, per_device(): call(sort_kernel, jax.ShapeDtypeStruct((PLACES, width), BF), [VMEM] * 3,...  8.05 us
    pallas_call x1, Pallas kernels, per_device(): call(loss_kernel, (jax.ShapeDtypeStruct((1, 1024), F32), jax.ShapeDtypeSt...  7.85 us
  transfers between devices with their start and end apart: 10, of which 6 were waited for; matrix products, arithmetic and copies ran while one was open for 3% of the time, Pallas kernels for 37%

profile of v8, /device:TPU:1, one launch (start us, length us, event | category | flops | bytes accessed | tf_op | source)
XLA Modules:
  0.0 122.9 jit_solution(7237682708190296956)
XLA Ops:
  0.6 0.9 pad_maximum_fusion
  1.5 1.2 broadcast_in_dim.31
  2.7 8.6 %all-to-all-start = ((bf16[16,16,2560]{2,1,0:T(8,128)(2,1)}), bf16[16,16,2560]{2,1,0:T(8,128)(2,1)S(1)}, u32[]{:S(2)}, u32[]{:S(2)}) async-start(bf16[16,16,2560]{2,1,0:T(8,128)(2,1)} %broadcast_in_dim.31), calls=%async_computation | async-start | bytes 2621440 | tf_op jit(solution)/shard_map/all_to_all | solution.py:427
  12.0 5.2 %shard_map.95 = (bf16[1024,512]{1,0:T(8,128)(2,1)S(1)}, s32[1536,128]{1,0:T(8,128)S(1)}, f32[1536,128]{1,0:T(8,128)S(1)}, s32[3,1024]{1,0:T(4,128)S(1)}, f32[2,6...) custom-call(s32[3]{0:T(128)S(1)} %pad_add_fusion.info_ref, bf16[1024,512]{1,0:T(8,128)(2,1)S(1)} %bitcast.11, ...), custom_call_target="tpu_custom_call" | custom-call | tf_op jit(solution)/shard_map/pallas_call | solution.py:431
  17.2 1.0 copy-done.6
  18.2 0.9 copy-done.8
  19.1 0.9 copy-done.10
  20.1 3.4 %gather_fusion = bf16[32,512]{1,0:T(8,128)(2,1)S(1)} fusion(bf16[4096,512]{1,0:T(8,128)(2,1)} %param.13, s32[1024]{0:T(1024)S(1)} %pad_clamp_fusion), kind=kCustom, calls=%fused_computation | custom fusion | bytes 65664 | tf_op jit(solution)/shard_map/gather | solution.py:447
  23.7 1.0 collective-permute-start
  25.7 0.9 copy-done.3
  26.6 2.8 %all-to-all-done = bf16[16,16,2560]{2,1,0:T(8,128)(2,1)S(1)} async-done(((bf16[16,16,2560]{2,1,0:T(8,128)(2,1)}), bf16[16,16,2560]{2,1,0:T(8,128)(2,1)S(1)}, u32[]{:S(2)}, u32[]{:S(2)}) %all-to-all-start) | async-done | bytes 1310752 | tf_op jit(solution)/shard_map/all_to_all | solution.py:427
  29.3 3.7 %collective-permute-start.1 = (bf16[256,2560]{1,0:T(8,128)(2,1)S(1)}, bf16[256,2560]{1,0:T(8,128)(2,1)}, u32[]{:S(2)}, u32[]{:S(2)}) collective-permute-start(bf16[256,2560]{1,0:T(8,128)(2,1)S(1)} %bitcast.15), channel_id=1, source_target_pairs={{0,1},{1,0},{2,3},{3,2},{4,5},{5,4},{6,7},{7,6},{8,9},{9,8},{10,11... | collective-permute-start | bytes 3932168 | tf_op jit(solution)/shard_map/ppermute | solution.py:412
  33.0 7.1 %all-to-all-start.1 = ((bf16[64,56,128]{2,1,0:T(8,128)(2,1)}), bf16[64,56,128]{2,1,0:T(8,128)(2,1)}, u32[]{:S(2)}, u32[]{:S(2)}) async-start(bf16[64,56,128]{2,1,0:T(8,128)(2,1)} %copy-done.3), calls=%async_computation.1 | async-start | bytes 1835008 | tf_op jit(solution)/shard_map/all_to_all | solution.py:416
  40.2 1.2 copy-done.7
  41.4 13.8 %shard_map.97 = (f32[1,1024]{1,0:T(1,128)S(1)}, bf16[1024,512]{1,0:T(8,128)(2,1)S(1)}, bf16[1536,512]{1,0:T(8,128)(2,1)}) custom-call(s32[3]{0:T(128)S(1)} %pad_add_fusion.info_ref, s32[3,1024]{1,0:T(4,128)S(1)} %get-tuple-element.33.slot_ref, bf16[256,2560]{1,0:T(8,128)(2,1)S(1)} %bitcast.16, bf16[1024,512]{1,0:T(8,128)(2,1)S(1)} %copy-done.7, ...), custom_call_target="tpu_custom_call" | custom-call | tf_op jit(solution)/shard_map/pallas_call | solution.py:459
  55.2 1.0 copy-done.4
  56.5 1.7 %collective-permute-start.2 = (bf16[64,56,128]{2,1,0:T(8,128)(2,1)}, bf16[64,56,128]{2,1,0:T(8,128)(2,1)S(1)}, u32[]{:S(2)}, u32[]{:S(2)}) collective-permute-start(bf16[64,56,128]{2,1,0:T(8,128)(2,1)} %all-to-all-done.1.own_ref), channel_id=1, source_target_pairs={{0,1},{1,0},{2,3},{3,2},{4,5},{5,4},{6,7},{7,6},{8,9},{9,8},{10,11... | collective-permute-start | bytes 2752520 | tf_op jit(solution)/shard_map/ppermute | solution.py:412
  58.2 8.1 %all-to-all-start.2 = ((bf16[64,24,512]{2,1,0:T(8,128)(2,1)}), bf16[64,24,512]{2,1,0:T(8,128)(2,1)S(1)}, u32[]{:S(2)}, u32[]{:S(2)}) async-start(bf16[64,24,512]{2,1,0:T(8,128)(2,1)} %bitcast.20), calls=%async_computation.2 | async-start | bytes 3145728 | tf_op jit(solution)/shard_map/all_to_all | solution.py:416
  66.4 1.5 %shard_map.98 = (bf16[1536,256]{1,0:T(8,128)(2,1)S(1)}, bf16[1536,256]{1,0:T(8,128)(2,1)S(1)}, s32[2,64,128]{2,1,0:T(8,128)S(1)}) custom-call(bf16[64,56,128]{2,1,0:T(8,128)(2,1)} %all-to-all-done.1.own_ref, bf16[64,56,128]{2,1,0:T(8,128)(2,1)S(1)} %collective-permute-done.2.other_ref), custom_call_target="tpu_custom_call" | custom-call | tf_op jit(solution)/shard_map/pallas_call | solution.py:487
  68.0 1.1 copy-done.11
  69.2 7.9 %shard_map.99 = (f32[1,1024]{1,0:T(1,128)}, f32[1536,256]{1,0:T(8,128)S(1)}, bf16[1536,256]{1,0:T(8,128)(2,1)}, f32[3,64,128]{2,1,0:T(8,128)S(1)}) custom-call(s32[3]{0:T(128)S(1)} %pad_add_fusion.info_ref, bf16[1024,512]{1,0:T(8,128)(2,1)S(1)} %copy-done.5, bf16[1536,256]{1,0:T(8,128)(2,1)S(1)} %get-tuple-element.44.own_ref, ...), custom_call_target="tpu_custom_call" | custom-call | tf_op jit(solution)/shard_map/pallas_call | solution.py:500
  77.4 6.1 %shard_map.100 = (s32[1,3072]{1,0:T(1,128)S(1)}, s32[16,128]{1,0:T(8,128)S(1)}, s32[32]{0:T(128)S(1)}, s32[64]{0:T(128)S(1)}) custom-call(s32[3]{0:T(128)S(1)} %pad_add_fusion.info_ref, s32[1,3072]{1,0:T(1,128)S(1)} %reshape.19.row_ref, s32[32,128]{1,0:T(8,128)S(1)} %get-tuple-element.35.neg_ref), custom_call_target="tpu_custom_call" | custom-call | tf_op jit(solution)/shard_map/pallas_call | solution.py:524
  83.6 2.3 %shard_map.101 = bf16[64,56,128]{2,1,0:T(8,128)(2,1)} custom-call(f32[1536,256]{1,0:T(8,128)S(1)} %get-tuple-element.54.own_ref, bf16[1536,256]{1,0:T(8,128)(2,1)} %collective-permute-done.3.other_ref, f32[3,64,128]{2,1,0:T(8,128)S(1)} %get-tuple-element.56.meta_ref), custom_call_target="tpu_custom_call" | custom-call | tf_op jit(solution)/shard_map/pallas_call | solution.py:520
  85.9 3.9 %all-to-all-done.2 = bf16[64,24,512]{2,1,0:T(8,128)(2,1)S(1)} async-done(((bf16[64,24,512]{2,1,0:T(8,128)(2,1)}), bf16[64,24,512]{2,1,0:T(8,128)(2,1)S(1)}, u32[]{:S(2)}, u32[]{:S(2)}) %all-to-all-start.2) | async-done | bytes 1572896 | tf_op jit(solution)/shard_map/all_to_all | solution.py:416
  89.8 1.6 %collective-permute-start.4 = (bf16[1536,512]{1,0:T(8,128)(2,1)S(1)}, bf16[1536,512]{1,0:T(8,128)(2,1)}, u32[]{:S(2)}, u32[]{:S(2)}) collective-permute-start(bf16[1536,512]{1,0:T(8,128)(2,1)S(1)} %bitcast.13), channel_id=1, source_target_pairs={{0,1},{1,0},{2,3},{3,2},{4,5},{5,4},{6,7},{7,6},{8,9},{9,8},{10,11... | collective-permute-start | bytes 4718600 | tf_op jit(solution)/shard_map/ppermute | solution.py:412
  91.4 5.1 %all-to-all-start.3 = ((bf16[64,56,128]{2,1,0:T(8,128)(2,1)}), bf16[64,56,128]{2,1,0:T(8,128)(2,1)S(1)}, u32[]{:S(2)}, u32[]{:S(2)}) async-start(bf16[64,56,128]{2,1,0:T(8,128)(2,1)} %shard_map.101), calls=%async_computation.3 | async-start | bytes 1835008 | tf_op jit(solution)/shard_map/all_to_all | solution.py:416
  96.6 1.4 %copy-done.2 = bf16[64,24,512]{2,1,0:T(8,128)(2,1)S(1)} copy-done((bf16[64,24,512]{2,1,0:T(8,128)(2,1)S(1)}, bf16[64,24,512]{2,1,0:T(8,128)(2,1)}, u32[]{:S(2)}) %copy-start.2) | copy-done | bytes 1572888
  98.0 8.0 %shard_map.102.rows_ref = bf16[2048,512]{1,0:T(8,128)(2,1)S(1)} custom-call(s32[1,3072]{1,0:T(1,128)S(1)} %get-tuple-element.59.at_ref, bf16[1536,512]{1,0:T(8,128)(2,1)S(1)} %bitcast.14, bf16[1536,512]{1,0:T(8,128)(2,1)} %collective-permute-done.4.other_ref), custom_call_target="tpu_custom_call" | custom-call | tf_op jit(solution)/shard_map/pallas_call | solution.py:540
  106.0 7.1 %all-to-all-done.3.got_ref = bf16[64,56,128]{2,1,0:T(8,128)(2,1)S(1)} async-done(((bf16[64,56,128]{2,1,0:T(8,128)(2,1)}), bf16[64,56,128]{2,1,0:T(8,128)(2,1)S(1)}, u32[]{:S(2)}, u32[]{:S(2)}) %all-to-all-start.3) | async-done | bytes 917536 | tf_op jit(solution)/shard_map/all_to_all | solution.py:416
  113.7 2.0 %collective-permute-start.5 = (f32[32,256]{1,0:T(8,128)S(1)}, f32[32,256]{1,0:T(8,128)S(1)}, u32[]{:S(2)}, u32[]{:S(2)}) collective-permute-start(f32[32,256]{1,0:T(8,128)S(1)} %shard_map.103.small_ref), channel_id=1, source_target_pairs={{0,1},{1,0},{2,3},{3,2},{4,5},{5,4},{6,7},{7,6},{8,9},{9,8},{10,11... | collective-permute-start | bytes 98312 | tf_op jit(solution)/shard_map/ppermute | solution.py:412
  115.7 0.9 collective-permute-done.5.small_other_ref
  116.6 6.1 %shard_map.104 = bf16[4096,512]{1,0:T(8,128)(2,1)} custom-call(s32[32]{0:T(128)S(1)} %get-tuple-element.51.start_ref, s32[64]{0:T(128)S(1)} %get-tuple-element.52.neg_at_ref, f32[32,256]{1,0:T(8,128)S(1)} %shard_map.103.small_ref, f32[32,256]{1,0:T(8,128)S(1)} %collective-permute-done.5.small_other_ref, s32[1,3072]{1,0:T(1,128)S(1)} %get-tuple-element.59.at_ref, ...), custom_call_target="tpu_custom_call" | custom-call | tf_op jit(solution)/shard_map/pallas_call | solution.py:548
  (40 shorter events, 2.7 us)
Async XLA Ops:
  2.7 9.3 %copy-start = (bf16[1,1024,512]{2,1,0:T(8,128)(2,1)S(1)}, bf16[1,1024,512]{2,1,0:T(8,128)(2,1)}, u32[]{:S(2)}) copy-start(bf16[1,1024,512]{2,1,0:T(8,128)(2,1)} %param.8) | copy-start | bytes 3145732
  2.7 9.3 %copy-start.12 = (s32[1,1024]{1,0:T(1,128)S(1)}, s32[1,1024]{1,0:T(1,128)}, u32[]{:S(2)}) copy-start(s32[1,1024]{1,0:T(1,128)} %targets_ref.3) | copy-start | bytes 12292
  2.7 9.3 %copy-start.13 = (s32[1024]{0:T(1024)S(1)}, s32[1024]{0:T(1024)}, u32[]{:S(2)}) copy-start(s32[1024]{0:T(1024)} %param.11) | copy-start | bytes 12292
  2.7 9.3 %copy-start.14 = (s32[1024]{0:T(1024)S(1)}, s32[1024]{0:T(1024)}, u32[]{:S(2)}) copy-start(s32[1024]{0:T(1024)} %param.12) | copy-start | bytes 12292
  2.7 26.7 %all-to-all-start = ((bf16[16,16,2560]{2,1,0:T(8,128)(2,1)}), bf16[16,16,2560]{2,1,0:T(8,128)(2,1)S(1)}, u32[]{:S(2)}, u32[]{:S(2)}) async-start(bf16[16,16,2560]{2,1,0:T(8,128)(2,1)} %broadcast_in_dim.31), calls=%async_computation | async-start | bytes 2621440 | tf_op jit(solution)/shard_map/all_to_all | solution.py:427
  17.2 1.0 copy-start.6
  18.2 0.9 copy-start.8
  19.1 0.9 copy-start.10
  23.7 1.9 %collective-permute-start = (bf16[32,256]{1,0:T(8,128)(2,1)S(1)}, bf16[32,256]{1,0:T(8,128)(2,1)S(1)}, u32[]{:S(2)}, u32[]{:S(2)}) collective-permute-start(bf16[32,256]{1,0:T(8,128)(2,1)S(1)} %get-tuple-element.64), channel_id=1, source_target_pairs={{0,1},{1,0},{2,3},{3,2},{4,5},{5,4},{6,7},{7,6},{8,9},{9,8},{10,11... | collective-permute-start | bytes 49160 | tf_op jit(solution)/shard_map/ppermute | solution.py:412
  25.7 0.9 copy-start.3
  29.3 10.8 %collective-permute-start.1 = (bf16[256,2560]{1,0:T(8,128)(2,1)S(1)}, bf16[256,2560]{1,0:T(8,128)(2,1)}, u32[]{:S(2)}, u32[]{:S(2)}) collective-permute-start(bf16[256,2560]{1,0:T(8,128)(2,1)S(1)} %bitcast.15), channel_id=1, source_target_pairs={{0,1},{1,0},{2,3},{3,2},{4,5},{5,4},{6,7},{7,6},{8,9},{9,8},{10,11... | collective-permute-start | bytes 3932168 | tf_op jit(solution)/shard_map/ppermute | solution.py:412
  33.0 23.5 %all-to-all-start.1 = ((bf16[64,56,128]{2,1,0:T(8,128)(2,1)}), bf16[64,56,128]{2,1,0:T(8,128)(2,1)}, u32[]{:S(2)}, u32[]{:S(2)}) async-start(bf16[64,56,128]{2,1,0:T(8,128)(2,1)} %copy-done.3), calls=%async_computation.1 | async-start | bytes 1835008 | tf_op jit(solution)/shard_map/all_to_all | solution.py:416
  40.2 1.2 copy-start.7
  55.2 1.0 copy-start.4
  56.5 9.9 %collective-permute-start.2 = (bf16[64,56,128]{2,1,0:T(8,128)(2,1)}, bf16[64,56,128]{2,1,0:T(8,128)(2,1)S(1)}, u32[]{:S(2)}, u32[]{:S(2)}) collective-permute-start(bf16[64,56,128]{2,1,0:T(8,128)(2,1)} %all-to-all-done.1.own_ref), channel_id=1, source_target_pairs={{0,1},{1,0},{2,3},{3,2},{4,5},{5,4},{6,7},{7,6},{8,9},{9,8},{10,11... | collective-permute-start | bytes 2752520 | tf_op jit(solution)/shard_map/ppermute | solution.py:412
  58.2 31.6 %all-to-all-start.2 = ((bf16[64,24,512]{2,1,0:T(8,128)(2,1)}), bf16[64,24,512]{2,1,0:T(8,128)(2,1)S(1)}, u32[]{:S(2)}, u32[]{:S(2)}) async-start(bf16[64,24,512]{2,1,0:T(8,128)(2,1)} %bitcast.20), calls=%async_computation.2 | async-start | bytes 3145728 | tf_op jit(solution)/shard_map/all_to_all | solution.py:416
  66.3 1.5 %copy-start.5 = (bf16[1024,512]{1,0:T(8,128)(2,1)S(1)}, bf16[1024,512]{1,0:T(8,128)(2,1)}, u32[]{:S(2)}) copy-start(bf16[1024,512]{1,0:T(8,128)(2,1)} %copy-done.4) | copy-start | bytes 3145732
  66.3 1.7 %copy-start.9 = (s32[1536,128]{1,0:T(8,128)S(1)}, s32[1536,128]{1,0:T(8,128)}, u32[]{:S(2)}) copy-start(s32[1536,128]{1,0:T(8,128)} %copy-done.8) | copy-start | bytes 2359300
  68.0 1.1 copy-start.11
  77.0 6.5 %collective-permute-start.3 = (bf16[1536,256]{1,0:T(8,128)(2,1)}, bf16[1536,256]{1,0:T(8,128)(2,1)}, u32[]{:S(2)}, u32[]{:S(2)}) collective-permute-start(bf16[1536,256]{1,0:T(8,128)(2,1)} %get-tuple-element.55), channel_id=1, source_target_pairs={{0,1},{1,0},{2,3},{3,2},{4,5},{5,4},{6,7},{7,6},{8,9},{9,8},{10,11... | collective-permute-start | bytes 2359304 | tf_op jit(solution)/shard_map/ppermute | solution.py:412
  89.8 6.7 %copy-start.1 = (bf16[64,24,512]{2,1,0:T(8,128)(2,1)}, bf16[64,24,512]{2,1,0:T(8,128)(2,1)S(1)}, u32[]{:S(2)}) copy-start(bf16[64,24,512]{2,1,0:T(8,128)(2,1)S(1)} %all-to-all-done.2) | copy-start | bytes 4718596
  89.8 6.8 %collective-permute-start.4 = (bf16[1536,512]{1,0:T(8,128)(2,1)S(1)}, bf16[1536,512]{1,0:T(8,128)(2,1)}, u32[]{:S(2)}, u32[]{:S(2)}) collective-permute-start(bf16[1536,512]{1,0:T(8,128)(2,1)S(1)} %bitcast.13), channel_id=1, source_target_pairs={{0,1},{1,0},{2,3},{3,2},{4,5},{5,4},{6,7},{7,6},{8,9},{9,8},{10,11... | collective-permute-start | bytes 4718600 | tf_op jit(solution)/shard_map/ppermute | solution.py:412
  91.4 21.7 %all-to-all-start.3 = ((bf16[64,56,128]{2,1,0:T(8,128)(2,1)}), bf16[64,56,128]{2,1,0:T(8,128)(2,1)S(1)}, u32[]{:S(2)}, u32[]{:S(2)}) async-start(bf16[64,56,128]{2,1,0:T(8,128)(2,1)} %shard_map.101), calls=%async_computation.3 | async-start | bytes 1835008 | tf_op jit(solution)/shard_map/all_to_all | solution.py:416
  96.6 1.4 %copy-start.2 = (bf16[64,24,512]{2,1,0:T(8,128)(2,1)S(1)}, bf16[64,24,512]{2,1,0:T(8,128)(2,1)}, u32[]{:S(2)}) copy-start(bf16[64,24,512]{2,1,0:T(8,128)(2,1)} %copy-done.1) | copy-start | bytes 4718596
  113.7 2.9 %collective-permute-start.5 = (f32[32,256]{1,0:T(8,128)S(1)}, f32[32,256]{1,0:T(8,128)S(1)}, u32[]{:S(2)}, u32[]{:S(2)}) collective-permute-start(f32[32,256]{1,0:T(8,128)S(1)} %shard_map.103.small_ref), channel_id=1, source_target_pairs={{0,1},{1,0},{2,3},{3,2},{4,5},{5,4},{6,7},{7,6},{8,9},{9,8},{10,11... | collective-permute-start | bytes 98312 | tf_op jit(solution)/shard_map/ppermute | solution.py:412
